TPU v7x, 32 devices: a whole 2x2x4 slice. The times are simulated.
32 devices in a mesh: ga: 2 (over y), gx: 16 (over z, x, core).
Axes of the slice: x: 2, y: 2, z: 4, core: 2. Of those that a mesh axis runs over, the one named last changes fastest.
Arguments:
- fields: bfloat16 [2048, 512, 128], P('gx', 'ga'), parts along dimension 1, may hold values from -6 to 6
- cotangent: bfloat16 [2048, 512, 128], P('gx', 'ga'), parts along dimension 1, may hold values from -6 to 6
- point_weight: bfloat16 [128, 128], replicated, may hold values from -0.5 to 0.5
- mix_weight: bfloat16 [12, 128, 128], replicated, may hold values from -0.5 to 0.5
- bias_vec: bfloat16 [128], replicated, may hold values from -3 to 3
Outputs:
- grad_input: bfloat16 [2048, 512, 128], P('gx', 'ga'), parts along dimension 1
- grad_mix: bfloat16 [24, 128, 128], P('ga'), parts along dimension 0
- grad_point: bfloat16 [256, 128], P('ga'), parts along dimension 0
- grad_bias: bfloat16 [256], P('ga'), parts along dimension 0
There are 2 independent parts, one for each index of `ga`. A program takes and returns all parts, laid end to end along the dimension named above; an argument that names none is the same for every part. Nothing has to cross between parts.
All inputs are finite; a program needn't handle non-finite values.
Results may differ from a plain program's by a relative error of at most 0.012.
Values sent between devices are 32-bit elements; how exact they have to be, the bound alone decides.
No kernel may reach another device: no remote copies, remote signals or barrier semaphores. Data moves between devices by JAX's collectives and lax.ppermute only.
A program may use at most 128 MiB of HBM per device.

v0:
```python
import math

import jax
import jax.numpy as jnp
import numpy as np
from jax import lax
from jax.sharding import PartitionSpec as P

NX = 2048
LEVELS = 11


root_half = 0.7071067811865476


def partner_2(block, axis, stride):
    count = lax.axis_size(axis)
    route = []
    for low in range(count):
        high = low | 1 << stride
        if high != low and high < count:
            route += [(low, high), (high, low)]
    return lax.ppermute(block, axis, route)


def haar_forward(signal, depth_count):
    for degree in range(depth_count):
        stride = 2**degree
        shaped = signal.reshape((signal.shape[0] // (2 * stride), 2, stride) + signal.shape[1:])
        even_rows = shaped[:, 0, 0]
        odd_rows = shaped[:, 1, 0]
        shaped = shaped.at[:, 0, 0].set((even_rows + odd_rows) * root_half)
        shaped = shaped.at[:, 1, 0].set((odd_rows - even_rows) * root_half)
        signal = shaped.reshape(signal.shape)
    return signal


def haar_inverse(signal, depth_count):
    for degree in reversed(range(depth_count)):
        stride = 2**degree
        shaped = signal.reshape((signal.shape[0] // (2 * stride), 2, stride) + signal.shape[1:])
        coarse_rows = shaped[:, 0, 0]
        detail_rows = shaped[:, 1, 0]
        shaped = shaped.at[:, 0, 0].set((coarse_rows - detail_rows) * root_half)
        shaped = shaped.at[:, 1, 0].set((coarse_rows + detail_rows) * root_half)
        signal = shaped.reshape(signal.shape)
    return signal


def mix_levels(coeffs_b, weights, depth_count, first_weight):
    output = jnp.zeros(coeffs_b.shape, jnp.float32)
    for degree in range(depth_count):
        stride = 2**degree
        picked = coeffs_b[stride :: 2 * stride]
        output = output.at[stride :: 2 * stride].set(
            jnp.dot(picked, weights[degree], preferred_element_type=jnp.float32)
        )
    output = output.at[0].set(
        jnp.dot(coeffs_b[0], first_weight, preferred_element_type=jnp.float32)
    )
    return output


def outer_sum(left, right):
    left_flat = left.reshape((-1, left.shape[-1]))
    right_flat = right.reshape((-1, right.shape[-1]))
    return lax.dot_general(
        left_flat, right_flat, (((0,), (0,)), ((), ())), preferred_element_type=jnp.float32
    )


def gelu_slope(pre_act, cotangent):
    unused_out, pullback = jax.vjp(jax.nn.gelu, pre_act)
    return pullback(cotangent.astype(pre_act.dtype))[0].astype(jnp.bfloat16)


def level_factors(columns):
    counts = [columns * NX / 2 ** (degree + 1) for degree in range(LEVELS)] + [columns]
    return np.array([1.0 / math.sqrt(value) for value in counts], np.float32)


def cross_levels(carry_row, inverse, position, cross_depth):
    degrees = list(range(cross_depth))
    if inverse:
        degrees = degrees[::-1]
    for degree in degrees:
        partner = partner_2(carry_row, "gx", degree)
        upper_half = position // 2**degree % 2 == 1
        active = position % 2**degree == 0
        summed = (carry_row + partner) * root_half
        differ = (carry_row - partner) * root_half
        if inverse:
            moved_row = jnp.where(upper_half, summed, differ)
        else:
            moved_row = jnp.where(upper_half, differ, summed)
        carry_row = jnp.where(active, moved_row, carry_row)
    return carry_row


def transform(signal, inverse, local_depth, position, cross_depth):
    if inverse:
        signal = signal.at[0].set(cross_levels(signal[0], True, position, cross_depth))
        return haar_inverse(signal, local_depth)
    signal = haar_forward(signal, local_depth)
    return signal.at[0].set(cross_levels(signal[0], False, position, cross_depth))


def shards(fields, cotangent, point_weight, mix_weight, bias_vec):
    rows_local = fields.shape[0]
    local_depth = rows_local.bit_length() - 1
    device_count = lax.axis_size("gx")
    cross_depth = device_count.bit_length() - 1
    position = lax.axis_index("gx")
    trailing = jnp.zeros((), jnp.int32)
    for degree in range(cross_depth):
        trailing = trailing + (position % 2 ** (degree + 1) == 0).astype(jnp.int32)
    first_level = local_depth + trailing
    transposed = jnp.swapaxes(mix_weight, 1, 2)
    first_weight = lax.dynamic_index_in_dim(mix_weight, first_level, 0, keepdims=False)
    first_back = lax.dynamic_index_in_dim(transposed, first_level, 0, keepdims=False)
    empty_grad = jnp.zeros((mix_weight.shape[1], mix_weight.shape[2]), jnp.float32)
    coeffs = transform(fields.astype(jnp.float32), False, local_depth, position, cross_depth)
    coeffs_b = coeffs.astype(jnp.bfloat16)
    mixed_rows = mix_levels(coeffs_b, mix_weight, local_depth, first_weight)
    spectral = transform(mixed_rows, True, local_depth, position, cross_depth)
    pre_act = (
        spectral
        + jnp.dot(fields, point_weight, preferred_element_type=jnp.float32)
        + bias_vec.astype(jnp.float32)
    )
    slope_b = gelu_slope(pre_act, cotangent)
    back_coeffs = transform(slope_b.astype(jnp.float32), False, local_depth, position, cross_depth)
    back_b = back_coeffs.astype(jnp.bfloat16)
    grads_list = []
    for degree in range(local_depth):
        stride = 2**degree
        grads_list.append(outer_sum(coeffs_b[stride :: 2 * stride], back_b[stride :: 2 * stride]))
    grads_list = grads_list + [empty_grad] * (LEVELS + 1 - local_depth)
    onehot = (jnp.arange(LEVELS + 1, dtype=jnp.int32) == first_level).astype(jnp.float32)
    stacked = (
        jnp.stack(grads_list) + onehot[:, None, None] * outer_sum(coeffs_b[0:1], back_b[0:1])[None]
    )
    point_grad = outer_sum(fields, slope_b)
    bias_grad = jnp.sum(slope_b.astype(jnp.float32), axis=(0, 1))
    back_mixed = mix_levels(back_b, transposed, local_depth, first_back)
    spectral_back = transform(back_mixed, True, local_depth, position, cross_depth)
    totals = lax.psum((stacked, point_grad, bias_grad), "gx")
    factors = jnp.asarray(level_factors(fields.shape[1]))
    scale_all = 1.0 / math.sqrt(NX * fields.shape[1])
    grad_mix = (totals[0] * factors[:, None, None]).astype(jnp.bfloat16)
    grad_point = (totals[1] * scale_all).astype(jnp.bfloat16)
    grad_bias = (totals[2] * scale_all).astype(jnp.bfloat16)
    grad_input = (
        spectral_back + jnp.dot(slope_b, point_weight.T, preferred_element_type=jnp.float32)
    ).astype(jnp.bfloat16)
    return (grad_input, grad_mix, grad_point, grad_bias)


def solution(mesh):
    in_specs = (P("gx", "ga", None), P("gx", "ga", None), P(), P(), P())
    out_specs = (P("gx", "ga", None), P("ga", None, None), P("ga", None), P("ga"))
    return jax.shard_map(shards, mesh=mesh, in_specs=in_specs, out_specs=out_specs, check_vma=False)
```

profile of v0, /device:TPU:0, one launch (start us, length us, event | category | flops | bytes accessed | tf_op | source)
XLA Modules:
  0.0 672.7 jit_solution(4957681307654745231)
XLA Ops:
  7.2 11.5 %convert.1 = f32[64,2,1,256,128]{4,3,1,0,2:T(8,128)} convert(bf16[64,2,1,256,128]{4,3,1,0,2:T(8,128)(2,1)} %bitcast.252) | non-fusion elementwise | flops 4194304 | bytes 25165824 | tf_op jit(solution)/shard_map/reshape | solution.py:29
  27.6 6.9 %multiply_dynamic-update-slice_fusion.6 = f32[64,2,1,256,128]{4,3,1,0,2:T(8,128)S(1)} fusion(f32[64,2,1,256,128]{4,3,1,0,2:T(8,128)S(1)} %multiply_dynamic-update-slice_fusion.7, f32[64,2,1,256,128]{4,3,1,0,2:T(8,128)} %convert.1), kind=kLoop, calls=%fused_computation.36 | loop fusion | flops 4194304 | bytes 25165824 | tf_op jit(solution)/shard_map/scatter | solution.py:33
  96.1 6.6 convert_element_type.52
  102.7 6.1 fusion.17
  117.2 7.8 %broadcast.1003.clone = f32[128,256,128]{2,1,0:T(8,128)} broadcast(f32[]{:T(128)} %constant.1621.clone.1), dimensions={} | broadcast | bytes 16777220 | tf_op jit(solution)/shard_map/broadcast.42
  125.1 16.3 %scatter_fusion = f32[128,256,128]{2,1,0:T(8,128)} fusion(f32[128,256,128]{2,1,0:T(8,128)} %broadcast.1003.clone, s32[64]{0:T(128)S(1)} %add_bitcast_fusion.5, f32[64,256,128]{2,1,0:T(8,128)} %fusion.17), kind=kCustom, calls=%fused_computation | custom fusion | bytes 25166080 | tf_op jit(solution)/shard_map/scatter | solution.py:55
  141.4 8.3 %scatter_fusion.1 = f32[128,256,128]{2,1,0:T(8,128)} fusion(f32[128,256,128]{2,1,0:T(8,128)} %scatter_fusion, s32[32]{0:T(128)S(1)} %add_bitcast_fusion.4, f32[32,256,128]{2,1,0:T(8,128)} %fusion.24), kind=kCustom, calls=%fused_computation.1 | custom fusion | bytes 12583040 | tf_op jit(solution)/shard_map/scatter | solution.py:55
  165.6 6.5 collective-permute-done.4
  228.5 11.6 %multiply_dynamic-update-slice_fusion.5 = f32[64,2,1,256,128]{4,3,1,0,2:T(8,128)} fusion(f32[64,2,1,256,128]{4,3,1,0,2:T(8,128)} %copy.62, f32[64,1,1,256,128]{4,3,1,0,2:T(8,128)} %slice.2362), kind=kLoop, calls=%fused_computation.35 | loop fusion | flops 4194304 | bytes 25165824 | tf_op jit(solution)/shard_map/scatter | solution.py:44
  240.1 10.3 %multiply_dynamic-update-slice_fusion.4 = f32[64,2,1,256,128]{4,3,1,0,2:T(8,128)} fusion(f32[64,2,1,256,128]{4,3,1,0,2:T(8,128)} %multiply_dynamic-update-slice_fusion.5, f32[64,2,1,256,128]{4,3,1,0,2:T(8,128)} %bitcast.220), kind=kLoop, calls=%fused_computation.34 | loop fusion | flops 4194304 | bytes 25165824 | tf_op jit(solution)/shard_map/scatter | solution.py:45
  250.4 28.9 %convert_reduce_fusion = (f32[128]{0:T(128)S(1)}, bf16[128,256,128]{2,1,0:T(8,128)(2,1)}) fusion(f32[128]{0:T(128)S(1)} %convert_element_type.57, bf16[128,256,128]{2,1,0:T(8,128)(2,1)S(1)} %bitcast.257, bf16[128,128]{1,0:T(8,128)(2,1)S(1)} %copy-done, f32[64,2,1,256,128]{4,3,1,0,2:T(8,128)} %multiply_dynamic-update-slice_fusion.4, ...), kind=kOutput, calls=%fused_computation.42 | convolution fusion | flops 1178599296 | bytes 41976832 | tf_op jit(solution)/shard_map/dot_general | solution.py:128
  279.3 11.5 %convert.2 = f32[64,2,1,256,128]{4,3,1,0,2:T(8,128)} convert(bf16[64,2,1,256,128]{4,3,1,0,2:T(8,128)(2,1)} %bitcast.230) | non-fusion elementwise | flops 4194304 | bytes 25165824 | tf_op jit(solution)/shard_map/reshape | solution.py:29
  299.5 6.9 %multiply_dynamic-update-slice_fusion.2 = f32[64,2,1,256,128]{4,3,1,0,2:T(8,128)S(1)} fusion(f32[64,2,1,256,128]{4,3,1,0,2:T(8,128)S(1)} %multiply_dynamic-update-slice_fusion.3, f32[64,2,1,256,128]{4,3,1,0,2:T(8,128)} %convert.2), kind=kLoop, calls=%fused_computation.32 | loop fusion | flops 4194304 | bytes 25165824 | tf_op jit(solution)/shard_map/scatter | solution.py:33
  356.3 8.8 %convolution_bitcast_fusion.7 = f32[128,128]{0,1:T(8,128)} fusion(bf16[128,256,128]{2,1,0:T(8,128)(2,1)} %get-tuple-element.783, bf16[128,256,128]{2,1,0:T(8,128)(2,1)} %param.134), kind=kOutput, calls=%fused_computation.87 | convolution fusion | flops 1073741824 | bytes 16842752 | tf_op jit(solution)/shard_map/dot_general | solution.py:67
  365.1 30.0 %psum.23 = f32[128]{0:T(128)S(1)} all-reduce(f32[128]{0:T(128)S(1)} %get-tuple-element.782), channel_id=1, replica_groups=mesh['ga'=2,'gx'=16] {'gx'}, use_global_device_ids=true, to_apply=%region_15.16 | all-reduce | flops 128 | bytes 1024 | tf_op jit(solution)/shard_map/psum | solution.py:147
  395.8 6.6 convert_element_type.60
  402.4 7.2 %fusion.43 = f32[12,128,128]{2,1,0:T(8,128)} fusion(bf16[128,256,128]{2,1,0:T(8,128)(2,1)S(1)} %convert_element_type.60, bf16[128,256,128]{2,1,0:T(8,128)(2,1)} %copy-done.9), kind=kOutput, calls=%fused_computation.76 | convolution fusion | flops 536870912 | bytes 8454144 | tf_op jit(solution)/shard_map/dot_general | solution.py:67
  434.7 7.8 %broadcast.1003 = f32[128,256,128]{2,1,0:T(8,128)} broadcast(f32[]{:T(128)} %constant.1621.clone.1), dimensions={} | broadcast | bytes 16777220 | tf_op jit(solution)/shard_map/broadcast.42
  442.5 16.3 %scatter_fusion.6 = f32[128,256,128]{2,1,0:T(8,128)} fusion(f32[128,256,128]{2,1,0:T(8,128)} %broadcast.1003, s32[64]{0:T(128)S(1)} %copy-done.14, f32[64,256,128]{2,1,0:T(8,128)} %fusion.14), kind=kCustom, calls=%fused_computation.6 | custom fusion | bytes 25166080 | tf_op jit(solution)/shard_map/scatter | solution.py:55
  458.9 8.3 %scatter_fusion.7 = f32[128,256,128]{2,1,0:T(8,128)} fusion(f32[128,256,128]{2,1,0:T(8,128)} %scatter_fusion.6, s32[32]{0:T(128)S(1)} %copy-done.16, f32[32,256,128]{2,1,0:T(8,128)} %fusion.21), kind=kCustom, calls=%fused_computation.7 | custom fusion | bytes 12583040 | tf_op jit(solution)/shard_map/scatter | solution.py:55
  498.7 82.5 %all-reduce.3.cloned.1.call-done = (f32[12,128,128]{2,1,0:T(8,128)}, f32[128,128]{0,1:T(8,128)}) async-done(((f32[12,128,128]{2,1,0:T(8,128)}, f32[128,128]{0,1:T(8,128)}), (f32[12,128,128]{2,1,0:T(8,128)}, f32[128,128]{0,1:T(8,128)})) %all-reduce.3.cloned.1.call-update) | async-done | bytes 851984 | tf_op jit(solution)/shard_map/psum | solution.py:147
  629.9 11.5 %multiply_dynamic-update-slice_fusion.1 = f32[64,2,1,256,128]{4,3,1,0,2:T(8,128)} fusion(f32[64,2,1,256,128]{4,3,1,0,2:T(8,128)} %copy.100, f32[64,1,1,256,128]{4,3,1,0,2:T(8,128)} %slice.2400), kind=kLoop, calls=%fused_computation.31 | loop fusion | flops 4194304 | bytes 25165824 | tf_op jit(solution)/shard_map/scatter | solution.py:44
  641.4 10.1 %multiply_dynamic-update-slice_fusion = f32[64,2,1,256,128]{4,3,1,0,2:T(8,128)} fusion(f32[64,2,1,256,128]{4,3,1,0,2:T(8,128)} %multiply_dynamic-update-slice_fusion.1, f32[64,2,1,256,128]{4,3,1,0,2:T(8,128)} %bitcast.223), kind=kLoop, calls=%fused_computation.30 | loop fusion | flops 4194304 | bytes 25165824 | tf_op jit(solution)/shard_map/scatter | solution.py:45
  651.5 13.9 %fusion.10 = bf16[128,256,128]{2,1,0:T(8,128)(2,1)} fusion(f32[64,2,1,256,128]{4,3,1,0,2:T(8,128)} %multiply_dynamic-update-slice_fusion, bf16[128,256,128]{2,1,0:T(8,128)(2,1)} %get-tuple-element.783, bf16[128,128]{1,0:T(8,128)(2,1)S(1)} %copy-done), kind=kOutput, calls=%fused_computation.27 | convolution fusion | flops 1082130432 | bytes 33587200 | tf_op jit(solution)/shard_map/dot_general | solution.py:154
  (268 shorter events, 314.8 us)
Async XLA Ops:
  7.2 243.2 %copy-start = (bf16[128,128]{1,0:T(8,128)(2,1)S(1)}, bf16[128,128]{1,0:T(8,128)(2,1)}, u32[]{:S(2)}) copy-start(bf16[128,128]{1,0:T(8,128)(2,1)} %param.136) | copy-start | bytes 98308
  7.2 574.1 %all-reduce.3.cloned.1.call-start = ((), (), s32[]{:S(2)}) async-start(), calls=%async_computation | async-start | bytes 1703936 | tf_op jit(solution)/shard_map/psum | solution.py:147
  73.2 1.5 collective-permute-start
  75.6 6.7 collective-permute-start.1
  82.4 5.1 collective-permute-start.2
  84.3 65.4 %copy-start.17 = (s32[16]{0:T(128)}, s32[16]{0:T(128)S(1)}, u32[]{:S(2)}) copy-start(s32[16]{0:T(128)S(1)} %add_bitcast_fusion.3) | copy-start | bytes 196
  84.3 69.1 %copy-start.23 = (s32[8]{0:T(128)}, s32[8]{0:T(128)S(1)}, u32[]{:S(2)}) copy-start(s32[8]{0:T(128)S(1)} %add_bitcast_fusion.2) | copy-start | bytes 100
  87.5 7.9 %collective-permute-start.3 = (f32[256,128]{1,0:T(8,128)S(1)}, f32[256,128]{1,0:T(8,128)S(1)}, u32[]{:S(2)}, u32[]{:S(2)}) collective-permute-start(f32[256,128]{1,0:T(8,128)S(1)} %select_select_fusion.8), channel_id=1, source_target_pairs={{0,8},{8,0},{1,9},{9,1},{2,10},{10,2},{3,11},{11,3},{4,12},{12,4},... | collective-permute-start | bytes 393224 | tf_op jit(solution)/shard_map/ppermute | solution.py:23
  90.4 65.9 %copy-start.19 = (s32[4]{0:T(128)}, s32[4]{0:T(128)S(1)}, u32[]{:S(2)}) copy-start(s32[4]{0:T(128)S(1)} %add_bitcast_fusion.1) | copy-start | bytes 52
  90.4 68.5 %copy-start.21 = (s32[2]{0:T(128)}, s32[2]{0:T(128)S(1)}, u32[]{:S(2)}) copy-start(s32[2]{0:T(128)S(1)} %add_bitcast_fusion) | copy-start | bytes 28
  164.7 7.4 %collective-permute-start.4 = (f32[256,128]{1,0:T(8,128)S(1)}, f32[256,128]{1,0:T(8,128)S(1)}, u32[]{:S(2)}, u32[]{:S(2)}) collective-permute-start(f32[256,128]{1,0:T(8,128)S(1)} %get-tuple-element.779), channel_id=1, source_target_pairs={{0,8},{8,0},{1,9},{9,1},{2,10},{10,2},{3,11},{11,3},{4,12},{12,4},... | collective-permute-start | bytes 393224 | tf_op jit(solution)/shard_map/ppermute | solution.py:23
  172.1 5.0 collective-permute-start.5
  177.2 5.0 collective-permute-start.6
  182.2 1.4 collective-permute-start.7
  339.5 1.4 collective-permute-start.8
  345.2 5.6 collective-permute-start.9
  350.9 5.0 collective-permute-start.10
  351.2 66.8 %copy-start.12 = (bf16[12,128,128]{1,2,0:T(8,128)(2,1)}, bf16[12,128,128]{1,2,0:T(8,128)(2,1)S(1)}, u32[]{:S(2)}) copy-start(bf16[12,128,128]{1,2,0:T(8,128)(2,1)S(1)} %copy.10) | copy-start | bytes 1179652
  355.9 39.2 %collective-permute-start.11 = (f32[256,128]{1,0:T(8,128)S(1)}, f32[256,128]{1,0:T(8,128)S(1)}, u32[]{:S(2)}, u32[]{:S(2)}) collective-permute-start(f32[256,128]{1,0:T(8,128)S(1)} %select_select_fusion.3), channel_id=1, source_target_pairs={{0,8},{8,0},{1,9},{9,1},{2,10},{10,2},{3,11},{11,3},{4,12},{12,4},... | collective-permute-start | bytes 393224 | tf_op jit(solution)/shard_map/ppermute | solution.py:23
  458.9 124.0 %copy-start.25 = (f32[12]{0:T(128)S(1)}, f32[12]{0:T(128)}, u32[]{:S(2)}) copy-start(f32[12]{0:T(128)} %constant.1644.clone) | copy-start | bytes 148
  481.9 5.9 collective-permute-start.12
  487.8 5.0 collective-permute-start.13
  492.9 5.7 collective-permute-start.14
  498.7 86.2 %collective-permute-start.15 = (f32[256,128]{1,0:T(8,128)S(1)}, f32[256,128]{1,0:T(8,128)S(1)}, u32[]{:S(2)}, u32[]{:S(2)}) collective-permute-start(f32[256,128]{1,0:T(8,128)S(1)} %select_select_fusion), channel_id=1, source_target_pairs={{0,1},{1,0},{2,3},{3,2},{4,5},{5,4},{6,7},{7,6},{8,9},{9,8},{10,11... | collective-permute-start | bytes 393224 | tf_op jit(solution)/shard_map/ppermute | solution.py:23
  (26 other events, 459.3 us)
Sparse Core Ops, SparseCore 0:
  490.2 90.9 all-reduce.2
where the time goes:
time: 684 us; the launch traced here: 673 us
  local copies, waits for them, and re-layouts  227 us (33%)
  other arithmetic  148 us (22%)
  waiting for transfers between devices  135 us (20%)
  matrix products  105 us (15%)
  blocking collectives  30 us (4%)
  between operations  15.4 us (2%)
  starting transfers between devices  12.5 us (2%)
    unnamed x95, local copies, waits for them, and re-layouts  123 us
    psum x1, waiting for transfers between devices, shards(): totals = lax.psum((stacked, point_grad, bias_grad), 'gx')  82.5 us
    scatter x12, local copies, waits for them, and re-layouts, mix_levels(): output.at[stride::2 * stride]  72.3 us
    ppermute x16, waiting for transfers between devices, partner_2(): return lax.ppermute(block, axis, route)  52.4 us
    scatter x14, other arithmetic, haar_inverse(): shaped = shaped.at[:, 1, 0].set((coarse_rows + detail_rows) * root_half)  31.5 us
    psum x1, blocking collectives, shards(): totals = lax.psum((stacked, point_grad, bias_grad), 'gx')  30 us
    scatter x14, other arithmetic, haar_inverse(): shaped = shaped.at[:, 0, 0].set((coarse_rows - detail_rows) * root_half)  29.8 us
    dot_general x9, matrix products, outer_sum(): lax.dot_general(left_flat, right_flat, (((0,), (0,)), ((), ())), preferre...  29.6 us
  transfers between devices with their start and end apart: 17, of which 15 were waited for; matrix products, arithmetic and copies ran while one was open for 2% of the time, Pallas kernels for 0%

commit v1 on v0

v1 whole, which is shorter than its diff:
```python
import functools
import math

import jax
import jax.numpy as jnp
from jax import lax
from jax.experimental import pallas as pl
from jax.experimental.pallas import tpu as pltpu
from jax.sharding import PartitionSpec as P

BF = jnp.bfloat16
F32 = jnp.float32
TILE = 32
GELU_A = math.sqrt(2.0 / math.pi)
GELU_B = 0.044715


def level_starts(depth):
    rows = 1 << depth
    starts, at = [], 0
    for level in range(depth):
        starts.append(at)
        at += rows >> (level + 1)
    return starts


def forward_tree(leaf, put, low, depth, starts):
    if depth == 0:
        return leaf(low)
    half = 1 << (depth - 1)
    even = forward_tree(leaf, put, low, depth - 1, starts)
    odd = forward_tree(leaf, put, low + half, depth - 1, starts)
    put(starts[depth - 1] + (low >> depth), odd - even)
    return even + odd


def inverse_tree(take, leaf, low, depth, starts, value):
    if depth == 0:
        leaf(low, value)
        return
    half = 1 << (depth - 1)
    detail = take(starts[depth - 1] + (low >> depth))
    inverse_tree(take, leaf, low, depth - 1, starts, value - detail)
    inverse_tree(take, leaf, low + half, depth - 1, starts, value + detail)


def mix_details(coeffs_ref, weight_ref, mixed_ref, depth, starts, back):
    columns, channels = coeffs_ref.shape[1:]
    for level in range(depth):
        count = 1 << (depth - 1 - level)
        span = slice(starts[level], starts[level] + count)
        left = coeffs_ref[span].reshape(count * columns, channels)
        dims = (((1,), (1 if back else 0,)), ((), ()))
        mixed = lax.dot_general(left, weight_ref[level], dims, preferred_element_type=F32)
        mixed_ref[span] = mixed.reshape(count, columns, channels)


def kernel_a(depth, fields_ref, weight_ref, coeffs_ref, partial_ref, mixed_ref):
    starts = level_starts(depth)

    def put(row, value):
        coeffs_ref[row] = value.astype(BF)

    forward_tree(lambda row: fields_ref[row].astype(F32), put, 0, depth, starts)
    coeffs_ref[(1 << depth) - 1] = jnp.zeros(coeffs_ref.shape[1:], BF)
    mix_details(coeffs_ref, weight_ref, mixed_ref, depth, starts, False)

    def leaf(row, value):
        partial_ref[row] = value.astype(BF)

    zero = jnp.zeros(mixed_ref.shape[1:], F32)
    inverse_tree(lambda row: mixed_ref[row], leaf, 0, depth, starts, zero)


def kernel_b(depth, partial_ref, cot_ref, base_ref, coeffs_ref, back_ref, coarse_ref, grads_ref):
    starts = level_starts(depth)
    columns, channels = base_ref.shape
    base = base_ref[...]

    def leaf(row):
        v = partial_ref[row].astype(F32) + base
        k = (GELU_A * GELU_B) * (v * v)
        t = jnp.tanh(v * (k + GELU_A))
        w = v * (3.0 * k + GELU_A)
        slope = (0.5 + 0.5 * t) * (1.0 + w * (1.0 - t))
        return (cot_ref[row].astype(F32) * slope).astype(BF).astype(F32)

    def put(row, value):
        back_ref[row] = value.astype(BF)

    coarse_ref[...] = forward_tree(leaf, put, 0, depth, starts)
    back_ref[(1 << depth) - 1] = jnp.zeros((columns, channels), BF)

    @pl.when(pl.program_id(0) == 0)
    def _():
        grads_ref[...] = jnp.zeros_like(grads_ref)

    for level in range(depth):
        count = 1 << (depth - 1 - level)
        span = slice(starts[level], starts[level] + count)
        left = coeffs_ref[span].reshape(count * columns, channels)
        right = back_ref[span].reshape(count * columns, channels)
        grads_ref[level] += lax.dot_general(
            left, right, (((0,), (0,)), ((), ())), preferred_element_type=F32
        )


def kernel_c(depth, back_ref, base_ref, weight_ref, out_ref, mixed_ref):
    starts = level_starts(depth)
    mix_details(back_ref, weight_ref, mixed_ref, depth, starts, True)

    def leaf(row, value):
        out_ref[row] = value.astype(BF)

    inverse_tree(lambda row: mixed_ref[row], leaf, 0, depth, starts, base_ref[...])


def swap(block, stride):
    count = lax.axis_size("gx")
    return lax.ppermute(block, "gx", [(low, low ^ stride) for low in range(count)])


def cross_coeffs(coarse, position, depth):
    found = []
    for degree in range(depth):
        other = swap(coarse, 1 << degree)
        upper = (position >> degree) % 2 == 1
        found.append(jnp.where(upper, coarse - other, other - coarse))
        coarse = coarse + other
    return found + [coarse]


def cross_mix(coeffs_b, weights, position, back):
    spec = "yc,dc->yd" if back else "yc,cd->yd"
    total = jnp.einsum(spec, coeffs_b[-1], weights[-1], preferred_element_type=F32)
    for degree in reversed(range(len(coeffs_b) - 1)):
        upper = (position >> degree) % 2 == 1
        part = jnp.einsum(spec, coeffs_b[degree], weights[degree], preferred_element_type=F32)
        total = total + jnp.where(upper, part, -part)
    return total


def sum_devices(block, position, depth):
    for degree in range(depth):
        half = block.shape[0] // 2
        upper = (position >> degree) % 2 == 1
        low, high = block[:half], block[half:]
        block = jnp.where(upper, high, low) + swap(jnp.where(upper, low, high), 1 << degree)
    for degree in reversed(range(depth)):
        other = swap(block, 1 << degree)
        upper = (position >> degree) % 2 == 1
        block = jnp.where(
            upper, jnp.concatenate([other, block]), jnp.concatenate([block, other])
        )
    return block


def shards(fields, cotangent, point_weight, mix_weight, bias_vec):
    rows, columns, channels = fields.shape
    depth = rows.bit_length() - 1
    device_count = lax.axis_size("gx")
    cross_depth = device_count.bit_length() - 1
    levels = depth + cross_depth
    position = lax.axis_index("gx")
    tile = min(TILE, columns)
    grid = (columns // tile,)
    params = pltpu.CompilerParams(
        dimension_semantics=("arbitrary",), vmem_limit_bytes=48 * 1024 * 1024
    )
    block = pl.BlockSpec((rows, tile, channels), lambda i: (0, i, 0))
    line = pl.BlockSpec((tile, channels), lambda i: (i, 0))
    whole = pl.BlockSpec((depth, channels, channels), lambda i: (0, 0, 0))
    flops = 2 * rows * columns * channels * channels
    moved = 2 * rows * columns * channels

    def cost(passes):
        return pl.CostEstimate(
            flops=flops, bytes_accessed=passes * moved, transcendentals=rows * columns * channels
        )

    powers = [2.0 ** -(level + 1) for level in range(levels)] + [2.0**-levels]
    scale = jnp.array(powers, F32)[:, None, None]
    joined = ((mix_weight.astype(F32) + point_weight.astype(F32)) * scale).astype(BF)

    coarse = jnp.sum(fields.astype(F32), axis=0)
    coeffs_up = [c.astype(BF) for c in cross_coeffs(coarse, position, cross_depth)]
    base = cross_mix(coeffs_up, joined[depth:], position, False) + bias_vec.astype(F32)

    big = jax.ShapeDtypeStruct((rows, columns, channels), BF)
    mixed_scratch = pltpu.VMEM((rows, tile, channels), F32)
    coeffs, partial = pl.pallas_call(
        functools.partial(kernel_a, depth),
        grid=grid,
        in_specs=[block, whole],
        out_specs=[block, block],
        out_shape=[big, big],
        scratch_shapes=[mixed_scratch],
        compiler_params=params,
        cost_estimate=cost(3),
    )(fields, joined[:depth])

    back, slope_coarse, grads = pl.pallas_call(
        functools.partial(kernel_b, depth),
        grid=grid,
        in_specs=[block, block, line, block],
        out_specs=[block, line, whole],
        out_shape=[
            big,
            jax.ShapeDtypeStruct((columns, channels), F32),
            jax.ShapeDtypeStruct((depth, channels, channels), F32),
        ],
        compiler_params=params,
        cost_estimate=cost(4),
    )(partial, cotangent, base, coeffs)

    slope_up = cross_coeffs(slope_coarse, position, cross_depth)
    slope_up_b = [c.astype(BF) for c in slope_up]
    back_base = cross_mix(slope_up_b, joined[depth:], position, True)

    high = slope_coarse.astype(BF)
    low = (slope_coarse - high.astype(F32)).astype(BF)
    outer = functools.partial(jnp.einsum, "yc,yd->cd", preferred_element_type=F32)
    upper_grads = []
    for degree in range(cross_depth - 1):
        part = outer(coeffs_up[degree], high) + outer(coeffs_up[degree], low)
        upper_grads.append(jnp.where((position >> degree) % 2 == 1, part, -part))
    partial_grads = jnp.concatenate([grads] + [g[None] for g in upper_grads])
    summed = sum_devices(partial_grads.reshape(-1, channels), position, cross_depth)
    summed = summed.reshape(-1, channels, channels)
    top = [outer(c, b) for c, b in zip(coeffs_up[-2:], slope_up_b[-2:])]
    raw = jnp.concatenate([summed, jnp.stack(top)]) * scale

    grad_input = pl.pallas_call(
        functools.partial(kernel_c, depth),
        grid=grid,
        in_specs=[block, line, whole],
        out_specs=block,
        out_shape=big,
        scratch_shapes=[mixed_scratch],
        compiler_params=params,
        cost_estimate=cost(2),
    )(back, back_base, joined[:depth])

    global_rows = rows * device_count
    counts = [columns * global_rows / 2 ** (level + 1) for level in range(levels)] + [columns]
    factors = jnp.array([1.0 / math.sqrt(value) for value in counts], F32)
    scale_all = 1.0 / math.sqrt(global_rows * columns)
    grad_mix = (raw * factors[:, None, None]).astype(BF)
    grad_point = (jnp.sum(raw, axis=0) * scale_all).astype(BF)
    grad_bias = (jnp.sum(slope_up[-1], axis=0) * scale_all).astype(BF)
    return (grad_input, grad_mix, grad_point, grad_bias)


def solution(mesh):
    in_specs = (P("gx", "ga", None), P("gx", "ga", None), P(), P(), P())
    out_specs = (P("gx", "ga", None), P("ga", None, None), P("ga", None), P("ga"))
    return jax.shard_map(shards, mesh=mesh, in_specs=in_specs, out_specs=out_specs, check_vma=False)
```

time: 684 us -> 113 us (0.17); the launches traced: 673 us -> 112 us
  local copies, waits for them, and re-layouts: 227 us -> 0.04 us
  other arithmetic: 148 us -> 7.33 us
  matrix products: 105 us -> 3.08 us
  waiting for transfers between devices: 135 us -> 38.1 us
  Pallas kernels: 0 us -> 43.8 us
  blocking collectives: 30 us -> 0 us
  between operations: 15.4 us -> 0.97 us
    unnamed x95 -> x10, local copies, waits for them, and re-layouts: 123 us -> 0.03 us
    scatter x60 -> x0, other arithmetic: 105 us -> none  [the longest x14 31.5 us: haar_inverse(): shaped = shaped.at[:, 1, 0].set((coarse_rows + detail_rows) * root_half)]
    dot_general x27 -> x18, matrix products: 105 us -> 3.08 us  [the longest x6 1.19 us: shards(): part = outer(coeffs_up[degree], high) + outer(coeffs_up[degree], low)]
    psum x1 -> x0, waiting for transfers between devices: 82.5 us -> none  [shards(): totals = lax.psum((stacked, point_grad, bias_grad), 'gx')]
    scatter x12 -> x0, local copies, waits for them, and re-layouts: 72.3 us -> none  [mix_levels(): output.at[stride::2 * stride]]
    pallas_call x0 -> x3, Pallas kernels: none -> 43.8 us  [the longest x1 20 us: shards(): pl.pallas_call(functools.partial(kernel_b, depth), grid=grid, in_specs=[b...]
    psum x1 -> x0, blocking collectives: 30 us -> none  [shards(): totals = lax.psum((stacked, point_grad, bias_grad), 'gx')]
    reshape x2 -> x0, other arithmetic: 23.1 us -> none  [haar_forward(): signal.reshape((signal.shape[0] // (2 * stride), 2, stride) + signal.shap...]
  transfers between devices with their start and end apart: 17 -> 16, of which waited for: 15 -> 13; matrix products, arithmetic and copies ran while one was open for 2% -> 2% of each run, Pallas kernels for 0% -> 21%
where the time goes in v1:
time: 113 us; the launch traced here: 112 us
  Pallas kernels  43.8 us (39%)
  waiting for transfers between devices  38.1 us (34%)
  starting transfers between devices  18.7 us (17%)
  other arithmetic  7.33 us (6%)
  matrix products  3.08 us (3%)
    ppermute x16, waiting for transfers between devices, swap(): lax.ppermute(block, 'gx', [(low, low ^ stride) for low in range(count)])  38.1 us
    pallas_call x1, Pallas kernels, shards(): pl.pallas_call(functools.partial(kernel_b, depth), grid=grid, in_specs=[b...  20 us
    ppermute x16, starting transfers between devices, swap(): lax.ppermute(block, 'gx', [(low, low ^ stride) for low in range(count)])  18.7 us
    pallas_call x1, Pallas kernels, shards(): pl.pallas_call(functools.partial(kernel_a, depth), grid=grid, in_specs=[b...  13.2 us
    pallas_call x1, Pallas kernels, shards(): pl.pallas_call(functools.partial(kernel_c, depth), grid=grid, in_specs=[b...  10.7 us
    reduce_sum x1, other arithmetic, shards(): coarse = jnp.sum(fields.astype(F32), axis=0)  4.61 us
  transfers between devices with their start and end apart: 16, of which 13 were waited for; matrix products, arithmetic and copies ran while one was open for 2% of the time, Pallas kernels for 21%

profile of v1, /device:TPU:0, one launch (start us, length us, event | category | flops | bytes accessed | tf_op | source)
XLA Modules:
  0.0 112.0 jit_solution(5804430519506115671)
XLA Ops:
  0.7 4.6 %convert_reduce_fusion = f32[256,128]{1,0:T(8,128)S(1)} fusion(bf16[128,256,128]{2,1,0:T(8,128)(2,1)} %fields_ref.1), kind=kLoop, calls=%fused_computation | loop fusion | flops 8355840 | bytes 8519680 | tf_op jit(solution)/shard_map/reduce_sum | solution.py:185
  6.0 13.2 %shard_map.102 = (bf16[128,256,128]{2,1,0:T(8,128)(2,1)}, bf16[128,256,128]{2,1,0:T(8,128)(2,1)}) custom-call(bf16[128,256,128]{2,1,0:T(8,128)(2,1)} %fields_ref.1, bf16[7,128,128]{2,1,0:T(8,128)(2,1)S(1)} %slice.72.weight_ref), custom_call_target="tpu_custom_call" | custom-call | flops 1073741824 | bytes 25165824 | tf_op jit(solution)/shard_map/pallas_call | solution.py:191
  19.2 2.6 %collective-permute-start.1 = (f32[256,128]{1,0:T(8,128)S(1)}, f32[256,128]{1,0:T(8,128)S(1)}, u32[]{:S(2)}, u32[]{:S(2)}) collective-permute-start(f32[256,128]{1,0:T(8,128)S(1)} %get-tuple-element.24), channel_id=1, source_target_pairs={{0,2},{1,3},{2,0},{3,1},{4,6},{5,7},{6,4},{7,5},{8,10},{9,11},{10,... | collective-permute-start | bytes 393224 | tf_op jit(solution)/shard_map/ppermute | solution.py:120
  22.0 4.0 %collective-permute-done.1 = f32[256,128]{1,0:T(8,128)S(1)} collective-permute-done((f32[256,128]{1,0:T(8,128)S(1)}, f32[256,128]{1,0:T(8,128)S(1)}, u32[]{:S(2)}, u32[]{:S(2)}) %collective-permute-start.1) | collective-permute-done | bytes 131104 | tf_op jit(solution)/shard_map/ppermute | solution.py:120
  26.0 1.9 %collective-permute-start.2 = (f32[256,128]{1,0:T(8,128)S(1)}, f32[256,128]{1,0:T(8,128)S(1)}, u32[]{:S(2)}, u32[]{:S(2)}) collective-permute-start(f32[256,128]{1,0:T(8,128)S(1)} %get-tuple-element.26), channel_id=1, source_target_pairs={{0,4},{1,5},{2,6},{3,7},{4,0},{5,1},{6,2},{7,3},{8,12},{9,13},{10,... | collective-permute-start | bytes 393224 | tf_op jit(solution)/shard_map/ppermute | solution.py:120
  28.0 3.3 %collective-permute-done.2 = f32[256,128]{1,0:T(8,128)S(1)} collective-permute-done((f32[256,128]{1,0:T(8,128)S(1)}, f32[256,128]{1,0:T(8,128)S(1)}, u32[]{:S(2)}, u32[]{:S(2)}) %collective-permute-start.2) | collective-permute-done | bytes 131104 | tf_op jit(solution)/shard_map/ppermute | solution.py:120
  31.4 2.7 %collective-permute-start.3 = (f32[256,128]{1,0:T(8,128)S(1)}, f32[256,128]{1,0:T(8,128)S(1)}, u32[]{:S(2)}, u32[]{:S(2)}) collective-permute-start(f32[256,128]{1,0:T(8,128)S(1)} %get-tuple-element.28), channel_id=1, source_target_pairs={{0,8},{1,9},{2,10},{3,11},{4,12},{5,13},{6,14},{7,15},{8,0},{9,1},... | collective-permute-start | bytes 393224 | tf_op jit(solution)/shard_map/ppermute | solution.py:120
  34.2 5.4 %collective-permute-done.3 = f32[256,128]{1,0:T(8,128)S(1)} collective-permute-done((f32[256,128]{1,0:T(8,128)S(1)}, f32[256,128]{1,0:T(8,128)S(1)}, u32[]{:S(2)}, u32[]{:S(2)}) %collective-permute-start.3) | collective-permute-done | bytes 131104 | tf_op jit(solution)/shard_map/ppermute | solution.py:120
  40.0 20.0 %shard_map.103 = (bf16[128,256,128]{2,1,0:T(8,128)(2,1)}, f32[256,128]{1,0:T(8,128)S(1)}, f32[7,128,128]{2,1,0:T(8,128)S(1)}) custom-call(bf16[128,256,128]{2,1,0:T(8,128)(2,1)} %get-tuple-element.9.partial_ref, bf16[128,256,128]{2,1,0:T(8,128)(2,1)} %cot_ref.1, f32[256,128]{1,0:T(8,128)S(1)} %fusion.6.base_ref, ...), custom_call_target="tpu_custom_call" | custom-call | flops 1073741824 | bytes 33554432 | tf_op jit(solution)/shard_map/pallas_call | solution.py:202
  60.0 1.3 %collective-permute-done.4 = f32[256,128]{1,0:T(8,128)S(1)} collective-permute-done((f32[256,128]{1,0:T(8,128)S(1)}, f32[256,128]{1,0:T(8,128)S(1)}, u32[]{:S(2)}, u32[]{:S(2)}) %collective-permute-start.4) | collective-permute-done | bytes 131104 | tf_op jit(solution)/shard_map/ppermute | solution.py:120
  62.8 1.3 %collective-permute-start.5 = (f32[256,128]{1,0:T(8,128)S(1)}, f32[256,128]{1,0:T(8,128)S(1)}, u32[]{:S(2)}, u32[]{:S(2)}) collective-permute-start(f32[256,128]{1,0:T(8,128)S(1)} %get-tuple-element.31), channel_id=1, source_target_pairs={{0,2},{1,3},{2,0},{3,1},{4,6},{5,7},{6,4},{7,5},{8,10},{9,11},{10,... | collective-permute-start | bytes 393224 | tf_op jit(solution)/shard_map/ppermute | solution.py:120
  64.4 1.4 %collective-permute-start.9 = (f32[320,128]{1,0:T(8,128)S(1)}, f32[320,128]{1,0:T(8,128)S(1)}, u32[]{:S(2)}, u32[]{:S(2)}) collective-permute-start(f32[320,128]{1,0:T(8,128)S(1)} %slice_select_fusion.2), channel_id=1, source_target_pairs={{0,2},{1,3},{2,0},{3,1},{4,6},{5,7},{6,4},{7,5},{8,10},{9,11},{10,... | collective-permute-start | bytes 491528 | tf_op jit(solution)/shard_map/ppermute | solution.py:120
  65.9 3.3 %collective-permute-done.5 = f32[256,128]{1,0:T(8,128)S(1)} collective-permute-done((f32[256,128]{1,0:T(8,128)S(1)}, f32[256,128]{1,0:T(8,128)S(1)}, u32[]{:S(2)}, u32[]{:S(2)}) %collective-permute-start.5) | collective-permute-done | bytes 131104 | tf_op jit(solution)/shard_map/ppermute | solution.py:120
  69.7 2.4 %collective-permute-done.9 = f32[320,128]{1,0:T(8,128)S(1)} collective-permute-done((f32[320,128]{1,0:T(8,128)S(1)}, f32[320,128]{1,0:T(8,128)S(1)}, u32[]{:S(2)}, u32[]{:S(2)}) %collective-permute-start.9) | collective-permute-done | bytes 163872 | tf_op jit(solution)/shard_map/ppermute | solution.py:120
  72.9 1.3 %collective-permute-done.6 = f32[256,128]{1,0:T(8,128)S(1)} collective-permute-done((f32[256,128]{1,0:T(8,128)S(1)}, f32[256,128]{1,0:T(8,128)S(1)}, u32[]{:S(2)}, u32[]{:S(2)}) %collective-permute-start.6) | collective-permute-done | bytes 131104 | tf_op jit(solution)/shard_map/ppermute | solution.py:120
  74.2 2.1 %collective-permute-start.7 = (f32[256,128]{1,0:T(8,128)S(1)}, f32[256,128]{1,0:T(8,128)S(1)}, u32[]{:S(2)}, u32[]{:S(2)}) collective-permute-start(f32[256,128]{1,0:T(8,128)S(1)} %add.139), channel_id=1, source_target_pairs={{0,8},{1,9},{2,10},{3,11},{4,12},{5,13},{6,14},{7,15},{8,0},{9,1},... | collective-permute-start | bytes 393224 | tf_op jit(solution)/shard_map/ppermute | solution.py:120
  77.1 2.4 %collective-permute-start.11 = (f32[80,128]{1,0:T(8,128)S(1)}, f32[80,128]{1,0:T(8,128)S(1)}, u32[]{:S(2)}, u32[]{:S(2)}) collective-permute-start(f32[80,128]{1,0:T(8,128)S(1)} %slice_select_fusion.4), channel_id=1, source_target_pairs={{0,8},{1,9},{2,10},{3,11},{4,12},{5,13},{6,14},{7,15},{8,0},{9,1},... | collective-permute-start | bytes 122888 | tf_op jit(solution)/shard_map/ppermute | solution.py:120
  79.7 4.2 %collective-permute-done.11 = f32[80,128]{1,0:T(8,128)S(1)} collective-permute-done((f32[80,128]{1,0:T(8,128)S(1)}, f32[80,128]{1,0:T(8,128)S(1)}, u32[]{:S(2)}, u32[]{:S(2)}) %collective-permute-start.11) | collective-permute-done | bytes 40992 | tf_op jit(solution)/shard_map/ppermute | solution.py:120
  84.6 4.3 %collective-permute-done.12 = f32[80,128]{1,0:T(8,128)S(1)} collective-permute-done((f32[80,128]{1,0:T(8,128)S(1)}, f32[80,128]{1,0:T(8,128)S(1)}, u32[]{:S(2)}, u32[]{:S(2)}) %collective-permute-start.12) | collective-permute-done | bytes 40992 | tf_op jit(solution)/shard_map/ppermute | solution.py:120
  89.3 4.1 %collective-permute-done.13 = f32[160,128]{1,0:T(8,128)S(1)} collective-permute-done((f32[160,128]{1,0:T(8,128)S(1)}, f32[160,128]{1,0:T(8,128)S(1)}, u32[]{:S(2)}, u32[]{:S(2)}) %collective-permute-start.13) | collective-permute-done | bytes 81952 | tf_op jit(solution)/shard_map/ppermute | solution.py:120
  93.5 1.6 %collective-permute-start.14 = (f32[320,128]{1,0:T(8,128)S(1)}, f32[320,128]{1,0:T(8,128)S(1)}, u32[]{:S(2)}, u32[]{:S(2)}) collective-permute-start(f32[320,128]{1,0:T(8,128)S(1)} %maximum_select_fusion.2), channel_id=1, source_target_pairs={{0,2},{1,3},{2,0},{3,1},{4,6},{5,7},{6,4},{7,5},{8,10},{9,11},{10,... | collective-permute-start | bytes 491528 | tf_op jit(solution)/shard_map/ppermute | solution.py:120
  95.4 3.5 %collective-permute-done.14 = f32[320,128]{1,0:T(8,128)S(1)} collective-permute-done((f32[320,128]{1,0:T(8,128)S(1)}, f32[320,128]{1,0:T(8,128)S(1)}, u32[]{:S(2)}, u32[]{:S(2)}) %collective-permute-start.14) | collective-permute-done | bytes 163872 | tf_op jit(solution)/shard_map/ppermute | solution.py:120
  99.2 10.7 %shard_map.104 = bf16[128,256,128]{2,1,0:T(8,128)(2,1)} custom-call(bf16[128,256,128]{2,1,0:T(8,128)(2,1)} %get-tuple-element.11.back_ref, f32[256,128]{1,0:T(8,128)S(1)} %fusion.2.base_ref, bf16[7,128,128]{2,1,0:T(8,128)(2,1)S(1)} %slice.72.weight_ref), custom_call_target="tpu_custom_call" | custom-call | flops 1073741824 | bytes 16777216 | tf_op jit(solution)/shard_map/pallas_call | solution.py:233
  110.4 0.9 fusion.7
  (67 shorter events, 8.6 us)
Async XLA Ops:
  0.6 5.2 %copy-start.2 = (f32[12]{0:T(128)S(1)}, f32[12]{0:T(128)}, u32[]{:S(2)}) copy-start(f32[12]{0:T(128)} %constant.88.clone) | copy-start | bytes 148
  0.6 5.2 %copy-start.1 = (bf16[128,128]{1,0:T(8,128)(2,1)S(1)}, bf16[128,128]{1,0:T(8,128)(2,1)}, u32[]{:S(2)}) copy-start(bf16[128,128]{1,0:T(8,128)(2,1)} %param.9) | copy-start | bytes 98308
  0.7 5.2 %copy-start = (bf16[12,128,128]{2,1,0:T(8,128)(2,1)S(1)}, bf16[12,128,128]{2,1,0:T(8,128)(2,1)}, u32[]{:S(2)}) copy-start(bf16[12,128,128]{2,1,0:T(8,128)(2,1)} %param.10) | copy-start | bytes 1179652
  0.7 5.3 %copy-start.4 = (bf16[128]{0:T(256)(128)(2,1)S(1)}, bf16[128]{0:T(256)(128)(2,1)}, u32[]{:S(2)}) copy-start(bf16[128]{0:T(256)(128)(2,1)} %param.11) | copy-start | bytes 772
  5.3 13.9 %collective-permute-start = (f32[256,128]{1,0:T(8,128)S(1)}, f32[256,128]{1,0:T(8,128)S(1)}, u32[]{:S(2)}, u32[]{:S(2)}) collective-permute-start(f32[256,128]{1,0:T(8,128)S(1)} %convert_reduce_fusion), channel_id=1, source_target_pairs={{0,1},{1,0},{2,3},{3,2},{4,5},{5,4},{6,7},{7,6},{8,9},{9,8},{10,11... | collective-permute-start | bytes 393224 | tf_op jit(solution)/shard_map/ppermute | solution.py:120
  19.2 6.7 %collective-permute-start.1 = (f32[256,128]{1,0:T(8,128)S(1)}, f32[256,128]{1,0:T(8,128)S(1)}, u32[]{:S(2)}, u32[]{:S(2)}) collective-permute-start(f32[256,128]{1,0:T(8,128)S(1)} %get-tuple-element.24), channel_id=1, source_target_pairs={{0,2},{1,3},{2,0},{3,1},{4,6},{5,7},{6,4},{7,5},{8,10},{9,11},{10,... | collective-permute-start | bytes 393224 | tf_op jit(solution)/shard_map/ppermute | solution.py:120
  26.0 5.4 %collective-permute-start.2 = (f32[256,128]{1,0:T(8,128)S(1)}, f32[256,128]{1,0:T(8,128)S(1)}, u32[]{:S(2)}, u32[]{:S(2)}) collective-permute-start(f32[256,128]{1,0:T(8,128)S(1)} %get-tuple-element.26), channel_id=1, source_target_pairs={{0,4},{1,5},{2,6},{3,7},{4,0},{5,1},{6,2},{7,3},{8,12},{9,13},{10,... | collective-permute-start | bytes 393224 | tf_op jit(solution)/shard_map/ppermute | solution.py:120
  31.4 8.2 %collective-permute-start.3 = (f32[256,128]{1,0:T(8,128)S(1)}, f32[256,128]{1,0:T(8,128)S(1)}, u32[]{:S(2)}, u32[]{:S(2)}) collective-permute-start(f32[256,128]{1,0:T(8,128)S(1)} %get-tuple-element.28), channel_id=1, source_target_pairs={{0,8},{1,9},{2,10},{3,11},{4,12},{5,13},{6,14},{7,15},{8,0},{9,1},... | collective-permute-start | bytes 393224 | tf_op jit(solution)/shard_map/ppermute | solution.py:120
  60.0 1.3 %collective-permute-start.4 = (f32[256,128]{1,0:T(8,128)S(1)}, f32[256,128]{1,0:T(8,128)S(1)}, u32[]{:S(2)}, u32[]{:S(2)}) collective-permute-start(f32[256,128]{1,0:T(8,128)S(1)} %get-tuple-element.12), channel_id=1, source_target_pairs={{0,1},{1,0},{2,3},{3,2},{4,5},{5,4},{6,7},{7,6},{8,9},{9,8},{10,11... | collective-permute-start | bytes 393224 | tf_op jit(solution)/shard_map/ppermute | solution.py:120
  62.6 1.7 %collective-permute-start.8 = (f32[640,128]{1,0:T(8,128)S(1)}, f32[640,128]{1,0:T(8,128)S(1)}, u32[]{:S(2)}, u32[]{:S(2)}) collective-permute-start(f32[640,128]{1,0:T(8,128)S(1)} %bitcast.58), channel_id=1, source_target_pairs={{0,1},{1,0},{2,3},{3,2},{4,5},{5,4},{6,7},{7,6},{8,9},{9,8},{10,11... | collective-permute-start | bytes 983048 | tf_op jit(solution)/shard_map/ppermute | solution.py:120
  62.8 6.3 %collective-permute-start.5 = (f32[256,128]{1,0:T(8,128)S(1)}, f32[256,128]{1,0:T(8,128)S(1)}, u32[]{:S(2)}, u32[]{:S(2)}) collective-permute-start(f32[256,128]{1,0:T(8,128)S(1)} %get-tuple-element.31), channel_id=1, source_target_pairs={{0,2},{1,3},{2,0},{3,1},{4,6},{5,7},{6,4},{7,5},{8,10},{9,11},{10,... | collective-permute-start | bytes 393224 | tf_op jit(solution)/shard_map/ppermute | solution.py:120
  64.4 7.7 %collective-permute-start.9 = (f32[320,128]{1,0:T(8,128)S(1)}, f32[320,128]{1,0:T(8,128)S(1)}, u32[]{:S(2)}, u32[]{:S(2)}) collective-permute-start(f32[320,128]{1,0:T(8,128)S(1)} %slice_select_fusion.2), channel_id=1, source_target_pairs={{0,2},{1,3},{2,0},{3,1},{4,6},{5,7},{6,4},{7,5},{8,10},{9,11},{10,... | collective-permute-start | bytes 491528 | tf_op jit(solution)/shard_map/ppermute | solution.py:120
  69.2 5.0 %collective-permute-start.6 = (f32[256,128]{1,0:T(8,128)S(1)}, f32[256,128]{1,0:T(8,128)S(1)}, u32[]{:S(2)}, u32[]{:S(2)}) collective-permute-start(f32[256,128]{1,0:T(8,128)S(1)} %add.138), channel_id=1, source_target_pairs={{0,4},{1,5},{2,6},{3,7},{4,0},{5,1},{6,2},{7,3},{8,12},{9,13},{10,... | collective-permute-start | bytes 393224 | tf_op jit(solution)/shard_map/ppermute | solution.py:120
  72.2 4.9 %collective-permute-start.10 = (f32[160,128]{1,0:T(8,128)S(1)}, f32[160,128]{1,0:T(8,128)S(1)}, u32[]{:S(2)}, u32[]{:S(2)}) collective-permute-start(f32[160,128]{1,0:T(8,128)S(1)} %slice_select_fusion.3), channel_id=1, source_target_pairs={{0,4},{1,5},{2,6},{3,7},{4,0},{5,1},{6,2},{7,3},{8,12},{9,13},{10,... | collective-permute-start | bytes 245768 | tf_op jit(solution)/shard_map/ppermute | solution.py:120
  74.2 10.3 %collective-permute-start.7 = (f32[256,128]{1,0:T(8,128)S(1)}, f32[256,128]{1,0:T(8,128)S(1)}, u32[]{:S(2)}, u32[]{:S(2)}) collective-permute-start(f32[256,128]{1,0:T(8,128)S(1)} %add.139), channel_id=1, source_target_pairs={{0,8},{1,9},{2,10},{3,11},{4,12},{5,13},{6,14},{7,15},{8,0},{9,1},... | collective-permute-start | bytes 393224 | tf_op jit(solution)/shard_map/ppermute | solution.py:120
  77.1 6.7 %collective-permute-start.11 = (f32[80,128]{1,0:T(8,128)S(1)}, f32[80,128]{1,0:T(8,128)S(1)}, u32[]{:S(2)}, u32[]{:S(2)}) collective-permute-start(f32[80,128]{1,0:T(8,128)S(1)} %slice_select_fusion.4), channel_id=1, source_target_pairs={{0,8},{1,9},{2,10},{3,11},{4,12},{5,13},{6,14},{7,15},{8,0},{9,1},... | collective-permute-start | bytes 122888 | tf_op jit(solution)/shard_map/ppermute | solution.py:120
  83.8 5.1 %collective-permute-start.12 = (f32[80,128]{1,0:T(8,128)S(1)}, f32[80,128]{1,0:T(8,128)S(1)}, u32[]{:S(2)}, u32[]{:S(2)}) collective-permute-start(f32[80,128]{1,0:T(8,128)S(1)} %select_add_fusion.2), channel_id=1, source_target_pairs={{0,8},{1,9},{2,10},{3,11},{4,12},{5,13},{6,14},{7,15},{8,0},{9,1},... | collective-permute-start | bytes 122888 | tf_op jit(solution)/shard_map/ppermute | solution.py:120
  89.0 4.5 %collective-permute-start.13 = (f32[160,128]{1,0:T(8,128)S(1)}, f32[160,128]{1,0:T(8,128)S(1)}, u32[]{:S(2)}, u32[]{:S(2)}) collective-permute-start(f32[160,128]{1,0:T(8,128)S(1)} %maximum_select_fusion.3), channel_id=1, source_target_pairs={{0,4},{1,5},{2,6},{3,7},{4,0},{5,1},{6,2},{7,3},{8,12},{9,13},{10,... | collective-permute-start | bytes 245768 | tf_op jit(solution)/shard_map/ppermute | solution.py:120
  93.5 5.4 %collective-permute-start.14 = (f32[320,128]{1,0:T(8,128)S(1)}, f32[320,128]{1,0:T(8,128)S(1)}, u32[]{:S(2)}, u32[]{:S(2)}) collective-permute-start(f32[320,128]{1,0:T(8,128)S(1)} %maximum_select_fusion.2), channel_id=1, source_target_pairs={{0,2},{1,3},{2,0},{3,1},{4,6},{5,7},{6,4},{7,5},{8,10},{9,11},{10,... | collective-permute-start | bytes 491528 | tf_op jit(solution)/shard_map/ppermute | solution.py:120
  98.9 11.5 %collective-permute-start.15 = (f32[640,128]{1,0:T(8,128)S(1)}, f32[640,128]{1,0:T(8,128)S(1)}, u32[]{:S(2)}, u32[]{:S(2)}) collective-permute-start(f32[640,128]{1,0:T(8,128)S(1)} %maximum_select_fusion.1), channel_id=1, source_target_pairs={{0,1},{1,0},{2,3},{3,2},{4,5},{5,4},{6,7},{7,6},{8,9},{9,8},{10,11... | collective-permute-start | bytes 983048 | tf_op jit(solution)/shard_map/ppermute | solution.py:120
  99.2 11.2 %copy-start.3 = (f32[12]{0:T(128)S(1)}, f32[12]{0:T(128)}, u32[]{:S(2)}) copy-start(f32[12]{0:T(128)} %constant.89.clone) | copy-start | bytes 148

commit v2 on v1

v2 whole, which is shorter than its diff:
```python
import functools
import math

import jax
import jax.numpy as jnp
from jax import lax
from jax.experimental import pallas as pl
from jax.experimental.pallas import tpu as pltpu
from jax.sharding import PartitionSpec as P

BF = jnp.bfloat16
F32 = jnp.float32
TILE = 32
HBM = pl.BlockSpec(memory_space=pltpu.HBM)
VMEM = pl.BlockSpec(memory_space=pltpu.VMEM)
MIB = 1024 * 1024

GELU_A = math.sqrt(2.0 / math.pi)
GELU_B = 0.044715
STRETCH = math.sqrt(1.5 * GELU_B)
KAPPA = GELU_A * GELU_B / STRETCH**3
UNIT = 1.5 * KAPPA
OFFSET = 1.0 / (3.0 * KAPPA)


def level_starts(depth):
    rows = 1 << depth
    starts, at = [], 0
    for level in range(depth):
        starts.append(at)
        at += rows >> (level + 1)
    return starts


def forward_tree(leaf, put, low, depth, starts):
    half = 1 << (depth - 1)
    row = starts[depth - 1] + (low >> depth)
    if depth == 1:
        even, odd = leaf(low), leaf(low + 1)
        put(0, row, odd - even)
        return even.astype(F32) + odd.astype(F32)
    even = forward_tree(leaf, put, low, depth - 1, starts)
    odd = forward_tree(leaf, put, low + half, depth - 1, starts)
    put(depth - 1, row, (odd - even).astype(BF))
    return even + odd


def inverse_tree(take, leaf, low, depth, starts, value):
    if depth == 0:
        leaf(low, value)
        return
    half = 1 << (depth - 1)
    detail = take(starts[depth - 1] + (low >> depth))
    inverse_tree(take, leaf, low, depth - 1, starts, value - detail)
    inverse_tree(take, leaf, low + half, depth - 1, starts, value + detail)


def mix_details(coeffs_ref, weight_ref, mixed_ref, columns, depth, starts, back):
    tile, channels = mixed_ref.shape[1:]
    for level in range(depth):
        count = 1 << (depth - 1 - level)
        span = slice(starts[level], starts[level] + count)
        left = coeffs_ref[span, columns].reshape(count * tile, channels)
        dims = (((1,), (1 if back else 0,)), ((), ()))
        mixed = lax.dot_general(left, weight_ref[level], dims, preferred_element_type=F32)
        mixed_ref[span] = mixed.reshape(count, tile, channels)


def tile_span(index, tile, first=0):
    return pl.ds(pl.multiple_of(first + index * tile, tile), tile)


def kernel_sum(tile, fields_v, flags_ref, out_ref, flags_out):
    flags_out[...] = flags_ref[...]
    rows, columns = fields_v.shape[:2]

    def step(index, unused):
        here = tile_span(index, tile)
        total = fields_v[0, here].astype(F32)
        for row in range(1, rows):
            total = total + fields_v[row, here].astype(F32)
        out_ref[here] = total
        return 0

    lax.fori_loop(0, columns // tile, step, 0)


def kernel_a(depth, tile, first, stop, fields_v, weight_ref, token_ref, old_c, old_p, coeffs_v, partial_v, mixed_ref):
    starts = level_starts(depth)
    zero = jnp.zeros(mixed_ref.shape[1:], F32)

    def step(index, unused):
        here = tile_span(index, tile, first)

        def put(level, row, value):
            coeffs_v[row, here] = value

        forward_tree(lambda row: fields_v[row, here], put, 0, depth, starts)
        mix_details(coeffs_v, weight_ref, mixed_ref, here, depth, starts, False)

        def leaf(row, value):
            partial_v[row, here] = (value * STRETCH).astype(BF)

        inverse_tree(lambda row: mixed_ref[row], leaf, 0, depth, starts, zero)
        return 0

    lax.fori_loop(0, (stop - first) // tile, step, 0)


def kernel_b(depth, tile, partial_v, cot_v, base_ref, coeffs_v, upper_ref, back_v, coarse_ref, grads_ref):
    starts = level_starts(depth)
    columns, channels = base_ref.shape
    group = max(1, 256 // tile)

    grads_ref[...] = jnp.zeros_like(grads_ref)
    outer = functools.partial(
        lax.dot_general, dimension_numbers=(((0,), (0,)), ((), ())), preferred_element_type=F32
    )

    def step(index, unused):
        here = tile_span(index, tile)
        base = base_ref[here]
        waiting = [[] for _ in range(depth)]

        def leaf(row):
            y = partial_v[row, here].astype(F32) + base
            x = y * (y * y + 1.5)
            t = jnp.tanh(KAPPA * x)
            slope = (1.0 + t) * (OFFSET + (x - y) * (1.0 - t))
            return slope.astype(BF) * cot_v[row, here]

        def put(level, row, value):
            back_v[row, here] = value
            held = waiting[level]
            held.append(value)
            size = len(held)
            if size == group or row + 1 == starts[level] + (1 << (depth - 1 - level)):
                right = jnp.stack(held).reshape(size * tile, channels)
                left = coeffs_v[row + 1 - size : row + 1, here].reshape(size * tile, channels)
                grads_ref[level] += outer(left, right)
                held.clear()

        coarse_ref[here] = forward_tree(leaf, put, 0, depth, starts)
        return 0

    lax.fori_loop(0, columns // tile, step, 0)
    coarse = coarse_ref[...]
    high = coarse.astype(BF)
    low = (coarse - high.astype(F32)).astype(BF)
    for n in range(upper_ref.shape[0]):
        grads_ref[depth + n] = outer(upper_ref[n], high) + outer(upper_ref[n], low)


def kernel_c(depth, tile, first, stop, back_v, base_ref, weight_ref, token_ref, old_out, out_ref, done_ref,
             out_v, mixed_ref, sems):
    starts = level_starts(depth)
    count = (stop - first) // tile
    done_ref[...] = jnp.zeros_like(done_ref)

    def copy(index):
        here = tile_span(index, tile)
        return pltpu.make_async_copy(
            out_v.at[:, here], out_ref.at[:, tile_span(index, tile, first)], sems.at[index]
        )

    def step(index, unused):
        here = tile_span(index, tile)
        there = tile_span(index, tile, first)
        mix_details(back_v, weight_ref, mixed_ref, there, depth, starts, True)

        def leaf(row, value):
            out_v[row, here] = value.astype(BF)

        inverse_tree(lambda row: mixed_ref[row], leaf, 0, depth, starts, base_ref[there])
        copy(index).start()
        return 0

    lax.fori_loop(0, count, step, 0)
    for index in range(count):
        copy(index).wait()


def swap(block, stride):
    count = lax.axis_size("gx")
    return lax.ppermute(block, "gx", [(low, low ^ stride) for low in range(count)])


def is_upper(flags, degree):
    return flags[degree : degree + 1] > 0.5


def cross_coeffs(coarse, flags, depth):
    found, sent = [], []
    for degree in range(depth):
        sent.append(coarse)
        other = swap(coarse, 1 << degree)
        found.append(jnp.where(is_upper(flags, degree), coarse - other, other - coarse))
        coarse = coarse + other
    return found + [coarse], sent


def cross_mix(coeffs_b, weights, flags, back):
    spec = "yc,dc->yd" if back else "yc,cd->yd"
    total = jnp.einsum(spec, coeffs_b[-1], weights[-1], preferred_element_type=F32)
    for degree in reversed(range(len(coeffs_b) - 1)):
        part = jnp.einsum(spec, coeffs_b[degree], weights[degree], preferred_element_type=F32)
        total = total + jnp.where(is_upper(flags, degree), part, -part)
    return total


def sum_devices(block, flags, depth, beside):
    zero = 0
    for degree in range(depth):
        half = block.shape[0] // 2
        upper = is_upper(flags, degree)
        low, high = block[:half], block[half:]
        keep, send = jnp.where(upper, high, low), jnp.where(upper, low, high)
        if degree == depth - 1:
            zero = beside(0, send)
            keep = jnp.where(is_upper(flags + zero, degree), high, low)
        block = keep + swap(send, 1 << degree)
    for degree in reversed(range(depth)):
        other = swap(block, 1 << degree)
        zero = beside(depth - degree, block) if degree else 0
        upper = is_upper(flags + zero, degree)
        block = jnp.where(
            upper, jnp.concatenate([other, block]), jnp.concatenate([block, other])
        )
    return block


def pieces(columns, tile, count):
    tiles = columns // tile
    count = min(count, tiles)
    edges = [tiles * n // count * tile for n in range(count + 1)]
    return list(zip(edges[:-1], edges[1:]))


def shards(fields, cotangent, point_weight, mix_weight, bias_vec):
    rows, columns, channels = fields.shape
    depth = rows.bit_length() - 1
    device_count = lax.axis_size("gx")
    cross_depth = device_count.bit_length() - 1
    levels = depth + cross_depth
    bits = (lax.axis_index("gx") >> jnp.arange(cross_depth, dtype=jnp.int32)) & 1
    flags = jnp.broadcast_to(bits.astype(F32)[:, None], (cross_depth, channels))
    tile = min(TILE, columns)
    tiles = columns // tile

    def params(grant):
        return pltpu.CompilerParams(vmem_limit_bytes=grant * MIB)

    shape = (rows, columns, channels)
    kept = pltpu.VMEM(shape, BF)
    DMA = pltpu.SemaphoreType.DMA
    mixed_scratch = pltpu.VMEM((rows, tile, channels), F32)

    def cost(passes, width, products):
        return pl.CostEstimate(
            flops=2 * products * rows * width * channels * channels,
            bytes_accessed=passes * 2 * rows * width * channels,
            transcendentals=0,
        )

    powers = [2.0 ** -(level + 1) for level in range(levels)] + [2.0**-levels]
    scale = jnp.array(powers, F32)[:, None, None]
    joined_f = (mix_weight.astype(F32) + point_weight.astype(F32)) * scale
    joined = joined_f.astype(BF)
    joined_back = (joined_f * UNIT).astype(BF)

    coarse, flags = pl.pallas_call(
        functools.partial(kernel_sum, tile),
        in_specs=[VMEM, VMEM],
        out_specs=[VMEM] * 2,
        out_shape=[
            jax.ShapeDtypeStruct((columns, channels), F32),
            jax.ShapeDtypeStruct((cross_depth, channels), F32),
        ],
        compiler_params=params(12),
        cost_estimate=cost(1, columns, 0),
    )(fields, flags)
    coeffs_up, sent = cross_coeffs(coarse, flags, cross_depth)
    coeffs_up = [c.astype(BF) for c in coeffs_up]
    base = (cross_mix(coeffs_up, joined[depth:], flags, False) + bias_vec.astype(F32)) * STRETCH

    old = []
    ranges = pieces(columns, tile, max(1, cross_depth - 1))
    for (start, stop), token in zip(ranges, sent[-len(ranges) :]):
        kernel = functools.partial(kernel_a, depth, tile, start, stop)
        if not old:
            kernel = functools.partial(first_call, kernel, 3, 2)
        old = pl.pallas_call(
            kernel,
            in_specs=[VMEM, VMEM, HBM] + [VMEM] * len(old),
            out_specs=[VMEM] * 2,
            out_shape=[kept] * 2,
            input_output_aliases={3: 0, 4: 1} if old else {},
            scratch_shapes=[mixed_scratch],
            compiler_params=params(12),
            cost_estimate=cost(3, stop - start, 1),
        )(fields, joined[:depth], token, *old)
    coeffs, partial = old

    count_up = cross_depth - 1
    upper = jnp.stack([
        jnp.where(is_upper(flags, degree), coeffs_up[degree], -coeffs_up[degree])
        for degree in range(count_up)
    ])
    back, slope_coarse, grads = pl.pallas_call(
        functools.partial(kernel_b, depth, tile),
        in_specs=[VMEM] * 5,
        out_specs=[VMEM] * 3,
        out_shape=[
            kept,
            jax.ShapeDtypeStruct((columns, channels), F32),
            jax.ShapeDtypeStruct((depth + count_up, channels, channels), F32),
        ],
        compiler_params=params(12),
        cost_estimate=cost(4, columns, 1),
    )(partial, cotangent, base, coeffs, upper)

    slope_up, unused_sent = cross_coeffs(slope_coarse, flags, cross_depth)
    slope_up_b = [c.astype(BF) for c in slope_up]
    back_base = cross_mix(slope_up_b, joined_back[depth:], flags, True)

    ranges = pieces(columns, tile, cross_depth)
    results = []

    def beside(n, token):
        if n >= len(ranges):
            return 0
        start, stop = ranges[n]
        kernel = functools.partial(kernel_c, depth, tile, start, stop)
        if not results:
            kernel = functools.partial(first_call, kernel, 4, 1)
        grad_input, zero = pl.pallas_call(
            kernel,
            in_specs=[VMEM, VMEM, VMEM, HBM] + [HBM] * len(results),
            out_specs=[HBM, VMEM],
            out_shape=[jax.ShapeDtypeStruct(shape, BF), jax.ShapeDtypeStruct((1, channels), F32)],
            input_output_aliases={4: 0} if results else {},
            scratch_shapes=[
                pltpu.VMEM((rows, stop - start, channels), BF), mixed_scratch, DMA(((stop - start) // tile,))
            ],
            compiler_params=params(12),
            cost_estimate=cost(2, stop - start, 1),
        )(back, back_base, joined_back[:depth], token, *results)
        results[:] = [grad_input]
        return zero

    summed = sum_devices(grads.reshape(-1, channels), flags, cross_depth, beside)
    grad_input = results[0]
    summed = summed.reshape(-1, channels, channels)
    outer = functools.partial(jnp.einsum, "yc,yd->cd", preferred_element_type=F32)
    top = [outer(c, b) for c, b in zip(coeffs_up[-2:], slope_up_b[-2:])]
    raw = jnp.concatenate([summed, jnp.stack(top)]) * (scale * UNIT)

    global_rows = rows * device_count
    counts = [columns * global_rows / 2 ** (level + 1) for level in range(levels)] + [columns]
    factors = jnp.array([1.0 / math.sqrt(value) for value in counts], F32)
    scale_all = 1.0 / math.sqrt(global_rows * columns)
    grad_mix = (raw * factors[:, None, None]).astype(BF)
    grad_point = (jnp.sum(raw, axis=0) * scale_all).astype(BF)
    grad_bias = (jnp.sum(slope_up[-1], axis=0) * (UNIT * scale_all)).astype(BF)
    return (grad_input, grad_mix, grad_point, grad_bias)


def first_call(kernel, at, count, *refs):
    kernel(*refs[:at], *[None] * count, *refs[at:])


def solution(mesh):
    in_specs = (P("gx", "ga", None), P("gx", "ga", None), P(), P(), P())
    out_specs = (P("gx", "ga", None), P("ga", None, None), P("ga", None), P("ga"))
    return jax.shard_map(shards, mesh=mesh, in_specs=in_specs, out_specs=out_specs, check_vma=False)
```

time: 113 us -> 85.4 us (0.76)
  waiting for transfers between devices: 38.1 us -> 20.9 us
  Pallas kernels: 43.8 us -> 30.7 us
  local copies, waits for them, and re-layouts: 0.04 us -> 3.56 us
  starting transfers between devices: 18.7 us -> 22 us
  other arithmetic: 7.33 us -> 5.11 us
  matrix products: 3.08 us -> 1.91 us
    ppermute x16, waiting for transfers between devices: 38.1 us -> 20.9 us  [swap(): lax.ppermute(block, 'gx', [(low, low ^ stride) for low in range(count)])]
    pallas_call x3 -> x9, Pallas kernels: 43.8 us -> 30.7 us  [the longest x1 12.7 us: shards(): pl.pallas_call(functools.partial(kernel_b, depth, tile), in_specs=[VMEM]...]
    reduce_sum x2 -> x1, other arithmetic: 4.66 us -> 0.05 us  [shards(): grad_bias = (jnp.sum(slope_up[-1], axis=0) * (UNIT * scale_all)).astype(BF)]
    unnamed x10 -> x16, local copies, waits for them, and re-layouts: 0.03 us -> 3.42 us
    ppermute x16, starting transfers between devices: 18.7 us -> 22 us  [swap(): lax.ppermute(block, 'gx', [(low, low ^ stride) for low in range(count)])]
    convert_element_type x8 -> x5, other arithmetic: 0.8 us -> 2.79 us  [the longest x1 1.19 us: shards(): joined_back = (joined_f * UNIT).astype(BF)]
    dot_general x6 -> x0, matrix products: 1.19 us -> none  [shards(): part = outer(coeffs_up[degree], high) + outer(coeffs_up[degree], low)]
  transfers between devices with their start and end apart: 16 -> 16, of which waited for: 13 -> 12; matrix products, arithmetic and copies ran while one was open for 2% -> 6% of each run, Pallas kernels for 21% -> 19%
where the time goes in v2:
time: 85.4 us; the launch traced here: 85.2 us
  Pallas kernels  30.7 us (36%)
  starting transfers between devices  22 us (26%)
  waiting for transfers between devices  20.9 us (24%)
  other arithmetic  5.11 us (6%)
  local copies, waits for them, and re-layouts  3.56 us (4%)
  matrix products  1.91 us (2%)
  between operations  1.12 us (1%)
    ppermute x16, starting transfers between devices, swap(): lax.ppermute(block, 'gx', [(low, low ^ stride) for low in range(count)])  22 us
    ppermute x16, waiting for transfers between devices, swap(): lax.ppermute(block, 'gx', [(low, low ^ stride) for low in range(count)])  20.9 us
    pallas_call x1, Pallas kernels, shards(): pl.pallas_call(functools.partial(kernel_b, depth, tile), in_specs=[VMEM]...  12.7 us
    pallas_call x4, Pallas kernels, beside(): pl.pallas_call(kernel, in_specs=[VMEM, VMEM, VMEM, HBM] + [HBM] * len(res...  9.56 us
    pallas_call x3, Pallas kernels, shards(): pl.pallas_call(kernel, in_specs=[VMEM, VMEM, HBM] + [VMEM] * len(old), ou...  6.86 us
    unnamed x16, local copies, waits for them, and re-layouts  3.42 us
  transfers between devices with their start and end apart: 16, of which 12 were waited for; matrix products, arithmetic and copies ran while one was open for 6% of the time, Pallas kernels for 19%

profile of v2, /device:TPU:0, one launch (start us, length us, event | category | flops | bytes accessed | tf_op | source)
XLA Modules:
  0.0 85.2 jit_solution(18436652846991995622)
XLA Ops:
  0.7 3.4 %copy-done = bf16[128,256,128]{2,1,0:T(8,128)(2,1)S(1)} copy-done((bf16[128,256,128]{2,1,0:T(8,128)(2,1)S(1)}, bf16[128,256,128]{2,1,0:T(8,128)(2,1)}, u32[]{:S(2)}) %copy-start) | copy-done | bytes 8388632
  4.1 1.6 %shard_map.102 = (f32[256,128]{1,0:T(8,128)S(1)}, f32[4,128]{1,0:T(4,128)S(1)}) custom-call(bf16[128,256,128]{2,1,0:T(8,128)(2,1)S(1)} %copy-done, f32[4,128]{1,0:T(4,128)S(1)} %broadcast_in_dim.166.flags_ref), custom_call_target="tpu_custom_call" | custom-call | bytes 8388608 | tf_op jit(solution)/shard_map/pallas_call | solution.py:271
  8.6 3.0 %collective-permute-start.1 = (f32[256,128]{1,0:T(8,128)S(1)}, f32[256,128]{1,0:T(8,128)S(1)}, u32[]{:S(2)}, u32[]{:S(2)}) collective-permute-start(f32[256,128]{1,0:T(8,128)S(1)} %add.118.refs_2_), channel_id=1, source_target_pairs={{0,2},{1,3},{2,0},{3,1},{4,6},{5,7},{6,4},{7,5},{8,10},{9,11},{10,... | collective-permute-start | bytes 393224 | tf_op jit(solution)/shard_map/ppermute | solution.py:185
  11.6 1.7 %shard_map.103 = (bf16[128,256,128]{2,1,0:T(8,128)(2,1)S(1)}, bf16[128,256,128]{2,1,0:T(8,128)(2,1)S(1)}) custom-call(bf16[128,256,128]{2,1,0:T(8,128)(2,1)S(1)} %copy-done.1, bf16[7,128,128]{2,1,0:T(8,128)(2,1)S(1)} %slice.157.refs_1_.weight_ref, f32[256,128]{1,0:T(8,128)S(1)} %add.118.refs_2_), custom_call_target="tpu_custom_call" | custom-call | flops 268435456 | bytes 6291456 | tf_op jit(solution)/shard_map/pallas_call | solution.py:292
  13.5 1.6 %collective-permute-done.1 = f32[256,128]{1,0:T(8,128)S(1)} collective-permute-done((f32[256,128]{1,0:T(8,128)S(1)}, f32[256,128]{1,0:T(8,128)S(1)}, u32[]{:S(2)}, u32[]{:S(2)}) %collective-permute-start.1) | collective-permute-done | bytes 131104 | tf_op jit(solution)/shard_map/ppermute | solution.py:185
  15.1 1.9 %collective-permute-start.2 = (f32[256,128]{1,0:T(8,128)S(1)}, f32[256,128]{1,0:T(8,128)S(1)}, u32[]{:S(2)}, u32[]{:S(2)}) collective-permute-start(f32[256,128]{1,0:T(8,128)S(1)} %add.119.token_ref), channel_id=1, source_target_pairs={{0,4},{1,5},{2,6},{3,7},{4,0},{5,1},{6,2},{7,3},{8,12},{9,13},{10,... | collective-permute-start | bytes 393224 | tf_op jit(solution)/shard_map/ppermute | solution.py:185
  17.2 2.6 %shard_map.104 = (bf16[128,256,128]{2,1,0:T(8,128)(2,1)S(1)}, bf16[128,256,128]{2,1,0:T(8,128)(2,1)S(1)}) custom-call(bf16[128,256,128]{2,1,0:T(8,128)(2,1)S(1)} %copy-done.1, bf16[7,128,128]{2,1,0:T(8,128)(2,1)S(1)} %slice.157.refs_1_.weight_ref, f32[256,128]{1,0:T(8,128)S(1)} %add.119.token_ref, ...), custom_call_target="tpu_custom_call", output_to_operand_aliasing={{0}: (3, {}), {1}: (4, {})} | custom-call | flops 402653184 | bytes 9437184 | tf_op jit(solution)/shard_map/pallas_call | solution.py:292
  20.2 2.9 %collective-permute-start.3 = (f32[256,128]{1,0:T(8,128)S(1)}, f32[256,128]{1,0:T(8,128)S(1)}, u32[]{:S(2)}, u32[]{:S(2)}) collective-permute-start(f32[256,128]{1,0:T(8,128)S(1)} %add.120.token_ref), channel_id=1, source_target_pairs={{0,8},{1,9},{2,10},{3,11},{4,12},{5,13},{6,14},{7,15},{8,0},{9,1},... | collective-permute-start | bytes 393224 | tf_op jit(solution)/shard_map/ppermute | solution.py:185
  23.3 2.6 %shard_map.105 = (bf16[128,256,128]{2,1,0:T(8,128)(2,1)S(1)}, bf16[128,256,128]{2,1,0:T(8,128)(2,1)S(1)}) custom-call(bf16[128,256,128]{2,1,0:T(8,128)(2,1)S(1)} %copy-done.1, bf16[7,128,128]{2,1,0:T(8,128)(2,1)S(1)} %slice.157.refs_1_.weight_ref, f32[256,128]{1,0:T(8,128)S(1)} %add.120.token_ref, ...), custom_call_target="tpu_custom_call", output_to_operand_aliasing={{0}: (3, {}), {1}: (4, {})} | custom-call | flops 402653184 | bytes 9437184 | tf_op jit(solution)/shard_map/pallas_call | solution.py:292
  25.9 1.8 %collective-permute-done.3 = f32[256,128]{1,0:T(8,128)S(1)} collective-permute-done((f32[256,128]{1,0:T(8,128)S(1)}, f32[256,128]{1,0:T(8,128)S(1)}, u32[]{:S(2)}, u32[]{:S(2)}) %collective-permute-start.3) | collective-permute-done | bytes 131104 | tf_op jit(solution)/shard_map/ppermute | solution.py:185
  28.0 12.7 %shard_map.106 = (bf16[128,256,128]{2,1,0:T(8,128)(2,1)S(1)}, f32[256,128]{1,0:T(8,128)S(1)}, f32[10,128,128]{2,1,0:T(8,128)S(1)}) custom-call(bf16[128,256,128]{2,1,0:T(8,128)(2,1)S(1)} %get-tuple-element.28.partial_v, bf16[128,256,128]{2,1,0:T(8,128)(2,1)S(1)} %bitcast.82, f32[256,128]{1,0:T(8,128)S(1)} %fusion.7.base_ref, ...), custom_call_target="tpu_custom_call" | custom-call | flops 1073741824 | bytes 33554432 | tf_op jit(solution)/shard_map/pallas_call | solution.py:309
  42.2 1.6 %collective-permute-start.5 = (f32[256,128]{1,0:T(8,128)S(1)}, f32[256,128]{1,0:T(8,128)S(1)}, u32[]{:S(2)}, u32[]{:S(2)}) collective-permute-start(f32[256,128]{1,0:T(8,128)S(1)} %add.128), channel_id=1, source_target_pairs={{0,2},{1,3},{2,0},{3,1},{4,6},{5,7},{6,4},{7,5},{8,10},{9,11},{10,... | collective-permute-start | bytes 393224 | tf_op jit(solution)/shard_map/ppermute | solution.py:185
  44.0 3.8 %collective-permute-done.5 = f32[256,128]{1,0:T(8,128)S(1)} collective-permute-done((f32[256,128]{1,0:T(8,128)S(1)}, f32[256,128]{1,0:T(8,128)S(1)}, u32[]{:S(2)}, u32[]{:S(2)}) %collective-permute-start.5) | collective-permute-done | bytes 131104 | tf_op jit(solution)/shard_map/ppermute | solution.py:185
  50.5 2.4 %collective-permute-done.6 = f32[256,128]{1,0:T(8,128)S(1)} collective-permute-done((f32[256,128]{1,0:T(8,128)S(1)}, f32[256,128]{1,0:T(8,128)S(1)}, u32[]{:S(2)}, u32[]{:S(2)}) %collective-permute-start.6) | collective-permute-done | bytes 131104 | tf_op jit(solution)/shard_map/ppermute | solution.py:185
  52.9 2.2 %collective-permute-start.7 = (f32[256,128]{1,0:T(8,128)S(1)}, f32[256,128]{1,0:T(8,128)S(1)}, u32[]{:S(2)}, u32[]{:S(2)}) collective-permute-start(f32[256,128]{1,0:T(8,128)S(1)} %add.130), channel_id=1, source_target_pairs={{0,8},{1,9},{2,10},{3,11},{4,12},{5,13},{6,14},{7,15},{8,0},{9,1},... | collective-permute-start | bytes 393224 | tf_op jit(solution)/shard_map/ppermute | solution.py:185
  55.3 2.1 %collective-permute-start.10 = (f32[160,128]{1,0:T(8,128)S(1)}, f32[160,128]{1,0:T(8,128)S(1)}, u32[]{:S(2)}, u32[]{:S(2)}) collective-permute-start(f32[160,128]{1,0:T(8,128)S(1)} %slice_select_fusion.1), channel_id=1, source_target_pairs={{0,4},{1,5},{2,6},{3,7},{4,0},{5,1},{6,2},{7,3},{8,12},{9,13},{10,... | collective-permute-start | bytes 245768 | tf_op jit(solution)/shard_map/ppermute | solution.py:185
  57.4 2.8 %collective-permute-done.7 = f32[256,128]{1,0:T(8,128)S(1)} collective-permute-done((f32[256,128]{1,0:T(8,128)S(1)}, f32[256,128]{1,0:T(8,128)S(1)}, u32[]{:S(2)}, u32[]{:S(2)}) %collective-permute-start.7) | collective-permute-done | bytes 131104 | tf_op jit(solution)/shard_map/ppermute | solution.py:185
  62.3 2.4 %shard_map.107 = (bf16[128,256,128]{2,1,0:T(8,128)(2,1)}, f32[1,128]{1,0:T(1,128)S(1)}) custom-call(bf16[128,256,128]{2,1,0:T(8,128)(2,1)S(1)} %get-tuple-element.31.refs_0_.back_v, f32[256,128]{1,0:T(8,128)S(1)} %fusion.2.refs_1_.base_ref, bf16[7,128,128]{2,1,0:T(8,128)(2,1)S(1)} %slice.168.refs_2_.weight_ref, f32[80,128]{1,0:T(8,128)S(1)} %slice_select_fusion.2.refs_3_), custom_call_target="tpu_custom_call" | custom-call | flops 268435456 | bytes 4194304 | tf_op jit(solution)/shard_map/pallas_call | solution.py:336
  64.8 1.7 %collective-permute-done.11 = f32[80,128]{1,0:T(8,128)S(1)} collective-permute-done((f32[80,128]{1,0:T(8,128)S(1)}, f32[80,128]{1,0:T(8,128)S(1)}, u32[]{:S(2)}, u32[]{:S(2)}) %collective-permute-start.11) | collective-permute-done | bytes 40992 | tf_op jit(solution)/shard_map/ppermute | solution.py:185
  67.3 2.4 %shard_map.108 = (bf16[128,256,128]{2,1,0:T(8,128)(2,1)}, f32[1,128]{1,0:T(1,128)S(1)}) custom-call(bf16[128,256,128]{2,1,0:T(8,128)(2,1)S(1)} %get-tuple-element.31.refs_0_.back_v, f32[256,128]{1,0:T(8,128)S(1)} %fusion.2.refs_1_.base_ref, bf16[7,128,128]{2,1,0:T(8,128)(2,1)S(1)} %slice.168.refs_2_.weight_ref, ...), custom_call_target="tpu_custom_call", output_to_operand_aliasing={{0}: (4, {})} | custom-call | flops 268435456 | bytes 4194304 | tf_op jit(solution)/shard_map/pallas_call | solution.py:336
  69.7 2.1 %collective-permute-done.12 = f32[80,128]{1,0:T(8,128)S(1)} collective-permute-done((f32[80,128]{1,0:T(8,128)S(1)}, f32[80,128]{1,0:T(8,128)S(1)}, u32[]{:S(2)}, u32[]{:S(2)}) %collective-permute-start.12) | collective-permute-done | bytes 40992 | tf_op jit(solution)/shard_map/ppermute | solution.py:185
  72.4 2.4 %shard_map.109 = (bf16[128,256,128]{2,1,0:T(8,128)(2,1)}, f32[1,128]{1,0:T(1,128)S(1)}) custom-call(bf16[128,256,128]{2,1,0:T(8,128)(2,1)S(1)} %get-tuple-element.31.refs_0_.back_v, f32[256,128]{1,0:T(8,128)S(1)} %fusion.2.refs_1_.base_ref, bf16[7,128,128]{2,1,0:T(8,128)(2,1)S(1)} %slice.168.refs_2_.weight_ref, ...), custom_call_target="tpu_custom_call", output_to_operand_aliasing={{0}: (4, {})} | custom-call | flops 268435456 | bytes 4194304 | tf_op jit(solution)/shard_map/pallas_call | solution.py:336
  76.4 1.7 %collective-permute-start.14 = (f32[320,128]{1,0:T(8,128)S(1)}, f32[320,128]{1,0:T(8,128)S(1)}, u32[]{:S(2)}, u32[]{:S(2)}) collective-permute-start(f32[320,128]{1,0:T(8,128)S(1)} %maximum_select_fusion.1.token_ref), channel_id=1, source_target_pairs={{0,2},{1,3},{2,0},{3,1},{4,6},{5,7},{6,4},{7,5},{8,10},{9,11},{10,... | collective-permute-start | bytes 491528 | tf_op jit(solution)/shard_map/ppermute | solution.py:185
  78.1 2.4 %shard_map.110 = (bf16[128,256,128]{2,1,0:T(8,128)(2,1)}, f32[1,128]{1,0:T(1,128)S(1)}) custom-call(bf16[128,256,128]{2,1,0:T(8,128)(2,1)S(1)} %get-tuple-element.31.refs_0_.back_v, f32[256,128]{1,0:T(8,128)S(1)} %fusion.2.refs_1_.base_ref, bf16[7,128,128]{2,1,0:T(8,128)(2,1)S(1)} %slice.168.refs_2_.weight_ref, ...), custom_call_target="tpu_custom_call", output_to_operand_aliasing={{0}: (4, {})} | custom-call | flops 268435456 | bytes 4194304 | tf_op jit(solution)/shard_map/pallas_call | solution.py:336
  (91 shorter events, 18.5 us)
Async XLA Ops:
  0.6 6.6 %copy-start.4 = (f32[12]{0:T(128)S(1)}, f32[12]{0:T(128)}, u32[]{:S(2)}) copy-start(f32[12]{0:T(128)} %constant.9.clone) | copy-start | bytes 148
  0.6 5.6 %copy-start.5 = (bf16[128]{0:T(256)(128)(2,1)S(1)}, bf16[128]{0:T(256)(128)(2,1)}, u32[]{:S(2)}) copy-start(bf16[128]{0:T(256)(128)(2,1)} %param.11) | copy-start | bytes 772
  0.7 3.4 %copy-start = (bf16[128,256,128]{2,1,0:T(8,128)(2,1)S(1)}, bf16[128,256,128]{2,1,0:T(8,128)(2,1)}, u32[]{:S(2)}) copy-start(bf16[128,256,128]{2,1,0:T(8,128)(2,1)} %fields_v.5) | copy-start | bytes 25165828
  4.1 7.5 %copy-start.1 = (bf16[128,256,128]{2,1,0:T(8,128)(2,1)S(1)}, bf16[128,256,128]{2,1,0:T(8,128)(2,1)}, u32[]{:S(2)}) copy-start(bf16[128,256,128]{2,1,0:T(8,128)(2,1)} %fields_v.5) | copy-start | bytes 25165828
  5.7 2.8 %collective-permute-start = (f32[256,128]{1,0:T(8,128)S(1)}, f32[256,128]{1,0:T(8,128)S(1)}, u32[]{:S(2)}, u32[]{:S(2)}) collective-permute-start(f32[256,128]{1,0:T(8,128)S(1)} %get-tuple-element.23), channel_id=1, source_target_pairs={{0,1},{1,0},{2,3},{3,2},{4,5},{5,4},{6,7},{7,6},{8,9},{9,8},{10,11... | collective-permute-start | bytes 393224 | tf_op jit(solution)/shard_map/ppermute | solution.py:185
  8.6 6.5 %collective-permute-start.1 = (f32[256,128]{1,0:T(8,128)S(1)}, f32[256,128]{1,0:T(8,128)S(1)}, u32[]{:S(2)}, u32[]{:S(2)}) collective-permute-start(f32[256,128]{1,0:T(8,128)S(1)} %add.118.refs_2_), channel_id=1, source_target_pairs={{0,2},{1,3},{2,0},{3,1},{4,6},{5,7},{6,4},{7,5},{8,10},{9,11},{10,... | collective-permute-start | bytes 393224 | tf_op jit(solution)/shard_map/ppermute | solution.py:185
  15.1 5.0 %collective-permute-start.2 = (f32[256,128]{1,0:T(8,128)S(1)}, f32[256,128]{1,0:T(8,128)S(1)}, u32[]{:S(2)}, u32[]{:S(2)}) collective-permute-start(f32[256,128]{1,0:T(8,128)S(1)} %add.119.token_ref), channel_id=1, source_target_pairs={{0,4},{1,5},{2,6},{3,7},{4,0},{5,1},{6,2},{7,3},{8,12},{9,13},{10,... | collective-permute-start | bytes 393224 | tf_op jit(solution)/shard_map/ppermute | solution.py:185
  20.1 7.9 %slice-start = ((s8[8388608]{0:T(1024)(128)(4,1)}), s8[4194304]{0:T(1024)(128)(4,1)S(1)}, s32[]{:S(2)}) async-start(s8[8388608]{0:T(1024)(128)(4,1)} %bitcast.81), calls=%async_computation | async-start | bytes 8388608
  20.2 7.5 %collective-permute-start.3 = (f32[256,128]{1,0:T(8,128)S(1)}, f32[256,128]{1,0:T(8,128)S(1)}, u32[]{:S(2)}, u32[]{:S(2)}) collective-permute-start(f32[256,128]{1,0:T(8,128)S(1)} %add.120.token_ref), channel_id=1, source_target_pairs={{0,8},{1,9},{2,10},{3,11},{4,12},{5,13},{6,14},{7,15},{8,0},{9,1},... | collective-permute-start | bytes 393224 | tf_op jit(solution)/shard_map/ppermute | solution.py:185
  23.2 4.8 %slice-start.1 = ((s8[8388608]{0:T(1024)(128)(4,1)}), s8[4194304]{0:T(1024)(128)(4,1)S(1)}, s32[]{:S(2)}) async-start(s8[8388608]{0:T(1024)(128)(4,1)} %bitcast.81), calls=%async_computation.1 | async-start | bytes 8388608
  40.8 1.4 %collective-permute-start.4 = (f32[256,128]{1,0:T(8,128)S(1)}, f32[256,128]{1,0:T(8,128)S(1)}, u32[]{:S(2)}, u32[]{:S(2)}) collective-permute-start(f32[256,128]{1,0:T(8,128)S(1)} %get-tuple-element.32), channel_id=1, source_target_pairs={{0,1},{1,0},{2,3},{3,2},{4,5},{5,4},{6,7},{7,6},{8,9},{9,8},{10,11... | collective-permute-start | bytes 393224 | tf_op jit(solution)/shard_map/ppermute | solution.py:185
  40.9 7.9 %collective-permute-start.8 = (f32[640,128]{1,0:T(8,128)S(1)}, f32[640,128]{1,0:T(8,128)S(1)}, u32[]{:S(2)}, u32[]{:S(2)}) collective-permute-start(f32[640,128]{1,0:T(8,128)S(1)} %bitcast_select_fusion), channel_id=1, source_target_pairs={{0,1},{1,0},{2,3},{3,2},{4,5},{5,4},{6,7},{7,6},{8,9},{9,8},{10,11... | collective-permute-start | bytes 983048 | tf_op jit(solution)/shard_map/ppermute | solution.py:185
  42.2 5.6 %collective-permute-start.5 = (f32[256,128]{1,0:T(8,128)S(1)}, f32[256,128]{1,0:T(8,128)S(1)}, u32[]{:S(2)}, u32[]{:S(2)}) collective-permute-start(f32[256,128]{1,0:T(8,128)S(1)} %add.128), channel_id=1, source_target_pairs={{0,2},{1,3},{2,0},{3,1},{4,6},{5,7},{6,4},{7,5},{8,10},{9,11},{10,... | collective-permute-start | bytes 393224 | tf_op jit(solution)/shard_map/ppermute | solution.py:185
  47.8 5.0 %collective-permute-start.6 = (f32[256,128]{1,0:T(8,128)S(1)}, f32[256,128]{1,0:T(8,128)S(1)}, u32[]{:S(2)}, u32[]{:S(2)}) collective-permute-start(f32[256,128]{1,0:T(8,128)S(1)} %add.129), channel_id=1, source_target_pairs={{0,4},{1,5},{2,6},{3,7},{4,0},{5,1},{6,2},{7,3},{8,12},{9,13},{10,... | collective-permute-start | bytes 393224 | tf_op jit(solution)/shard_map/ppermute | solution.py:185
  48.9 6.4 %collective-permute-start.9 = (f32[320,128]{1,0:T(8,128)S(1)}, f32[320,128]{1,0:T(8,128)S(1)}, u32[]{:S(2)}, u32[]{:S(2)}) collective-permute-start(f32[320,128]{1,0:T(8,128)S(1)} %slice_select_fusion), channel_id=1, source_target_pairs={{0,2},{1,3},{2,0},{3,1},{4,6},{5,7},{6,4},{7,5},{8,10},{9,11},{10,... | collective-permute-start | bytes 491528 | tf_op jit(solution)/shard_map/ppermute | solution.py:185
  52.9 7.3 %collective-permute-start.7 = (f32[256,128]{1,0:T(8,128)S(1)}, f32[256,128]{1,0:T(8,128)S(1)}, u32[]{:S(2)}, u32[]{:S(2)}) collective-permute-start(f32[256,128]{1,0:T(8,128)S(1)} %add.130), channel_id=1, source_target_pairs={{0,8},{1,9},{2,10},{3,11},{4,12},{5,13},{6,14},{7,15},{8,0},{9,1},... | collective-permute-start | bytes 393224 | tf_op jit(solution)/shard_map/ppermute | solution.py:185
  55.3 5.5 %collective-permute-start.10 = (f32[160,128]{1,0:T(8,128)S(1)}, f32[160,128]{1,0:T(8,128)S(1)}, u32[]{:S(2)}, u32[]{:S(2)}) collective-permute-start(f32[160,128]{1,0:T(8,128)S(1)} %slice_select_fusion.1), channel_id=1, source_target_pairs={{0,4},{1,5},{2,6},{3,7},{4,0},{5,1},{6,2},{7,3},{8,12},{9,13},{10,... | collective-permute-start | bytes 245768 | tf_op jit(solution)/shard_map/ppermute | solution.py:185
  60.9 5.5 %collective-permute-start.11 = (f32[80,128]{1,0:T(8,128)S(1)}, f32[80,128]{1,0:T(8,128)S(1)}, u32[]{:S(2)}, u32[]{:S(2)}) collective-permute-start(f32[80,128]{1,0:T(8,128)S(1)} %slice_select_fusion.2.refs_3_), channel_id=1, source_target_pairs={{0,8},{1,9},{2,10},{3,11},{4,12},{5,13},{6,14},{7,15},{8,0},{9,1},... | collective-permute-start | bytes 122888 | tf_op jit(solution)/shard_map/ppermute | solution.py:185
  66.4 5.4 %collective-permute-start.12 = (f32[80,128]{1,0:T(8,128)S(1)}, f32[80,128]{1,0:T(8,128)S(1)}, u32[]{:S(2)}, u32[]{:S(2)}) collective-permute-start(f32[80,128]{1,0:T(8,128)S(1)} %select_add_fusion.2.token_ref), channel_id=1, source_target_pairs={{0,8},{1,9},{2,10},{3,11},{4,12},{5,13},{6,14},{7,15},{8,0},{9,1},... | collective-permute-start | bytes 122888 | tf_op jit(solution)/shard_map/ppermute | solution.py:185
  71.8 4.5 %collective-permute-start.13 = (f32[160,128]{1,0:T(8,128)S(1)}, f32[160,128]{1,0:T(8,128)S(1)}, u32[]{:S(2)}, u32[]{:S(2)}) collective-permute-start(f32[160,128]{1,0:T(8,128)S(1)} %maximum_select_fusion.2.token_ref), channel_id=1, source_target_pairs={{0,4},{1,5},{2,6},{3,7},{4,0},{5,1},{6,2},{7,3},{8,12},{9,13},{10,... | collective-permute-start | bytes 245768 | tf_op jit(solution)/shard_map/ppermute | solution.py:185
  76.4 5.4 %collective-permute-start.14 = (f32[320,128]{1,0:T(8,128)S(1)}, f32[320,128]{1,0:T(8,128)S(1)}, u32[]{:S(2)}, u32[]{:S(2)}) collective-permute-start(f32[320,128]{1,0:T(8,128)S(1)} %maximum_select_fusion.1.token_ref), channel_id=1, source_target_pairs={{0,2},{1,3},{2,0},{3,1},{4,6},{5,7},{6,4},{7,5},{8,10},{9,11},{10,... | collective-permute-start | bytes 491528 | tf_op jit(solution)/shard_map/ppermute | solution.py:185
  78.1 5.5 %copy-start.2 = (f32[12]{0:T(128)S(1)}, f32[12]{0:T(128)}, u32[]{:S(2)}) copy-start(f32[12]{0:T(128)} %constant.25) | copy-start | bytes 148
  78.1 5.5 %copy-start.3 = (f32[12]{0:T(128)S(1)}, f32[12]{0:T(128)}, u32[]{:S(2)}) copy-start(f32[12]{0:T(128)} %constant.24.clone) | copy-start | bytes 148
  81.8 1.7 %collective-permute-start.15 = (f32[640,128]{1,0:T(8,128)S(1)}, f32[640,128]{1,0:T(8,128)S(1)}, u32[]{:S(2)}, u32[]{:S(2)}) collective-permute-start(f32[640,128]{1,0:T(8,128)S(1)} %maximum_select_fusion), channel_id=1, source_target_pairs={{0,1},{1,0},{2,3},{3,2},{4,5},{5,4},{6,7},{7,6},{8,9},{9,8},{10,11... | collective-permute-start | bytes 983048 | tf_op jit(solution)/shard_map/ppermute | solution.py:185

commit v3 on v2

--- a/solution.py
+++ b/solution.py
@@ -55,6 +55,12 @@
     inverse_tree(take, leaf, low + half, depth - 1, starts, value + detail)
 
 
+def join_weights(mix_ref, point_ref, joined_ref, unit):
+    point = point_ref[...].astype(F32)
+    for level in range(joined_ref.shape[0]):
+        joined_ref[level] = ((mix_ref[level].astype(F32) + point) * (unit * 2.0 ** -(level + 1))).astype(BF)
+
+
 def mix_details(coeffs_ref, weight_ref, mixed_ref, columns, depth, starts, back):
     tile, channels = mixed_ref.shape[1:]
     for level in range(depth):
@@ -85,9 +91,11 @@
     lax.fori_loop(0, columns // tile, step, 0)
 
 
-def kernel_a(depth, tile, first, stop, fields_v, weight_ref, token_ref, old_c, old_p, coeffs_v, partial_v, mixed_ref):
+def kernel_a(depth, tile, first, stop, fields_v, mix_ref, point_ref, token_ref, old_c, old_p,
+             coeffs_v, partial_v, weight_ref, mixed_ref):
     starts = level_starts(depth)
     zero = jnp.zeros(mixed_ref.shape[1:], F32)
+    join_weights(mix_ref, point_ref, weight_ref, 1.0)
 
     def step(index, unused):
         here = tile_span(index, tile, first)
@@ -151,11 +159,12 @@
         grads_ref[depth + n] = outer(upper_ref[n], high) + outer(upper_ref[n], low)
 
 
-def kernel_c(depth, tile, first, stop, back_v, base_ref, weight_ref, token_ref, old_out, out_ref, done_ref,
-             out_v, mixed_ref, sems):
+def kernel_c(depth, tile, first, stop, back_v, base_ref, mix_ref, point_ref, token_ref, old_out, out_ref, done_ref,
+             out_v, weight_ref, mixed_ref, sems):
     starts = level_starts(depth)
     count = (stop - first) // tile
     done_ref[...] = jnp.zeros_like(done_ref)
+    join_weights(mix_ref, point_ref, weight_ref, UNIT)
 
     def copy(index):
         here = tile_span(index, tile)
@@ -199,41 +208,68 @@
     return found + [coarse], sent
 
 
-def cross_mix(coeffs_b, weights, flags, back):
+def mix_row(coeffs_b, weight, back):
     spec = "yc,dc->yd" if back else "yc,cd->yd"
-    total = jnp.einsum(spec, coeffs_b[-1], weights[-1], preferred_element_type=F32)
-    for degree in reversed(range(len(coeffs_b) - 1)):
-        part = jnp.einsum(spec, coeffs_b[degree], weights[degree], preferred_element_type=F32)
+    return jnp.einsum(spec, coeffs_b, weight, preferred_element_type=F32)
+
+
+def cross_mix(coeffs_b, weights, flags, back, lowest=0):
+    total = mix_row(coeffs_b[-1], weights[-1], back)
+    for degree in reversed(range(lowest, len(coeffs_b) - 1)):
+        part = mix_row(coeffs_b[degree], weights[degree], back)
         total = total + jnp.where(is_upper(flags, degree), part, -part)
     return total
 
 
-def sum_devices(block, flags, depth, beside):
-    zero = 0
+def pick(upper, low, high):
+    return jnp.where(upper, high, low), jnp.where(upper, low, high)
+
+
+def join(upper, mine, other):
+    return jnp.where(upper, jnp.concatenate([other, mine]), jnp.concatenate([mine, other]))
+
+
+def reduce_down(block, coarse, flags, depth):
+    found = []
+    columns = coarse.shape[0] // 2
     for degree in range(depth):
+        upper = is_upper(flags, degree)
         half = block.shape[0] // 2
-        upper = is_upper(flags, degree)
-        low, high = block[:half], block[half:]
-        keep, send = jnp.where(upper, high, low), jnp.where(upper, low, high)
-        if degree == depth - 1:
-            zero = beside(0, send)
-            keep = jnp.where(is_upper(flags + zero, degree), high, low)
-        block = keep + swap(send, 1 << degree)
-    for degree in reversed(range(depth)):
-        other = swap(block, 1 << degree)
-        zero = beside(depth - degree, block) if degree else 0
-        upper = is_upper(flags + zero, degree)
-        block = jnp.where(
-            upper, jnp.concatenate([other, block]), jnp.concatenate([block, other])
-        )
-    return block
-
-
-def pieces(columns, tile, count):
+        keep, send = pick(upper, block[:half], block[half:])
+        row_send = coarse
+        if degree == 0:
+            coarse, row_send = pick(upper, coarse[:columns], coarse[columns:])
+        got = swap(jnp.concatenate([send, row_send]), 1 << degree)
+        block, other = keep + got[:half], got[half:]
+        found.append(jnp.where(upper, coarse - other, other - coarse))
+        coarse = coarse + other
+    return block, found + [coarse]
+
+
+def pieces(columns, tile, shares):
     tiles = columns // tile
-    count = min(count, tiles)
-    edges = [tiles * n // count * tile for n in range(count + 1)]
-    return list(zip(edges[:-1], edges[1:]))
+    total = sum(shares)
+    edges = [tiles * sum(shares[:n]) // total * tile for n in range(len(shares) + 1)]
+    return [(start, stop) for start, stop in zip(edges[:-1], edges[1:]) if stop > start]
+
+
+def kernel_last(scales, point_scale, bias_scale, low_ref, high_ref, top_ref, bias_ref, mix_ref, point_ref, out_ref):
+    channels = mix_ref.shape[2]
+    half = low_ref.shape[0]
+    total = jnp.zeros(point_ref.shape, F32)
+    for level, (power, factor) in enumerate(scales):
+        at = level * channels
+        if at + channels <= half:
+            raw = low_ref[at : at + channels]
+        elif half <= at < 2 * half:
+            raw = high_ref[at - half : at - half + channels]
+        else:
+            raw = top_ref[at - 2 * half : at - 2 * half + channels]
+        raw = raw * power
+        total = total + raw
+        mix_ref[level] = (raw * factor).astype(BF)
+    point_ref[...] = (total * point_scale).astype(BF)
+    out_ref[...] = (bias_ref[...] * bias_scale).astype(BF)
 
 
 def shards(fields, cotangent, point_weight, mix_weight, bias_vec):
@@ -253,6 +289,7 @@
     shape = (rows, columns, channels)
     kept = pltpu.VMEM(shape, BF)
     DMA = pltpu.SemaphoreType.DMA
+    weight_scratch = pltpu.VMEM((depth, channels, channels), BF)
     mixed_scratch = pltpu.VMEM((rows, tile, channels), F32)
 
     def cost(passes, width, products):
@@ -263,8 +300,8 @@
         )
 
     powers = [2.0 ** -(level + 1) for level in range(levels)] + [2.0**-levels]
-    scale = jnp.array(powers, F32)[:, None, None]
-    joined_f = (mix_weight.astype(F32) + point_weight.astype(F32)) * scale
+    scale = jnp.array(powers[depth:], F32)[:, None, None]
+    joined_f = (mix_weight[depth:].astype(F32) + point_weight.astype(F32)) * scale
     joined = joined_f.astype(BF)
     joined_back = (joined_f * UNIT).astype(BF)
 
@@ -281,24 +318,24 @@
     )(fields, flags)
     coeffs_up, sent = cross_coeffs(coarse, flags, cross_depth)
     coeffs_up = [c.astype(BF) for c in coeffs_up]
-    base = (cross_mix(coeffs_up, joined[depth:], flags, False) + bias_vec.astype(F32)) * STRETCH
+    base = (cross_mix(coeffs_up, joined, flags, False) + bias_vec.astype(F32)) * STRETCH
 
     old = []
-    ranges = pieces(columns, tile, max(1, cross_depth - 1))
+    ranges = pieces(columns, tile, [1] * max(1, cross_depth - 1))
     for (start, stop), token in zip(ranges, sent[-len(ranges) :]):
         kernel = functools.partial(kernel_a, depth, tile, start, stop)
         if not old:
-            kernel = functools.partial(first_call, kernel, 3, 2)
+            kernel = functools.partial(first_call, kernel, 4, 2)
         old = pl.pallas_call(
             kernel,
-            in_specs=[VMEM, VMEM, HBM] + [VMEM] * len(old),
+            in_specs=[VMEM, VMEM, VMEM, HBM] + [VMEM] * len(old),
             out_specs=[VMEM] * 2,
             out_shape=[kept] * 2,
-            input_output_aliases={3: 0, 4: 1} if old else {},
-            scratch_shapes=[mixed_scratch],
+            input_output_aliases={4: 0, 5: 1} if old else {},
+            scratch_shapes=[weight_scratch, mixed_scratch],
             compiler_params=params(12),
             cost_estimate=cost(3, stop - start, 1),
-        )(fields, joined[:depth], token, *old)
+        )(fields, mix_weight, point_weight, token, *old)
     coeffs, partial = old
 
     count_up = cross_depth - 1
@@ -319,11 +356,15 @@
         cost_estimate=cost(4, columns, 1),
     )(partial, cotangent, base, coeffs, upper)
 
-    slope_up, unused_sent = cross_coeffs(slope_coarse, flags, cross_depth)
+    block, slope_up = reduce_down(grads.reshape(-1, channels), slope_coarse, flags, cross_depth)
     slope_up_b = [c.astype(BF) for c in slope_up]
-    back_base = cross_mix(slope_up_b, joined_back[depth:], flags, True)
-
-    ranges = pieces(columns, tile, cross_depth)
+    core = is_upper(flags, 0)
+    upper_part = cross_mix(slope_up_b, joined_back, flags, True, 1)
+    part = mix_row(slope_up_b[0], joined_back[0], True)
+    mine, others = pick(core, upper_part - part, upper_part + part)
+    back_base = join(core, mine, swap(others, 1))
+
+    ranges = pieces(columns, tile, [3, 4, 1] if cross_depth == 4 else [1] * (cross_depth - 1))
     results = []
 
     def beside(n, token):
@@ -332,37 +373,55 @@
         start, stop = ranges[n]
         kernel = functools.partial(kernel_c, depth, tile, start, stop)
         if not results:
-            kernel = functools.partial(first_call, kernel, 4, 1)
+            kernel = functools.partial(first_call, kernel, 5, 1)
         grad_input, zero = pl.pallas_call(
             kernel,
-            in_specs=[VMEM, VMEM, VMEM, HBM] + [HBM] * len(results),
+            in_specs=[VMEM, VMEM, VMEM, VMEM, HBM] + [HBM] * len(results),
             out_specs=[HBM, VMEM],
             out_shape=[jax.ShapeDtypeStruct(shape, BF), jax.ShapeDtypeStruct((1, channels), F32)],
-            input_output_aliases={4: 0} if results else {},
+            input_output_aliases={5: 0} if results else {},
             scratch_shapes=[
-                pltpu.VMEM((rows, stop - start, channels), BF), mixed_scratch, DMA(((stop - start) // tile,))
+                pltpu.VMEM((rows, stop - start, channels), BF), weight_scratch, mixed_scratch, DMA(((stop - start) // tile,))
             ],
             compiler_params=params(12),
             cost_estimate=cost(2, stop - start, 1),
-        )(back, back_base, joined_back[:depth], token, *results)
+        )(back, back_base, mix_weight, point_weight, token, *results)
         results[:] = [grad_input]
         return zero
 
-    summed = sum_devices(grads.reshape(-1, channels), flags, cross_depth, beside)
+    outer = functools.partial(jnp.einsum, "yc,yd->cd", preferred_element_type=F32)
+    own_columns = [pick(core, c[: columns // 2], c[columns // 2 :])[0] for c in coeffs_up[-2:]]
+    top = jnp.concatenate(
+        [outer(c, b) for c, b in zip(own_columns, slope_up_b[-2:])]
+        + [jnp.broadcast_to(jnp.sum(slope_up[-1], axis=0, keepdims=True), (8, channels))]
+    )
+    for degree in reversed(range(1, cross_depth)):
+        other = swap(block, 1 << degree)
+        zero = beside(cross_depth - 2 - degree, block) if degree < cross_depth - 1 else 0.0
+        block = join(is_upper(flags + zero, degree), block, other)
+    other = swap(jnp.concatenate([block, top]), 1)
+    beside(cross_depth - 2, block)
+    half = block.shape[0]
+    low, high = jnp.where(core, other[:half], block), jnp.where(core, block, other[:half])
+    top = top + other[half:]
     grad_input = results[0]
-    summed = summed.reshape(-1, channels, channels)
-    outer = functools.partial(jnp.einsum, "yc,yd->cd", preferred_element_type=F32)
-    top = [outer(c, b) for c, b in zip(coeffs_up[-2:], slope_up_b[-2:])]
-    raw = jnp.concatenate([summed, jnp.stack(top)]) * (scale * UNIT)
 
     global_rows = rows * device_count
     counts = [columns * global_rows / 2 ** (level + 1) for level in range(levels)] + [columns]
-    factors = jnp.array([1.0 / math.sqrt(value) for value in counts], F32)
+    scales = [(power * UNIT, 1.0 / math.sqrt(value)) for power, value in zip(powers, counts)]
     scale_all = 1.0 / math.sqrt(global_rows * columns)
-    grad_mix = (raw * factors[:, None, None]).astype(BF)
-    grad_point = (jnp.sum(raw, axis=0) * scale_all).astype(BF)
-    grad_bias = (jnp.sum(slope_up[-1], axis=0) * (UNIT * scale_all)).astype(BF)
-    return (grad_input, grad_mix, grad_point, grad_bias)
+    grad_mix, grad_point, grad_bias = pl.pallas_call(
+        functools.partial(kernel_last, scales, scale_all, UNIT * scale_all),
+        in_specs=[VMEM] * 4,
+        out_specs=[VMEM] * 3,
+        out_shape=[
+            jax.ShapeDtypeStruct(mix_weight.shape, BF),
+            jax.ShapeDtypeStruct(point_weight.shape, BF),
+            jax.ShapeDtypeStruct((8, channels), BF),
+        ],
+        compiler_params=params(12),
+    )(low, high, top, top[-8:])
+    return (grad_input, grad_mix, grad_point, grad_bias[0])
 
 
 def first_call(kernel, at, count, *refs):

time: 85.4 us -> 81.9 us (0.959)
  starting transfers between devices: 22 us -> 15 us
  waiting for transfers between devices: 20.9 us -> 27.4 us
  other arithmetic: 5.11 us -> 0.93 us
    ppermute x16 -> x13, starting transfers between devices: 22 us -> 15 us  [swap(): lax.ppermute(block, 'gx', [(low, low ^ stride) for low in range(count)])]
    ppermute x16 -> x13, waiting for transfers between devices: 20.9 us -> 27.4 us  [swap(): lax.ppermute(block, 'gx', [(low, low ^ stride) for low in range(count)])]
    convert_element_type x3 -> x1, other arithmetic: 2.17 us -> 0.01 us  [shards(): point_weight.astype(F32)]
    convert_element_type x1, other arithmetic: 1.19 us -> 0.12 us  [shards(): joined_back = (joined_f * UNIT).astype(BF)]
    reduce_sum x2 -> x1, other arithmetic: 1 us -> 0.04 us  [shards(): jnp.sum(slope_up[-1], axis=0, keepdims=True)]
    unnamed x16 -> x14, local copies, waits for them, and re-layouts: 3.42 us -> 3.41 us
  transfers between devices with their start and end apart: 16 -> 13, of which waited for: 12 -> 10; matrix products, arithmetic and copies ran while one was open for 6% -> 2% of each run, Pallas kernels for 19% -> 20%
where the time goes in v3:
time: 81.9 us; the launch traced here: 81.7 us
  Pallas kernels  31.3 us (38%)
  waiting for transfers between devices  27.4 us (33%)
  starting transfers between devices  15 us (18%)
  local copies, waits for them, and re-layouts  4.04 us (5%)
  matrix products  1.84 us (2%)
  between operations  1.11 us (1%)
  other arithmetic  0.93 us (1%)
    ppermute x13, waiting for transfers between devices, swap(): lax.ppermute(block, 'gx', [(low, low ^ stride) for low in range(count)])  27.4 us
    ppermute x13, starting transfers between devices, swap(): lax.ppermute(block, 'gx', [(low, low ^ stride) for low in range(count)])  15 us
    pallas_call x1, Pallas kernels, shards(): pl.pallas_call(functools.partial(kernel_b, depth, tile), in_specs=[VMEM]...  12.8 us
    pallas_call x3, Pallas kernels, beside(): pl.pallas_call(kernel, in_specs=[VMEM, VMEM, VMEM, VMEM, HBM] + [HBM] * l...  9.08 us
    pallas_call x3, Pallas kernels, shards(): pl.pallas_call(kernel, in_specs=[VMEM, VMEM, VMEM, HBM] + [VMEM] * len(ol...  7.05 us
    unnamed x14, local copies, waits for them, and re-layouts  3.41 us
  transfers between devices with their start and end apart: 13, of which 10 were waited for; matrix products, arithmetic and copies ran while one was open for 2% of the time, Pallas kernels for 20%

profile of v3, /device:TPU:0, one launch (start us, length us, event | category | flops | bytes accessed | tf_op | source)
XLA Modules:
  0.0 81.7 jit_solution(15736065012073703380)
XLA Ops:
  0.7 3.4 %copy-done = bf16[128,256,128]{2,1,0:T(8,128)(2,1)S(1)} copy-done((bf16[128,256,128]{2,1,0:T(8,128)(2,1)S(1)}, bf16[128,256,128]{2,1,0:T(8,128)(2,1)}, u32[]{:S(2)}) %copy-start) | copy-done | bytes 8388632
  4.1 1.6 %shard_map.93 = (f32[256,128]{1,0:T(8,128)S(1)}, f32[4,128]{1,0:T(4,128)S(1)}) custom-call(bf16[128,256,128]{2,1,0:T(8,128)(2,1)S(1)} %copy-done, f32[4,128]{1,0:T(4,128)S(1)} %broadcast_in_dim.195.flags_ref), custom_call_target="tpu_custom_call" | custom-call | bytes 8388608 | tf_op jit(solution)/shard_map/pallas_call | solution.py:308
  7.2 2.9 %collective-permute-start.1 = (f32[256,128]{1,0:T(8,128)S(1)}, f32[256,128]{1,0:T(8,128)S(1)}, u32[]{:S(2)}, u32[]{:S(2)}) collective-permute-start(f32[256,128]{1,0:T(8,128)S(1)} %add.99.refs_3_), channel_id=1, source_target_pairs={{0,2},{1,3},{2,0},{3,1},{4,6},{5,7},{6,4},{7,5},{8,10},{9,11},{10,... | collective-permute-start | bytes 393224 | tf_op jit(solution)/shard_map/ppermute | solution.py:194
  10.2 1.8 %shard_map.94 = (bf16[128,256,128]{2,1,0:T(8,128)(2,1)S(1)}, bf16[128,256,128]{2,1,0:T(8,128)(2,1)S(1)}) custom-call(bf16[128,256,128]{2,1,0:T(8,128)(2,1)S(1)} %copy-done, bf16[12,128,128]{2,1,0:T(8,128)(2,1)S(1)} %copy-done.1, bf16[128,128]{1,0:T(8,128)(2,1)S(1)} %copy-done.2, f32[256,128]{1,0:T(8,128)S(1)} %add.99.refs_3_), custom_call_target="tpu_custom_call" | custom-call | flops 268435456 | bytes 6291456 | tf_op jit(solution)/shard_map/pallas_call | solution.py:329
  12.1 1.8 %collective-permute-done.1 = f32[256,128]{1,0:T(8,128)S(1)} collective-permute-done((f32[256,128]{1,0:T(8,128)S(1)}, f32[256,128]{1,0:T(8,128)S(1)}, u32[]{:S(2)}, u32[]{:S(2)}) %collective-permute-start.1) | collective-permute-done | bytes 131104 | tf_op jit(solution)/shard_map/ppermute | solution.py:194
  14.0 1.9 %collective-permute-start.2 = (f32[256,128]{1,0:T(8,128)S(1)}, f32[256,128]{1,0:T(8,128)S(1)}, u32[]{:S(2)}, u32[]{:S(2)}) collective-permute-start(f32[256,128]{1,0:T(8,128)S(1)} %add.100.token_ref), channel_id=1, source_target_pairs={{0,4},{1,5},{2,6},{3,7},{4,0},{5,1},{6,2},{7,3},{8,12},{9,13},{10,... | collective-permute-start | bytes 393224 | tf_op jit(solution)/shard_map/ppermute | solution.py:194
  16.1 2.6 %shard_map.95 = (bf16[128,256,128]{2,1,0:T(8,128)(2,1)S(1)}, bf16[128,256,128]{2,1,0:T(8,128)(2,1)S(1)}) custom-call(bf16[128,256,128]{2,1,0:T(8,128)(2,1)S(1)} %copy-done, bf16[12,128,128]{2,1,0:T(8,128)(2,1)S(1)} %copy-done.1, bf16[128,128]{1,0:T(8,128)(2,1)S(1)} %copy-done.2, ...), custom_call_target="tpu_custom_call", output_to_operand_aliasing={{0}: (4, {}), {1}: (5, {})} | custom-call | flops 402653184 | bytes 9437184 | tf_op jit(solution)/shard_map/pallas_call | solution.py:329
  19.1 2.8 %collective-permute-start.3 = (f32[256,128]{1,0:T(8,128)S(1)}, f32[256,128]{1,0:T(8,128)S(1)}, u32[]{:S(2)}, u32[]{:S(2)}) collective-permute-start(f32[256,128]{1,0:T(8,128)S(1)} %add.101.token_ref), channel_id=1, source_target_pairs={{0,8},{1,9},{2,10},{3,11},{4,12},{5,13},{6,14},{7,15},{8,0},{9,1},... | collective-permute-start | bytes 393224 | tf_op jit(solution)/shard_map/ppermute | solution.py:194
  22.1 2.7 %shard_map.96 = (bf16[128,256,128]{2,1,0:T(8,128)(2,1)S(1)}, bf16[128,256,128]{2,1,0:T(8,128)(2,1)S(1)}) custom-call(bf16[128,256,128]{2,1,0:T(8,128)(2,1)S(1)} %copy-done, bf16[12,128,128]{2,1,0:T(8,128)(2,1)S(1)} %copy-done.1, bf16[128,128]{1,0:T(8,128)(2,1)S(1)} %copy-done.2, ...), custom_call_target="tpu_custom_call", output_to_operand_aliasing={{0}: (4, {}), {1}: (5, {})} | custom-call | flops 402653184 | bytes 9437184 | tf_op jit(solution)/shard_map/pallas_call | solution.py:329
  24.8 2.2 %collective-permute-done.3 = f32[256,128]{1,0:T(8,128)S(1)} collective-permute-done((f32[256,128]{1,0:T(8,128)S(1)}, f32[256,128]{1,0:T(8,128)S(1)}, u32[]{:S(2)}, u32[]{:S(2)}) %collective-permute-start.3) | collective-permute-done | bytes 131104 | tf_op jit(solution)/shard_map/ppermute | solution.py:194
  27.4 12.8 %shard_map.97 = (bf16[128,256,128]{2,1,0:T(8,128)(2,1)S(1)}, f32[256,128]{1,0:T(8,128)S(1)}, f32[10,128,128]{2,1,0:T(8,128)S(1)}) custom-call(bf16[128,256,128]{2,1,0:T(8,128)(2,1)S(1)} %get-tuple-element.28.partial_v, bf16[128,256,128]{2,1,0:T(8,128)(2,1)S(1)} %bitcast.72, f32[256,128]{1,0:T(8,128)S(1)} %fusion.4.base_ref, ...), custom_call_target="tpu_custom_call" | custom-call | flops 1073741824 | bytes 33554432 | tf_op jit(solution)/shard_map/pallas_call | solution.py:346
  40.4 1.7 %collective-permute-done.4 = f32[768,128]{1,0:T(8,128)S(1)} collective-permute-done((f32[768,128]{1,0:T(8,128)S(1)}, f32[768,128]{1,0:T(8,128)S(1)}, u32[]{:S(2)}, u32[]{:S(2)}) %collective-permute-start.4) | collective-permute-done | bytes 393248 | tf_op jit(solution)/shard_map/ppermute | solution.py:194
  42.3 1.5 %collective-permute-start.5 = (f32[448,128]{1,0:T(8,128)S(1)}, f32[448,128]{1,0:T(8,128)S(1)}, u32[]{:S(2)}, u32[]{:S(2)}) collective-permute-start(f32[448,128]{1,0:T(8,128)S(1)} %pad_maximum_fusion.2), channel_id=1, source_target_pairs={{0,2},{1,3},{2,0},{3,1},{4,6},{5,7},{6,4},{7,5},{8,10},{9,11},{10,... | collective-permute-start | bytes 688136 | tf_op jit(solution)/shard_map/ppermute | solution.py:194
  43.9 6.1 %collective-permute-done.5 = f32[448,128]{1,0:T(8,128)S(1)} collective-permute-done((f32[448,128]{1,0:T(8,128)S(1)}, f32[448,128]{1,0:T(8,128)S(1)}, u32[]{:S(2)}, u32[]{:S(2)}) %collective-permute-start.5) | collective-permute-done | bytes 229408 | tf_op jit(solution)/shard_map/ppermute | solution.py:194
  50.7 4.6 %collective-permute-done.6 = f32[288,128]{1,0:T(8,128)S(1)} collective-permute-done((f32[288,128]{1,0:T(8,128)S(1)}, f32[288,128]{1,0:T(8,128)S(1)}, u32[]{:S(2)}, u32[]{:S(2)}) %collective-permute-start.6) | collective-permute-done | bytes 147488 | tf_op jit(solution)/shard_map/ppermute | solution.py:194
  55.3 2.0 %collective-permute-start.7 = (f32[208,128]{1,0:T(8,128)S(1)}, f32[208,128]{1,0:T(8,128)S(1)}, u32[]{:S(2)}, u32[]{:S(2)}) collective-permute-start(f32[208,128]{1,0:T(8,128)S(1)} %pad_maximum_fusion.5), channel_id=1, source_target_pairs={{0,8},{1,9},{2,10},{3,11},{4,12},{5,13},{6,14},{7,15},{8,0},{9,1},... | collective-permute-start | bytes 319496 | tf_op jit(solution)/shard_map/ppermute | solution.py:194
  57.5 4.6 %collective-permute-done.7 = f32[208,128]{1,0:T(8,128)S(1)} collective-permute-done((f32[208,128]{1,0:T(8,128)S(1)}, f32[208,128]{1,0:T(8,128)S(1)}, u32[]{:S(2)}, u32[]{:S(2)}) %collective-permute-start.7) | collective-permute-done | bytes 106528 | tf_op jit(solution)/shard_map/ppermute | solution.py:194
  62.6 1.0 %collective-permute-start.9 = (f32[80,128]{1,0:T(8,128)S(1)}, f32[80,128]{1,0:T(8,128)S(1)}, u32[]{:S(2)}, u32[]{:S(2)}) collective-permute-start(f32[80,128]{1,0:T(8,128)S(1)} %slice_add_fusion.8), channel_id=1, source_target_pairs={{0,8},{1,9},{2,10},{3,11},{4,12},{5,13},{6,14},{7,15},{8,0},{9,1},... | collective-permute-start | bytes 122888 | tf_op jit(solution)/shard_map/ppermute | solution.py:194
  64.0 3.9 %collective-permute-done.9 = f32[80,128]{1,0:T(8,128)S(1)} collective-permute-done((f32[80,128]{1,0:T(8,128)S(1)}, f32[80,128]{1,0:T(8,128)S(1)}, u32[]{:S(2)}, u32[]{:S(2)}) %collective-permute-start.9) | collective-permute-done | bytes 40992 | tf_op jit(solution)/shard_map/ppermute | solution.py:194
  68.1 3.0 %shard_map.98 = (bf16[128,256,128]{2,1,0:T(8,128)(2,1)}, f32[1,128]{1,0:T(1,128)S(1)}) custom-call(bf16[128,256,128]{2,1,0:T(8,128)(2,1)S(1)} %get-tuple-element.31.refs_0_.back_v, f32[256,128]{1,0:T(8,128)S(1)} %maximum_select_fusion.2.refs_1_.base_ref, bf16[12,128,128]{2,1,0:T(8,128)(2,1)S(1)} %copy-done.1, bf16[128,128]{1,0:T(8,128)(2,1)S(1)} %copy-done.2, ...), custom_call_target="tpu_custom_call" | custom-call | flops 402653184 | bytes 6291456 | tf_op jit(solution)/shard_map/pallas_call | solution.py:377
  71.2 1.2 %collective-permute-done.10 = f32[160,128]{1,0:T(8,128)S(1)} collective-permute-done((f32[160,128]{1,0:T(8,128)S(1)}, f32[160,128]{1,0:T(8,128)S(1)}, u32[]{:S(2)}, u32[]{:S(2)}) %collective-permute-start.10) | collective-permute-done | bytes 81952 | tf_op jit(solution)/shard_map/ppermute | solution.py:194
  72.4 1.5 %collective-permute-start.11 = (f32[320,128]{1,0:T(8,128)S(1)}, f32[320,128]{1,0:T(8,128)S(1)}, u32[]{:S(2)}, u32[]{:S(2)}) collective-permute-start(f32[320,128]{1,0:T(8,128)S(1)} %maximum_select_fusion.1.token_ref), channel_id=1, source_target_pairs={{0,2},{1,3},{2,0},{3,1},{4,6},{5,7},{6,4},{7,5},{8,10},{9,11},{10,... | collective-permute-start | bytes 491528 | tf_op jit(solution)/shard_map/ppermute | solution.py:194
  74.0 3.9 %shard_map.99 = (bf16[128,256,128]{2,1,0:T(8,128)(2,1)}, f32[1,128]{1,0:T(1,128)S(1)}) custom-call(bf16[128,256,128]{2,1,0:T(8,128)(2,1)S(1)} %get-tuple-element.31.refs_0_.back_v, f32[256,128]{1,0:T(8,128)S(1)} %maximum_select_fusion.2.refs_1_.base_ref, bf16[12,128,128]{2,1,0:T(8,128)(2,1)S(1)} %copy-done.1, ...), custom_call_target="tpu_custom_call", output_to_operand_aliasing={{0}: (5, {})} | custom-call | flops 536870912 | bytes 8388608 | tf_op jit(solution)/shard_map/pallas_call | solution.py:377
  78.0 2.2 %shard_map.100 = (bf16[128,256,128]{2,1,0:T(8,128)(2,1)}, f32[1,128]{1,0:T(1,128)}) custom-call(bf16[128,256,128]{2,1,0:T(8,128)(2,1)S(1)} %get-tuple-element.31.refs_0_.back_v, f32[256,128]{1,0:T(8,128)S(1)} %maximum_select_fusion.2.refs_1_.base_ref, bf16[12,128,128]{2,1,0:T(8,128)(2,1)S(1)} %copy-done.1, ...), custom_call_target="tpu_custom_call", output_to_operand_aliasing={{0}: (5, {})} | custom-call | flops 134217728 | bytes 2097152 | tf_op jit(solution)/shard_map/pallas_call | solution.py:377
  (84 shorter events, 6.9 us)
Async XLA Ops:
  0.6 5.6 %copy-start.3 = (f32[5]{0:T(128)S(1)}, f32[5]{0:T(128)}, u32[]{:S(2)}) copy-start(f32[5]{0:T(128)} %constant.16.clone) | copy-start | bytes 64
  0.6 5.6 %copy-start.4 = (bf16[128]{0:T(256)(128)(2,1)S(1)}, bf16[128]{0:T(256)(128)(2,1)}, u32[]{:S(2)}) copy-start(bf16[128]{0:T(256)(128)(2,1)} %param.10) | copy-start | bytes 772
  0.7 3.4 %copy-start = (bf16[128,256,128]{2,1,0:T(8,128)(2,1)S(1)}, bf16[128,256,128]{2,1,0:T(8,128)(2,1)}, u32[]{:S(2)}) copy-start(bf16[128,256,128]{2,1,0:T(8,128)(2,1)} %fields_v.5) | copy-start | bytes 25165828
  4.1 2.1 %copy-start.2 = (bf16[128,128]{1,0:T(8,128)(2,1)S(1)}, bf16[128,128]{1,0:T(8,128)(2,1)}, u32[]{:S(2)}) copy-start(bf16[128,128]{1,0:T(8,128)(2,1)} %point_ref.7) | copy-start | bytes 98308
  4.1 2.1 %copy-start.1 = (bf16[12,128,128]{2,1,0:T(8,128)(2,1)S(1)}, bf16[12,128,128]{2,1,0:T(8,128)(2,1)}, u32[]{:S(2)}) copy-start(bf16[12,128,128]{2,1,0:T(8,128)(2,1)} %mix_ref.7) | copy-start | bytes 1179652
  5.7 1.5 %collective-permute-start = (f32[256,128]{1,0:T(8,128)S(1)}, f32[256,128]{1,0:T(8,128)S(1)}, u32[]{:S(2)}, u32[]{:S(2)}) collective-permute-start(f32[256,128]{1,0:T(8,128)S(1)} %get-tuple-element.23), channel_id=1, source_target_pairs={{0,1},{1,0},{2,3},{3,2},{4,5},{5,4},{6,7},{7,6},{8,9},{9,8},{10,11... | collective-permute-start | bytes 393224 | tf_op jit(solution)/shard_map/ppermute | solution.py:194
  7.2 6.7 %collective-permute-start.1 = (f32[256,128]{1,0:T(8,128)S(1)}, f32[256,128]{1,0:T(8,128)S(1)}, u32[]{:S(2)}, u32[]{:S(2)}) collective-permute-start(f32[256,128]{1,0:T(8,128)S(1)} %add.99.refs_3_), channel_id=1, source_target_pairs={{0,2},{1,3},{2,0},{3,1},{4,6},{5,7},{6,4},{7,5},{8,10},{9,11},{10,... | collective-permute-start | bytes 393224 | tf_op jit(solution)/shard_map/ppermute | solution.py:194
  14.0 5.1 %collective-permute-start.2 = (f32[256,128]{1,0:T(8,128)S(1)}, f32[256,128]{1,0:T(8,128)S(1)}, u32[]{:S(2)}, u32[]{:S(2)}) collective-permute-start(f32[256,128]{1,0:T(8,128)S(1)} %add.100.token_ref), channel_id=1, source_target_pairs={{0,4},{1,5},{2,6},{3,7},{4,0},{5,1},{6,2},{7,3},{8,12},{9,13},{10,... | collective-permute-start | bytes 393224 | tf_op jit(solution)/shard_map/ppermute | solution.py:194
  19.1 8.3 %slice-start = ((s8[8388608]{0:T(1024)(128)(4,1)}), s8[4194304]{0:T(1024)(128)(4,1)S(1)}, s32[]{:S(2)}) async-start(s8[8388608]{0:T(1024)(128)(4,1)} %bitcast.71), calls=%async_computation | async-start | bytes 8388608
  19.1 7.9 %collective-permute-start.3 = (f32[256,128]{1,0:T(8,128)S(1)}, f32[256,128]{1,0:T(8,128)S(1)}, u32[]{:S(2)}, u32[]{:S(2)}) collective-permute-start(f32[256,128]{1,0:T(8,128)S(1)} %add.101.token_ref), channel_id=1, source_target_pairs={{0,8},{1,9},{2,10},{3,11},{4,12},{5,13},{6,14},{7,15},{8,0},{9,1},... | collective-permute-start | bytes 393224 | tf_op jit(solution)/shard_map/ppermute | solution.py:194
  22.1 5.3 %slice-start.1 = ((s8[8388608]{0:T(1024)(128)(4,1)}), s8[4194304]{0:T(1024)(128)(4,1)S(1)}, s32[]{:S(2)}) async-start(s8[8388608]{0:T(1024)(128)(4,1)} %bitcast.71), calls=%async_computation.1 | async-start | bytes 8388608
  40.3 1.8 %collective-permute-start.4 = (f32[768,128]{1,0:T(8,128)S(1)}, f32[768,128]{1,0:T(8,128)S(1)}, u32[]{:S(2)}, u32[]{:S(2)}) collective-permute-start(f32[768,128]{1,0:T(8,128)S(1)} %pad_maximum_fusion.1), channel_id=1, source_target_pairs={{0,1},{1,0},{2,3},{3,2},{4,5},{5,4},{6,7},{7,6},{8,9},{9,8},{10,11... | collective-permute-start | bytes 1179656 | tf_op jit(solution)/shard_map/ppermute | solution.py:194
  42.3 7.7 %collective-permute-start.5 = (f32[448,128]{1,0:T(8,128)S(1)}, f32[448,128]{1,0:T(8,128)S(1)}, u32[]{:S(2)}, u32[]{:S(2)}) collective-permute-start(f32[448,128]{1,0:T(8,128)S(1)} %pad_maximum_fusion.2), channel_id=1, source_target_pairs={{0,2},{1,3},{2,0},{3,1},{4,6},{5,7},{6,4},{7,5},{8,10},{9,11},{10,... | collective-permute-start | bytes 688136 | tf_op jit(solution)/shard_map/ppermute | solution.py:194
  50.1 5.2 %collective-permute-start.6 = (f32[288,128]{1,0:T(8,128)S(1)}, f32[288,128]{1,0:T(8,128)S(1)}, u32[]{:S(2)}, u32[]{:S(2)}) collective-permute-start(f32[288,128]{1,0:T(8,128)S(1)} %pad_maximum_fusion.4), channel_id=1, source_target_pairs={{0,4},{1,5},{2,6},{3,7},{4,0},{5,1},{6,2},{7,3},{8,12},{9,13},{10,... | collective-permute-start | bytes 442376 | tf_op jit(solution)/shard_map/ppermute | solution.py:194
  55.3 6.8 %collective-permute-start.7 = (f32[208,128]{1,0:T(8,128)S(1)}, f32[208,128]{1,0:T(8,128)S(1)}, u32[]{:S(2)}, u32[]{:S(2)}) collective-permute-start(f32[208,128]{1,0:T(8,128)S(1)} %pad_maximum_fusion.5), channel_id=1, source_target_pairs={{0,8},{1,9},{2,10},{3,11},{4,12},{5,13},{6,14},{7,15},{8,0},{9,1},... | collective-permute-start | bytes 319496 | tf_op jit(solution)/shard_map/ppermute | solution.py:194
  62.6 5.3 %collective-permute-start.9 = (f32[80,128]{1,0:T(8,128)S(1)}, f32[80,128]{1,0:T(8,128)S(1)}, u32[]{:S(2)}, u32[]{:S(2)}) collective-permute-start(f32[80,128]{1,0:T(8,128)S(1)} %slice_add_fusion.8), channel_id=1, source_target_pairs={{0,8},{1,9},{2,10},{3,11},{4,12},{5,13},{6,14},{7,15},{8,0},{9,1},... | collective-permute-start | bytes 122888 | tf_op jit(solution)/shard_map/ppermute | solution.py:194
  63.9 4.3 %collective-permute-start.8 = (f32[128,128]{1,0:T(8,128)S(1)}, f32[128,128]{1,0:T(8,128)S(1)}, u32[]{:S(2)}, u32[]{:S(2)}) collective-permute-start(f32[128,128]{1,0:T(8,128)S(1)} %get-tuple-element.59), channel_id=1, source_target_pairs={{0,1},{1,0},{2,3},{3,2},{4,5},{5,4},{6,7},{7,6},{8,9},{9,8},{10,11... | collective-permute-start | bytes 196616 | tf_op jit(solution)/shard_map/ppermute | solution.py:194
  67.9 4.5 %collective-permute-start.10 = (f32[160,128]{1,0:T(8,128)S(1)}, f32[160,128]{1,0:T(8,128)S(1)}, u32[]{:S(2)}, u32[]{:S(2)}) collective-permute-start(f32[160,128]{1,0:T(8,128)S(1)} %maximum_select_fusion.3.refs_4_), channel_id=1, source_target_pairs={{0,4},{1,5},{2,6},{3,7},{4,0},{5,1},{6,2},{7,3},{8,12},{9,13},{10,... | collective-permute-start | bytes 245768 | tf_op jit(solution)/shard_map/ppermute | solution.py:194
  72.4 5.4 %collective-permute-start.11 = (f32[320,128]{1,0:T(8,128)S(1)}, f32[320,128]{1,0:T(8,128)S(1)}, u32[]{:S(2)}, u32[]{:S(2)}) collective-permute-start(f32[320,128]{1,0:T(8,128)S(1)} %maximum_select_fusion.1.token_ref), channel_id=1, source_target_pairs={{0,2},{1,3},{2,0},{3,1},{4,6},{5,7},{6,4},{7,5},{8,10},{9,11},{10,... | collective-permute-start | bytes 491528 | tf_op jit(solution)/shard_map/ppermute | solution.py:194
  78.0 2.3 %collective-permute-start.12 = (f32[904,128]{1,0:T(8,128)S(1)}, f32[904,128]{1,0:T(8,128)S(1)}, u32[]{:S(2)}, u32[]{:S(2)}) collective-permute-start(f32[904,128]{1,0:T(8,128)S(1)} %pad_maximum_fusion), channel_id=1, source_target_pairs={{0,1},{1,0},{2,3},{3,2},{4,5},{5,4},{6,7},{7,6},{8,9},{9,8},{10,11... | collective-permute-start | bytes 1388552 | tf_op jit(solution)/shard_map/ppermute | solution.py:194

commit v4 on v3

--- a/solution.py
+++ b/solution.py
@@ -92,9 +92,10 @@
 
 
 def kernel_a(depth, tile, first, stop, fields_v, mix_ref, point_ref, token_ref, old_c, old_p,
-             coeffs_v, partial_v, weight_ref, mixed_ref):
+             coeffs_v, partial_v, done_ref, weight_ref, mixed_ref):
     starts = level_starts(depth)
     zero = jnp.zeros(mixed_ref.shape[1:], F32)
+    done_ref[...] = jnp.zeros_like(done_ref)
     join_weights(mix_ref, point_ref, weight_ref, 1.0)
 
     def step(index, unused):
@@ -198,27 +199,18 @@
     return flags[degree : degree + 1] > 0.5
 
 
-def cross_coeffs(coarse, flags, depth):
-    found, sent = [], []
-    for degree in range(depth):
-        sent.append(coarse)
-        other = swap(coarse, 1 << degree)
-        found.append(jnp.where(is_upper(flags, degree), coarse - other, other - coarse))
-        coarse = coarse + other
-    return found + [coarse], sent
-
-
 def mix_row(coeffs_b, weight, back):
     spec = "yc,dc->yd" if back else "yc,cd->yd"
     return jnp.einsum(spec, coeffs_b, weight, preferred_element_type=F32)
 
 
-def cross_mix(coeffs_b, weights, flags, back, lowest=0):
+def cross_mix(coeffs_b, weights, flags, back):
     total = mix_row(coeffs_b[-1], weights[-1], back)
-    for degree in reversed(range(lowest, len(coeffs_b) - 1)):
+    for degree in reversed(range(1, len(coeffs_b) - 1)):
         part = mix_row(coeffs_b[degree], weights[degree], back)
         total = total + jnp.where(is_upper(flags, degree), part, -part)
-    return total
+    part = mix_row(coeffs_b[0], weights[0], back)
+    return pick(is_upper(flags, 0), total - part, total + part)
 
 
 def pick(upper, low, high):
@@ -229,20 +221,26 @@
     return jnp.where(upper, jnp.concatenate([other, mine]), jnp.concatenate([mine, other]))
 
 
-def reduce_down(block, coarse, flags, depth):
+def climb(coarse, flags, depth, block=None, beside=None):
     found = []
     columns = coarse.shape[0] // 2
     for degree in range(depth):
         upper = is_upper(flags, degree)
-        half = block.shape[0] // 2
-        keep, send = pick(upper, block[:half], block[half:])
-        row_send = coarse
+        send = coarse
         if degree == 0:
-            coarse, row_send = pick(upper, coarse[:columns], coarse[columns:])
-        got = swap(jnp.concatenate([send, row_send]), 1 << degree)
-        block, other = keep + got[:half], got[half:]
+            coarse, send = pick(upper, coarse[:columns], coarse[columns:])
+        other = half = None
+        if block is not None:
+            half = block.shape[0] // 2
+            keep, gone = pick(upper, block[:half], block[half:])
+            send = jnp.concatenate([gone, send])
+        other = swap(send, 1 << degree)
+        if block is not None:
+            block, other = keep + other[:half], other[half:]
         found.append(jnp.where(upper, coarse - other, other - coarse))
         coarse = coarse + other
+        if beside is not None:
+            coarse = coarse + beside(degree, send)
     return block, found + [coarse]
 
 
@@ -253,7 +251,7 @@
     return [(start, stop) for start, stop in zip(edges[:-1], edges[1:]) if stop > start]
 
 
-def kernel_last(scales, point_scale, bias_scale, low_ref, high_ref, top_ref, bias_ref, mix_ref, point_ref, out_ref):
+def kernel_last(scales, point_scale, bias_scale, low_ref, high_ref, top_ref, mix_ref, point_ref, out_ref):
     channels = mix_ref.shape[2]
     half = low_ref.shape[0]
     total = jnp.zeros(point_ref.shape, F32)
@@ -269,7 +267,7 @@
         total = total + raw
         mix_ref[level] = (raw * factor).astype(BF)
     point_ref[...] = (total * point_scale).astype(BF)
-    out_ref[...] = (bias_ref[...] * bias_scale).astype(BF)
+    out_ref[...] = (top_ref[top_ref.shape[0] - 8 : top_ref.shape[0] - 7] * bias_scale).astype(BF)
 
 
 def shards(fields, cotangent, point_weight, mix_weight, bias_vec):
@@ -316,33 +314,45 @@
         compiler_params=params(12),
         cost_estimate=cost(1, columns, 0),
     )(fields, flags)
-    coeffs_up, sent = cross_coeffs(coarse, flags, cross_depth)
-    coeffs_up = [c.astype(BF) for c in coeffs_up]
-    base = (cross_mix(coeffs_up, joined, flags, False) + bias_vec.astype(F32)) * STRETCH
-
+    core = is_upper(flags, 0)
+    count_up = cross_depth - 1
     old = []
-    ranges = pieces(columns, tile, [1] * max(1, cross_depth - 1))
-    for (start, stop), token in zip(ranges, sent[-len(ranges) :]):
+    ranges = pieces(columns, tile, [1] * cross_depth)
+
+    def beside_a(n, token):
+        if not 0 <= n < len(ranges):
+            return 0.0
+        start, stop = ranges[n]
         kernel = functools.partial(kernel_a, depth, tile, start, stop)
         if not old:
             kernel = functools.partial(first_call, kernel, 4, 2)
-        old = pl.pallas_call(
+        coeffs, partial, zero = pl.pallas_call(
             kernel,
             in_specs=[VMEM, VMEM, VMEM, HBM] + [VMEM] * len(old),
-            out_specs=[VMEM] * 2,
-            out_shape=[kept] * 2,
+            out_specs=[VMEM] * 3,
+            out_shape=[kept, kept, jax.ShapeDtypeStruct((1, channels), F32)],
             input_output_aliases={4: 0, 5: 1} if old else {},
             scratch_shapes=[weight_scratch, mixed_scratch],
             compiler_params=params(12),
             cost_estimate=cost(3, stop - start, 1),
         )(fields, mix_weight, point_weight, token, *old)
+        old[:] = [coeffs, partial]
+        return zero
+
+    unused_block, coeffs_up = climb(coarse, flags, cross_depth, None, lambda n, token: beside_a(n - 1, token))
+    coeffs_up_b = [c.astype(BF) for c in coeffs_up]
+    mine, others = cross_mix(coeffs_up_b, joined, flags, False)
+    width = columns // 2
+    message = jnp.concatenate([others] + coeffs_up[:count_up])
+    got = swap(message, 1)
+    beside_a(count_up, message)
     coeffs, partial = old
-
-    count_up = cross_depth - 1
+    base = (join(core, mine, got[:width]) + bias_vec.astype(F32)) * STRETCH
     upper = jnp.stack([
-        jnp.where(is_upper(flags, degree), coeffs_up[degree], -coeffs_up[degree])
-        for degree in range(count_up)
+        (join(core, coeffs_up[n], got[(n + 1) * width : (n + 2) * width]) * (2.0 * flags[n : n + 1] - 1.0)).astype(BF)
+        for n in range(count_up)
     ])
+
     back, slope_coarse, grads = pl.pallas_call(
         functools.partial(kernel_b, depth, tile),
         in_specs=[VMEM] * 5,
@@ -356,15 +366,12 @@
         cost_estimate=cost(4, columns, 1),
     )(partial, cotangent, base, coeffs, upper)
 
-    block, slope_up = reduce_down(grads.reshape(-1, channels), slope_coarse, flags, cross_depth)
+    block, slope_up = climb(slope_coarse, flags, cross_depth, grads.reshape(-1, channels))
     slope_up_b = [c.astype(BF) for c in slope_up]
-    core = is_upper(flags, 0)
-    upper_part = cross_mix(slope_up_b, joined_back, flags, True, 1)
-    part = mix_row(slope_up_b[0], joined_back[0], True)
-    mine, others = pick(core, upper_part - part, upper_part + part)
+    mine, others = cross_mix(slope_up_b, joined_back, flags, True)
     back_base = join(core, mine, swap(others, 1))
 
-    ranges = pieces(columns, tile, [3, 4, 1] if cross_depth == 4 else [1] * (cross_depth - 1))
+    ranges = pieces(columns, tile, [3, 5] if cross_depth == 4 else [1] * (cross_depth - 1))
     results = []
 
     def beside(n, token):
@@ -390,9 +397,8 @@
         return zero
 
     outer = functools.partial(jnp.einsum, "yc,yd->cd", preferred_element_type=F32)
-    own_columns = [pick(core, c[: columns // 2], c[columns // 2 :])[0] for c in coeffs_up[-2:]]
     top = jnp.concatenate(
-        [outer(c, b) for c, b in zip(own_columns, slope_up_b[-2:])]
+        [outer(c, b) for c, b in zip(coeffs_up_b[-2:], slope_up_b[-2:])]
         + [jnp.broadcast_to(jnp.sum(slope_up[-1], axis=0, keepdims=True), (8, channels))]
     )
     for degree in reversed(range(1, cross_depth)):
@@ -412,16 +418,16 @@
     scale_all = 1.0 / math.sqrt(global_rows * columns)
     grad_mix, grad_point, grad_bias = pl.pallas_call(
         functools.partial(kernel_last, scales, scale_all, UNIT * scale_all),
-        in_specs=[VMEM] * 4,
+        in_specs=[VMEM] * 3,
         out_specs=[VMEM] * 3,
         out_shape=[
             jax.ShapeDtypeStruct(mix_weight.shape, BF),
             jax.ShapeDtypeStruct(point_weight.shape, BF),
-            jax.ShapeDtypeStruct((8, channels), BF),
+            jax.ShapeDtypeStruct((1, channels), BF),
         ],
         compiler_params=params(12),
-    )(low, high, top, top[-8:])
-    return (grad_input, grad_mix, grad_point, grad_bias[0])
+    )(low, high, top)
+    return (grad_input, grad_mix, grad_point, grad_bias.reshape(channels))
 
 
 def first_call(kernel, at, count, *refs):

time: 81.9 us -> 80.1 us (0.978)
  waiting for transfers between devices: 27.4 us -> 21.5 us
  starting transfers between devices: 15 us -> 20.2 us
  Pallas kernels: 31.3 us -> 29.9 us
    ppermute x13 -> x14, waiting for transfers between devices: 27.4 us -> 21.5 us  [swap(): lax.ppermute(block, 'gx', [(low, low ^ stride) for low in range(count)])]
    ppermute x13 -> x14, starting transfers between devices: 15 us -> 20.2 us  [swap(): lax.ppermute(block, 'gx', [(low, low ^ stride) for low in range(count)])]
    pallas_call x3 -> x2, Pallas kernels: 9.08 us -> 7.41 us  [beside(): pl.pallas_call(kernel, in_specs=[VMEM, VMEM, VMEM, VMEM, HBM] + [HBM] * l...]
    unnamed x14 -> x18, local copies, waits for them, and re-layouts: 3.41 us -> 4.37 us
    pallas_call x3 -> x4, Pallas kernels: 7.05 us -> 7.21 us  [beside_a(): pl.pallas_call(kernel, in_specs=[VMEM, VMEM, VMEM, HBM] + [VMEM] * len(ol...]
  transfers between devices with their start and end apart: 13 -> 14, of which waited for: 10 -> 11; matrix products, arithmetic and copies ran while one was open for 2% -> 2% of each run, Pallas kernels for 20% -> 18%
where the time goes in v4:
time: 80.1 us; the launch traced here: 79.9 us
  Pallas kernels  29.9 us (37%)
  waiting for transfers between devices  21.5 us (27%)
  starting transfers between devices  20.2 us (25%)
  local copies, waits for them, and re-layouts  4.51 us (6%)
  matrix products  1.79 us (2%)
  between operations  1.12 us (1%)
  other arithmetic  0.93 us (1%)
    ppermute x14, waiting for transfers between devices, swap(): lax.ppermute(block, 'gx', [(low, low ^ stride) for low in range(count)])  21.5 us
    ppermute x14, starting transfers between devices, swap(): lax.ppermute(block, 'gx', [(low, low ^ stride) for low in range(count)])  20.2 us
    pallas_call x1, Pallas kernels, shards(): pl.pallas_call(functools.partial(kernel_b, depth, tile), in_specs=[VMEM]...  12.7 us
    pallas_call x2, Pallas kernels, beside(): pl.pallas_call(kernel, in_specs=[VMEM, VMEM, VMEM, VMEM, HBM] + [HBM] * l...  7.41 us
    pallas_call x4, Pallas kernels, beside_a(): pl.pallas_call(kernel, in_specs=[VMEM, VMEM, VMEM, HBM] + [VMEM] * len(ol...  7.21 us
    unnamed x18, local copies, waits for them, and re-layouts  4.37 us
  transfers between devices with their start and end apart: 14, of which 11 were waited for; matrix products, arithmetic and copies ran while one was open for 2% of the time, Pallas kernels for 18%

profile of v4, /device:TPU:0, one launch (start us, length us, event | category | flops | bytes accessed | tf_op | source)
XLA Modules:
  0.0 79.9 jit_solution(8931464983075162101)
XLA Ops:
  0.7 3.4 %copy-done = bf16[128,256,128]{2,1,0:T(8,128)(2,1)S(1)} copy-done((bf16[128,256,128]{2,1,0:T(8,128)(2,1)S(1)}, bf16[128,256,128]{2,1,0:T(8,128)(2,1)}, u32[]{:S(2)}) %copy-start) | copy-done | bytes 8388632
  4.1 1.6 %shard_map.93 = (f32[256,128]{1,0:T(8,128)S(1)}, f32[4,128]{1,0:T(4,128)S(1)}) custom-call(bf16[128,256,128]{2,1,0:T(8,128)(2,1)S(1)} %copy-done, f32[4,128]{1,0:T(4,128)S(1)} %broadcast_in_dim.191.flags_ref), custom_call_target="tpu_custom_call" | custom-call | bytes 8388608 | tf_op jit(solution)/shard_map/pallas_call | solution.py:306
  7.2 2.9 %collective-permute-start.1 = (f32[128,128]{1,0:T(8,128)S(1)}, f32[128,128]{1,0:T(8,128)S(1)}, u32[]{:S(2)}, u32[]{:S(2)}) collective-permute-start(f32[128,128]{1,0:T(8,128)S(1)} %get-tuple-element.61.refs_3_), channel_id=1, source_target_pairs={{0,2},{1,3},{2,0},{3,1},{4,6},{5,7},{6,4},{7,5},{8,10},{9,11},{10,... | collective-permute-start | bytes 196616 | tf_op jit(solution)/shard_map/ppermute | solution.py:195
  10.2 1.8 %shard_map.94 = (bf16[128,256,128]{2,1,0:T(8,128)(2,1)S(1)}, bf16[128,256,128]{2,1,0:T(8,128)(2,1)S(1)}, f32[1,128]{1,0:T(1,128)S(1)}) custom-call(bf16[128,256,128]{2,1,0:T(8,128)(2,1)S(1)} %copy-done, bf16[12,128,128]{2,1,0:T(8,128)(2,1)S(1)} %copy-done.1, bf16[128,128]{1,0:T(8,128)(2,1)S(1)} %copy-done.2, f32[128,128]{1,0:T(8,128)S(1)} %get-tuple-element.61.refs_3_), custom_call_target="tpu_custom_call" | custom-call | flops 268435456 | bytes 6291456 | tf_op jit(solution)/shard_map/pallas_call | solution.py:329
  12.5 2.0 %collective-permute-start.2 = (f32[128,128]{1,0:T(8,128)S(1)}, f32[128,128]{1,0:T(8,128)S(1)}, u32[]{:S(2)}, u32[]{:S(2)}) collective-permute-start(f32[128,128]{1,0:T(8,128)S(1)} %get-tuple-element.74.token_ref), channel_id=1, source_target_pairs={{0,4},{1,5},{2,6},{3,7},{4,0},{5,1},{6,2},{7,3},{8,12},{9,13},{10,... | collective-permute-start | bytes 196616 | tf_op jit(solution)/shard_map/ppermute | solution.py:195
  14.7 1.8 %shard_map.95 = (bf16[128,256,128]{2,1,0:T(8,128)(2,1)S(1)}, bf16[128,256,128]{2,1,0:T(8,128)(2,1)S(1)}, f32[1,128]{1,0:T(1,128)S(1)}) custom-call(bf16[128,256,128]{2,1,0:T(8,128)(2,1)S(1)} %copy-done, bf16[12,128,128]{2,1,0:T(8,128)(2,1)S(1)} %copy-done.1, bf16[128,128]{1,0:T(8,128)(2,1)S(1)} %copy-done.2, ...), custom_call_target="tpu_custom_call", output_to_operand_aliasing={{0}: (4, {}), {1}: (5, {})} | custom-call | flops 268435456 | bytes 6291456 | tf_op jit(solution)/shard_map/pallas_call | solution.py:329
  16.9 3.0 %collective-permute-start.3 = (f32[128,128]{1,0:T(8,128)S(1)}, f32[128,128]{1,0:T(8,128)S(1)}, u32[]{:S(2)}, u32[]{:S(2)}) collective-permute-start(f32[128,128]{1,0:T(8,128)S(1)} %get-tuple-element.71.token_ref), channel_id=1, source_target_pairs={{0,8},{1,9},{2,10},{3,11},{4,12},{5,13},{6,14},{7,15},{8,0},{9,1},... | collective-permute-start | bytes 196616 | tf_op jit(solution)/shard_map/ppermute | solution.py:195
  20.0 1.8 %shard_map.96 = (bf16[128,256,128]{2,1,0:T(8,128)(2,1)S(1)}, bf16[128,256,128]{2,1,0:T(8,128)(2,1)S(1)}, f32[1,128]{1,0:T(1,128)S(1)}) custom-call(bf16[128,256,128]{2,1,0:T(8,128)(2,1)S(1)} %copy-done, bf16[12,128,128]{2,1,0:T(8,128)(2,1)S(1)} %copy-done.1, bf16[128,128]{1,0:T(8,128)(2,1)S(1)} %copy-done.2, ...), custom_call_target="tpu_custom_call", output_to_operand_aliasing={{0}: (4, {}), {1}: (5, {})} | custom-call | flops 268435456 | bytes 6291456 | tf_op jit(solution)/shard_map/pallas_call | solution.py:329
  22.7 1.9 %shard_map.97 = (bf16[128,256,128]{2,1,0:T(8,128)(2,1)S(1)}, bf16[128,256,128]{2,1,0:T(8,128)(2,1)S(1)}, f32[1,128]{1,0:T(1,128)}) custom-call(bf16[128,256,128]{2,1,0:T(8,128)(2,1)S(1)} %bitcast.84, bf16[12,128,128]{2,1,0:T(8,128)(2,1)S(1)} %copy-done.1, bf16[128,128]{1,0:T(8,128)(2,1)S(1)} %copy-done.2, ...), custom_call_target="tpu_custom_call", output_to_operand_aliasing={{0}: (4, {}), {1}: (5, {})} | custom-call | flops 268435456 | bytes 6291456 | tf_op jit(solution)/shard_map/pallas_call | solution.py:329
  25.7 12.7 %shard_map.98 = (bf16[128,256,128]{2,1,0:T(8,128)(2,1)S(1)}, f32[256,128]{1,0:T(8,128)S(1)}, f32[10,128,128]{2,1,0:T(8,128)S(1)}) custom-call(bf16[128,256,128]{2,1,0:T(8,128)(2,1)S(1)} %get-tuple-element.38.partial_v, bf16[128,256,128]{2,1,0:T(8,128)(2,1)S(1)} %bitcast.86, f32[256,128]{1,0:T(8,128)S(1)} %fusion.6.base_ref, ...), custom_call_target="tpu_custom_call" | custom-call | flops 1073741824 | bytes 33554432 | tf_op jit(solution)/shard_map/pallas_call | solution.py:356
  38.7 1.7 %collective-permute-done.5 = f32[768,128]{1,0:T(8,128)S(1)} collective-permute-done((f32[768,128]{1,0:T(8,128)S(1)}, f32[768,128]{1,0:T(8,128)S(1)}, u32[]{:S(2)}, u32[]{:S(2)}) %collective-permute-start.5) | collective-permute-done | bytes 393248 | tf_op jit(solution)/shard_map/ppermute | solution.py:195
  40.5 2.0 %collective-permute-start.6 = (f32[448,128]{1,0:T(8,128)S(1)}, f32[448,128]{1,0:T(8,128)S(1)}, u32[]{:S(2)}, u32[]{:S(2)}) collective-permute-start(f32[448,128]{1,0:T(8,128)S(1)} %pad_maximum_fusion.3), channel_id=1, source_target_pairs={{0,2},{1,3},{2,0},{3,1},{4,6},{5,7},{6,4},{7,5},{8,10},{9,11},{10,... | collective-permute-start | bytes 688136 | tf_op jit(solution)/shard_map/ppermute | solution.py:195
  42.6 5.8 %collective-permute-done.6 = f32[448,128]{1,0:T(8,128)S(1)} collective-permute-done((f32[448,128]{1,0:T(8,128)S(1)}, f32[448,128]{1,0:T(8,128)S(1)}, u32[]{:S(2)}, u32[]{:S(2)}) %collective-permute-start.6) | collective-permute-done | bytes 229408 | tf_op jit(solution)/shard_map/ppermute | solution.py:195
  48.5 1.9 %collective-permute-start.7 = (f32[288,128]{1,0:T(8,128)S(1)}, f32[288,128]{1,0:T(8,128)S(1)}, u32[]{:S(2)}, u32[]{:S(2)}) collective-permute-start(f32[288,128]{1,0:T(8,128)S(1)} %pad_maximum_fusion.5), channel_id=1, source_target_pairs={{0,4},{1,5},{2,6},{3,7},{4,0},{5,1},{6,2},{7,3},{8,12},{9,13},{10,... | collective-permute-start | bytes 442376 | tf_op jit(solution)/shard_map/ppermute | solution.py:195
  50.5 3.3 %collective-permute-done.7 = f32[288,128]{1,0:T(8,128)S(1)} collective-permute-done((f32[288,128]{1,0:T(8,128)S(1)}, f32[288,128]{1,0:T(8,128)S(1)}, u32[]{:S(2)}, u32[]{:S(2)}) %collective-permute-start.7) | collective-permute-done | bytes 147488 | tf_op jit(solution)/shard_map/ppermute | solution.py:195
  53.9 3.1 %collective-permute-start.8 = (f32[208,128]{1,0:T(8,128)S(1)}, f32[208,128]{1,0:T(8,128)S(1)}, u32[]{:S(2)}, u32[]{:S(2)}) collective-permute-start(f32[208,128]{1,0:T(8,128)S(1)} %pad_maximum_fusion.6), channel_id=1, source_target_pairs={{0,8},{1,9},{2,10},{3,11},{4,12},{5,13},{6,14},{7,15},{8,0},{9,1},... | collective-permute-start | bytes 319496 | tf_op jit(solution)/shard_map/ppermute | solution.py:195
  57.1 4.0 %collective-permute-done.8 = f32[208,128]{1,0:T(8,128)S(1)} collective-permute-done((f32[208,128]{1,0:T(8,128)S(1)}, f32[208,128]{1,0:T(8,128)S(1)}, u32[]{:S(2)}, u32[]{:S(2)}) %collective-permute-start.8) | collective-permute-done | bytes 106528 | tf_op jit(solution)/shard_map/ppermute | solution.py:195
  61.5 1.6 %collective-permute-start.10 = (f32[80,128]{1,0:T(8,128)S(1)}, f32[80,128]{1,0:T(8,128)S(1)}, u32[]{:S(2)}, u32[]{:S(2)}) collective-permute-start(f32[80,128]{1,0:T(8,128)S(1)} %slice_add_fusion.8), channel_id=1, source_target_pairs={{0,8},{1,9},{2,10},{3,11},{4,12},{5,13},{6,14},{7,15},{8,0},{9,1},... | collective-permute-start | bytes 122888 | tf_op jit(solution)/shard_map/ppermute | solution.py:195
  63.6 2.9 %collective-permute-done.10 = f32[80,128]{1,0:T(8,128)S(1)} collective-permute-done((f32[80,128]{1,0:T(8,128)S(1)}, f32[80,128]{1,0:T(8,128)S(1)}, u32[]{:S(2)}, u32[]{:S(2)}) %collective-permute-start.10) | collective-permute-done | bytes 40992 | tf_op jit(solution)/shard_map/ppermute | solution.py:195
  66.5 1.3 %collective-permute-start.11 = (f32[160,128]{1,0:T(8,128)S(1)}, f32[160,128]{1,0:T(8,128)S(1)}, u32[]{:S(2)}, u32[]{:S(2)}) collective-permute-start(f32[160,128]{1,0:T(8,128)S(1)} %maximum_select_fusion.7.refs_4_), channel_id=1, source_target_pairs={{0,4},{1,5},{2,6},{3,7},{4,0},{5,1},{6,2},{7,3},{8,12},{9,13},{10,... | collective-permute-start | bytes 245768 | tf_op jit(solution)/shard_map/ppermute | solution.py:195
  67.7 3.0 %shard_map.99 = (bf16[128,256,128]{2,1,0:T(8,128)(2,1)}, f32[1,128]{1,0:T(1,128)S(1)}) custom-call(bf16[128,256,128]{2,1,0:T(8,128)(2,1)S(1)} %get-tuple-element.40.refs_0_.back_v, f32[256,128]{1,0:T(8,128)S(1)} %maximum_select_fusion.6.refs_1_.base_ref, bf16[12,128,128]{2,1,0:T(8,128)(2,1)S(1)} %copy-done.1, bf16[128,128]{1,0:T(8,128)(2,1)S(1)} %copy-done.2, ...), custom_call_target="tpu_custom_call" | custom-call | flops 402653184 | bytes 6291456 | tf_op jit(solution)/shard_map/pallas_call | solution.py:384
  71.0 1.6 %collective-permute-start.12 = (f32[320,128]{1,0:T(8,128)S(1)}, f32[320,128]{1,0:T(8,128)S(1)}, u32[]{:S(2)}, u32[]{:S(2)}) collective-permute-start(f32[320,128]{1,0:T(8,128)S(1)} %maximum_select_fusion.1.token_ref), channel_id=1, source_target_pairs={{0,2},{1,3},{2,0},{3,1},{4,6},{5,7},{6,4},{7,5},{8,10},{9,11},{10,... | collective-permute-start | bytes 491528 | tf_op jit(solution)/shard_map/ppermute | solution.py:195
  72.6 4.4 %shard_map.100 = (bf16[128,256,128]{2,1,0:T(8,128)(2,1)}, f32[1,128]{1,0:T(1,128)S(1)}) custom-call(bf16[128,256,128]{2,1,0:T(8,128)(2,1)S(1)} %get-tuple-element.40.refs_0_.back_v, f32[256,128]{1,0:T(8,128)S(1)} %maximum_select_fusion.6.refs_1_.base_ref, bf16[12,128,128]{2,1,0:T(8,128)(2,1)S(1)} %copy-done.1, ...), custom_call_target="tpu_custom_call", output_to_operand_aliasing={{0}: (5, {})} | custom-call | flops 671088640 | bytes 10485760 | tf_op jit(solution)/shard_map/pallas_call | solution.py:384
  77.1 1.8 %collective-permute-done.13 = f32[904,128]{1,0:T(8,128)S(1)} collective-permute-done((f32[904,128]{1,0:T(8,128)S(1)}, f32[904,128]{1,0:T(8,128)S(1)}, u32[]{:S(2)}, u32[]{:S(2)}) %collective-permute-start.13) | collective-permute-done | bytes 462880 | tf_op jit(solution)/shard_map/ppermute | solution.py:195
  (92 shorter events, 7.7 us)
Async XLA Ops:
  0.6 5.6 %copy-start.3 = (f32[5]{0:T(128)S(1)}, f32[5]{0:T(128)}, u32[]{:S(2)}) copy-start(f32[5]{0:T(128)} %constant.23.clone) | copy-start | bytes 64
  0.7 3.4 %copy-start = (bf16[128,256,128]{2,1,0:T(8,128)(2,1)S(1)}, bf16[128,256,128]{2,1,0:T(8,128)(2,1)}, u32[]{:S(2)}) copy-start(bf16[128,256,128]{2,1,0:T(8,128)(2,1)} %fields_v.7) | copy-start | bytes 25165828
  4.1 2.2 %copy-start.2 = (bf16[128,128]{1,0:T(8,128)(2,1)S(1)}, bf16[128,128]{1,0:T(8,128)(2,1)}, u32[]{:S(2)}) copy-start(bf16[128,128]{1,0:T(8,128)(2,1)} %point_ref.7) | copy-start | bytes 98308
  4.1 2.2 %copy-start.1 = (bf16[12,128,128]{2,1,0:T(8,128)(2,1)S(1)}, bf16[12,128,128]{2,1,0:T(8,128)(2,1)}, u32[]{:S(2)}) copy-start(bf16[12,128,128]{2,1,0:T(8,128)(2,1)} %mix_ref.7) | copy-start | bytes 1179652
  5.7 1.4 %collective-permute-start = (f32[128,128]{1,0:T(8,128)S(1)}, f32[128,128]{1,0:T(8,128)S(1)}, u32[]{:S(2)}, u32[]{:S(2)}) collective-permute-start(f32[128,128]{1,0:T(8,128)S(1)} %slice_select_fusion.6), channel_id=1, source_target_pairs={{0,1},{1,0},{2,3},{3,2},{4,5},{5,4},{6,7},{7,6},{8,9},{9,8},{10,11... | collective-permute-start | bytes 196616 | tf_op jit(solution)/shard_map/ppermute | solution.py:195
  7.2 5.3 %collective-permute-start.1 = (f32[128,128]{1,0:T(8,128)S(1)}, f32[128,128]{1,0:T(8,128)S(1)}, u32[]{:S(2)}, u32[]{:S(2)}) collective-permute-start(f32[128,128]{1,0:T(8,128)S(1)} %get-tuple-element.61.refs_3_), channel_id=1, source_target_pairs={{0,2},{1,3},{2,0},{3,1},{4,6},{5,7},{6,4},{7,5},{8,10},{9,11},{10,... | collective-permute-start | bytes 196616 | tf_op jit(solution)/shard_map/ppermute | solution.py:195
  12.5 4.3 %collective-permute-start.2 = (f32[128,128]{1,0:T(8,128)S(1)}, f32[128,128]{1,0:T(8,128)S(1)}, u32[]{:S(2)}, u32[]{:S(2)}) collective-permute-start(f32[128,128]{1,0:T(8,128)S(1)} %get-tuple-element.74.token_ref), channel_id=1, source_target_pairs={{0,4},{1,5},{2,6},{3,7},{4,0},{5,1},{6,2},{7,3},{8,12},{9,13},{10,... | collective-permute-start | bytes 196616 | tf_op jit(solution)/shard_map/ppermute | solution.py:195
  14.7 8.0 %slice-start = ((s8[8388608]{0:T(1024)(128)(4,1)}), s8[4194304]{0:T(1024)(128)(4,1)S(1)}, s32[]{:S(2)}) async-start(s8[8388608]{0:T(1024)(128)(4,1)} %bitcast.83), calls=%async_computation | async-start | bytes 8388608
  16.9 5.3 %collective-permute-start.3 = (f32[128,128]{1,0:T(8,128)S(1)}, f32[128,128]{1,0:T(8,128)S(1)}, u32[]{:S(2)}, u32[]{:S(2)}) collective-permute-start(f32[128,128]{1,0:T(8,128)S(1)} %get-tuple-element.71.token_ref), channel_id=1, source_target_pairs={{0,8},{1,9},{2,10},{3,11},{4,12},{5,13},{6,14},{7,15},{8,0},{9,1},... | collective-permute-start | bytes 196616 | tf_op jit(solution)/shard_map/ppermute | solution.py:195
  20.0 2.6 %copy-start.4 = (bf16[128]{0:T(256)(128)(2,1)S(1)}, bf16[128]{0:T(256)(128)(2,1)}, u32[]{:S(2)}) copy-start(bf16[128]{0:T(256)(128)(2,1)} %param.10) | copy-start | bytes 772
  20.0 2.6 %slice-start.1 = ((s8[8388608]{0:T(1024)(128)(4,1)}), s8[4194304]{0:T(1024)(128)(4,1)S(1)}, s32[]{:S(2)}) async-start(s8[8388608]{0:T(1024)(128)(4,1)} %bitcast.83), calls=%async_computation.1 | async-start | bytes 8388608
  22.2 2.5 %slice-start.2 = ((s8[8388608]{0:T(1024)(128)(4,1)}), s8[4194304]{0:T(1024)(128)(4,1)S(1)}, s32[]{:S(2)}) async-start(s8[8388608]{0:T(1024)(128)(4,1)} %bitcast.85), calls=%async_computation.2 | async-start | bytes 8388608
  22.5 2.0 %collective-permute-start.4 = (f32[512,128]{1,0:T(8,128)S(1)}, f32[512,128]{1,0:T(8,128)S(1)}, u32[]{:S(2)}, u32[]{:S(2)}) collective-permute-start(f32[512,128]{1,0:T(8,128)S(1)} %pad_maximum_fusion.2.token_ref), channel_id=1, source_target_pairs={{0,1},{1,0},{2,3},{3,2},{4,5},{5,4},{6,7},{7,6},{8,9},{9,8},{10,11... | collective-permute-start | bytes 786440 | tf_op jit(solution)/shard_map/ppermute | solution.py:195
  22.6 3.0 %slice-start.3 = ((s8[8388608]{0:T(1024)(128)(4,1)}), s8[4194304]{0:T(1024)(128)(4,1)S(1)}, s32[]{:S(2)}) async-start(s8[8388608]{0:T(1024)(128)(4,1)} %bitcast.85), calls=%async_computation.3 | async-start | bytes 8388608
  38.6 1.8 %collective-permute-start.5 = (f32[768,128]{1,0:T(8,128)S(1)}, f32[768,128]{1,0:T(8,128)S(1)}, u32[]{:S(2)}, u32[]{:S(2)}) collective-permute-start(f32[768,128]{1,0:T(8,128)S(1)} %pad_maximum_fusion.1), channel_id=1, source_target_pairs={{0,1},{1,0},{2,3},{3,2},{4,5},{5,4},{6,7},{7,6},{8,9},{9,8},{10,11... | collective-permute-start | bytes 1179656 | tf_op jit(solution)/shard_map/ppermute | solution.py:195
  40.5 7.9 %collective-permute-start.6 = (f32[448,128]{1,0:T(8,128)S(1)}, f32[448,128]{1,0:T(8,128)S(1)}, u32[]{:S(2)}, u32[]{:S(2)}) collective-permute-start(f32[448,128]{1,0:T(8,128)S(1)} %pad_maximum_fusion.3), channel_id=1, source_target_pairs={{0,2},{1,3},{2,0},{3,1},{4,6},{5,7},{6,4},{7,5},{8,10},{9,11},{10,... | collective-permute-start | bytes 688136 | tf_op jit(solution)/shard_map/ppermute | solution.py:195
  48.5 5.3 %collective-permute-start.7 = (f32[288,128]{1,0:T(8,128)S(1)}, f32[288,128]{1,0:T(8,128)S(1)}, u32[]{:S(2)}, u32[]{:S(2)}) collective-permute-start(f32[288,128]{1,0:T(8,128)S(1)} %pad_maximum_fusion.5), channel_id=1, source_target_pairs={{0,4},{1,5},{2,6},{3,7},{4,0},{5,1},{6,2},{7,3},{8,12},{9,13},{10,... | collective-permute-start | bytes 442376 | tf_op jit(solution)/shard_map/ppermute | solution.py:195
  53.9 7.2 %collective-permute-start.8 = (f32[208,128]{1,0:T(8,128)S(1)}, f32[208,128]{1,0:T(8,128)S(1)}, u32[]{:S(2)}, u32[]{:S(2)}) collective-permute-start(f32[208,128]{1,0:T(8,128)S(1)} %pad_maximum_fusion.6), channel_id=1, source_target_pairs={{0,8},{1,9},{2,10},{3,11},{4,12},{5,13},{6,14},{7,15},{8,0},{9,1},... | collective-permute-start | bytes 319496 | tf_op jit(solution)/shard_map/ppermute | solution.py:195
  61.5 5.0 %collective-permute-start.10 = (f32[80,128]{1,0:T(8,128)S(1)}, f32[80,128]{1,0:T(8,128)S(1)}, u32[]{:S(2)}, u32[]{:S(2)}) collective-permute-start(f32[80,128]{1,0:T(8,128)S(1)} %slice_add_fusion.8), channel_id=1, source_target_pairs={{0,8},{1,9},{2,10},{3,11},{4,12},{5,13},{6,14},{7,15},{8,0},{9,1},... | collective-permute-start | bytes 122888 | tf_op jit(solution)/shard_map/ppermute | solution.py:195
  63.5 4.2 %collective-permute-start.9 = (f32[128,128]{1,0:T(8,128)S(1)}, f32[128,128]{1,0:T(8,128)S(1)}, u32[]{:S(2)}, u32[]{:S(2)}) collective-permute-start(f32[128,128]{1,0:T(8,128)S(1)} %get-tuple-element.65), channel_id=1, source_target_pairs={{0,1},{1,0},{2,3},{3,2},{4,5},{5,4},{6,7},{7,6},{8,9},{9,8},{10,11... | collective-permute-start | bytes 196616 | tf_op jit(solution)/shard_map/ppermute | solution.py:195
  66.5 4.5 %collective-permute-start.11 = (f32[160,128]{1,0:T(8,128)S(1)}, f32[160,128]{1,0:T(8,128)S(1)}, u32[]{:S(2)}, u32[]{:S(2)}) collective-permute-start(f32[160,128]{1,0:T(8,128)S(1)} %maximum_select_fusion.7.refs_4_), channel_id=1, source_target_pairs={{0,4},{1,5},{2,6},{3,7},{4,0},{5,1},{6,2},{7,3},{8,12},{9,13},{10,... | collective-permute-start | bytes 245768 | tf_op jit(solution)/shard_map/ppermute | solution.py:195
  71.0 6.0 %collective-permute-start.12 = (f32[320,128]{1,0:T(8,128)S(1)}, f32[320,128]{1,0:T(8,128)S(1)}, u32[]{:S(2)}, u32[]{:S(2)}) collective-permute-start(f32[320,128]{1,0:T(8,128)S(1)} %maximum_select_fusion.1.token_ref), channel_id=1, source_target_pairs={{0,2},{1,3},{2,0},{3,1},{4,6},{5,7},{6,4},{7,5},{8,10},{9,11},{10,... | collective-permute-start | bytes 491528 | tf_op jit(solution)/shard_map/ppermute | solution.py:195
  77.1 1.9 %collective-permute-start.13 = (f32[904,128]{1,0:T(8,128)S(1)}, f32[904,128]{1,0:T(8,128)S(1)}, u32[]{:S(2)}, u32[]{:S(2)}) collective-permute-start(f32[904,128]{1,0:T(8,128)S(1)} %pad_maximum_fusion), channel_id=1, source_target_pairs={{0,1},{1,0},{2,3},{3,2},{4,5},{5,4},{6,7},{7,6},{8,9},{9,8},{10,11... | collective-permute-start | bytes 1388552 | tf_op jit(solution)/shard_map/ppermute | solution.py:195

commit v5 on v4

--- a/solution.py
+++ b/solution.py
@@ -11,6 +11,7 @@
 BF = jnp.bfloat16
 F32 = jnp.float32
 TILE = 32
+WIDE = 64
 HBM = pl.BlockSpec(memory_space=pltpu.HBM)
 VMEM = pl.BlockSpec(memory_space=pltpu.VMEM)
 MIB = 1024 * 1024
@@ -289,6 +290,8 @@
     DMA = pltpu.SemaphoreType.DMA
     weight_scratch = pltpu.VMEM((depth, channels, channels), BF)
     mixed_scratch = pltpu.VMEM((rows, tile, channels), F32)
+    wide = min(WIDE, columns)
+    wide_scratch = pltpu.VMEM((rows, wide, channels), F32)
 
     def cost(passes, width, products):
         return pl.CostEstimate(
@@ -317,13 +320,13 @@
     core = is_upper(flags, 0)
     count_up = cross_depth - 1
     old = []
-    ranges = pieces(columns, tile, [1] * cross_depth)
+    ranges = pieces(columns, wide, [1] * cross_depth)
 
     def beside_a(n, token):
         if not 0 <= n < len(ranges):
             return 0.0
         start, stop = ranges[n]
-        kernel = functools.partial(kernel_a, depth, tile, start, stop)
+        kernel = functools.partial(kernel_a, depth, wide, start, stop)
         if not old:
             kernel = functools.partial(first_call, kernel, 4, 2)
         coeffs, partial, zero = pl.pallas_call(
@@ -332,7 +335,7 @@
             out_specs=[VMEM] * 3,
             out_shape=[kept, kept, jax.ShapeDtypeStruct((1, channels), F32)],
             input_output_aliases={4: 0, 5: 1} if old else {},
-            scratch_shapes=[weight_scratch, mixed_scratch],
+            scratch_shapes=[weight_scratch, wide_scratch],
             compiler_params=params(12),
             cost_estimate=cost(3, stop - start, 1),
         )(fields, mix_weight, point_weight, token, *old)
@@ -354,7 +357,7 @@
     ])
 
     back, slope_coarse, grads = pl.pallas_call(
-        functools.partial(kernel_b, depth, tile),
+        functools.partial(kernel_b, depth, wide),
         in_specs=[VMEM] * 5,
         out_specs=[VMEM] * 3,
         out_shape=[

time: 80.1 us -> 79.2 us (0.989)
  Pallas kernels: 29.9 us -> 28.8 us
    pallas_call x1, Pallas kernels: 12.7 us -> 11.9 us  [shards(): pl.pallas_call(functools.partial(kernel_b, depth, wide), in_specs=[VMEM]...]
where the time goes in v5:
time: 79.2 us; the launch traced here: 79 us
  Pallas kernels  28.8 us (36%)
  waiting for transfers between devices  22 us (28%)
  starting transfers between devices  20.2 us (26%)
  local copies, waits for them, and re-layouts  4.21 us (5%)
  matrix products  1.79 us (2%)
  between operations  1.1 us (1%)
  other arithmetic  0.93 us (1%)
    ppermute x14, waiting for transfers between devices, swap(): lax.ppermute(block, 'gx', [(low, low ^ stride) for low in range(count)])  22 us
    ppermute x14, starting transfers between devices, swap(): lax.ppermute(block, 'gx', [(low, low ^ stride) for low in range(count)])  20.2 us
    pallas_call x1, Pallas kernels, shards(): pl.pallas_call(functools.partial(kernel_b, depth, wide), in_specs=[VMEM]...  11.9 us
    pallas_call x2, Pallas kernels, beside(): pl.pallas_call(kernel, in_specs=[VMEM, VMEM, VMEM, VMEM, HBM] + [HBM] * l...  7.4 us
    pallas_call x4, Pallas kernels, beside_a(): pl.pallas_call(kernel, in_specs=[VMEM, VMEM, VMEM, HBM] + [VMEM] * len(ol...  7.06 us
    unnamed x18, local copies, waits for them, and re-layouts  4.08 us
    pallas_call x1, Pallas kernels, shards(): pl.pallas_call(functools.partial(kernel_sum, tile), in_specs=[VMEM, VMEM]...  1.6 us
  transfers between devices with their start and end apart: 14, of which 11 were waited for; matrix products, arithmetic and copies ran while one was open for 2% of the time, Pallas kernels for 18%

profile of v5, /device:TPU:0, one launch (start us, length us, event | category | flops | bytes accessed | tf_op | source)
XLA Modules:
  0.0 79.0 jit_solution(6626790016594520852)
XLA Ops:
  0.7 3.4 %copy-done = bf16[128,256,128]{2,1,0:T(8,128)(2,1)S(1)} copy-done((bf16[128,256,128]{2,1,0:T(8,128)(2,1)S(1)}, bf16[128,256,128]{2,1,0:T(8,128)(2,1)}, u32[]{:S(2)}) %copy-start) | copy-done | bytes 8388632
  4.1 1.6 %shard_map.93 = (f32[256,128]{1,0:T(8,128)S(1)}, f32[4,128]{1,0:T(4,128)S(1)}) custom-call(bf16[128,256,128]{2,1,0:T(8,128)(2,1)S(1)} %copy-done, f32[4,128]{1,0:T(4,128)S(1)} %broadcast_in_dim.191.flags_ref), custom_call_target="tpu_custom_call" | custom-call | bytes 8388608 | tf_op jit(solution)/shard_map/pallas_call | solution.py:309
  7.2 2.9 %collective-permute-start.1 = (f32[128,128]{1,0:T(8,128)S(1)}, f32[128,128]{1,0:T(8,128)S(1)}, u32[]{:S(2)}, u32[]{:S(2)}) collective-permute-start(f32[128,128]{1,0:T(8,128)S(1)} %get-tuple-element.61.refs_3_), channel_id=1, source_target_pairs={{0,2},{1,3},{2,0},{3,1},{4,6},{5,7},{6,4},{7,5},{8,10},{9,11},{10,... | collective-permute-start | bytes 196616 | tf_op jit(solution)/shard_map/ppermute | solution.py:196
  10.2 1.6 %shard_map.94 = (bf16[128,256,128]{2,1,0:T(8,128)(2,1)S(1)}, bf16[128,256,128]{2,1,0:T(8,128)(2,1)S(1)}, f32[1,128]{1,0:T(1,128)S(1)}) custom-call(bf16[128,256,128]{2,1,0:T(8,128)(2,1)S(1)} %copy-done, bf16[12,128,128]{2,1,0:T(8,128)(2,1)S(1)} %copy-done.1, bf16[128,128]{1,0:T(8,128)(2,1)S(1)} %copy-done.2, f32[128,128]{1,0:T(8,128)S(1)} %get-tuple-element.61.refs_3_), custom_call_target="tpu_custom_call" | custom-call | flops 268435456 | bytes 6291456 | tf_op jit(solution)/shard_map/pallas_call | solution.py:332
  12.5 2.0 %collective-permute-start.2 = (f32[128,128]{1,0:T(8,128)S(1)}, f32[128,128]{1,0:T(8,128)S(1)}, u32[]{:S(2)}, u32[]{:S(2)}) collective-permute-start(f32[128,128]{1,0:T(8,128)S(1)} %get-tuple-element.74.token_ref), channel_id=1, source_target_pairs={{0,4},{1,5},{2,6},{3,7},{4,0},{5,1},{6,2},{7,3},{8,12},{9,13},{10,... | collective-permute-start | bytes 196616 | tf_op jit(solution)/shard_map/ppermute | solution.py:196
  14.7 1.6 %shard_map.95 = (bf16[128,256,128]{2,1,0:T(8,128)(2,1)S(1)}, bf16[128,256,128]{2,1,0:T(8,128)(2,1)S(1)}, f32[1,128]{1,0:T(1,128)S(1)}) custom-call(bf16[128,256,128]{2,1,0:T(8,128)(2,1)S(1)} %copy-done, bf16[12,128,128]{2,1,0:T(8,128)(2,1)S(1)} %copy-done.1, bf16[128,128]{1,0:T(8,128)(2,1)S(1)} %copy-done.2, ...), custom_call_target="tpu_custom_call", output_to_operand_aliasing={{0}: (4, {}), {1}: (5, {})} | custom-call | flops 268435456 | bytes 6291456 | tf_op jit(solution)/shard_map/pallas_call | solution.py:332
  16.9 3.0 %collective-permute-start.3 = (f32[128,128]{1,0:T(8,128)S(1)}, f32[128,128]{1,0:T(8,128)S(1)}, u32[]{:S(2)}, u32[]{:S(2)}) collective-permute-start(f32[128,128]{1,0:T(8,128)S(1)} %get-tuple-element.71.token_ref), channel_id=1, source_target_pairs={{0,8},{1,9},{2,10},{3,11},{4,12},{5,13},{6,14},{7,15},{8,0},{9,1},... | collective-permute-start | bytes 196616 | tf_op jit(solution)/shard_map/ppermute | solution.py:196
  20.0 1.6 %shard_map.96 = (bf16[128,256,128]{2,1,0:T(8,128)(2,1)S(1)}, bf16[128,256,128]{2,1,0:T(8,128)(2,1)S(1)}, f32[1,128]{1,0:T(1,128)S(1)}) custom-call(bf16[128,256,128]{2,1,0:T(8,128)(2,1)S(1)} %copy-done, bf16[12,128,128]{2,1,0:T(8,128)(2,1)S(1)} %copy-done.1, bf16[128,128]{1,0:T(8,128)(2,1)S(1)} %copy-done.2, ...), custom_call_target="tpu_custom_call", output_to_operand_aliasing={{0}: (4, {}), {1}: (5, {})} | custom-call | flops 268435456 | bytes 6291456 | tf_op jit(solution)/shard_map/pallas_call | solution.py:332
  22.7 2.2 %shard_map.97 = (bf16[128,256,128]{2,1,0:T(8,128)(2,1)S(1)}, bf16[128,256,128]{2,1,0:T(8,128)(2,1)S(1)}, f32[1,128]{1,0:T(1,128)}) custom-call(bf16[128,256,128]{2,1,0:T(8,128)(2,1)S(1)} %bitcast.84, bf16[12,128,128]{2,1,0:T(8,128)(2,1)S(1)} %copy-done.1, bf16[128,128]{1,0:T(8,128)(2,1)S(1)} %copy-done.2, ...), custom_call_target="tpu_custom_call", output_to_operand_aliasing={{0}: (4, {}), {1}: (5, {})} | custom-call | flops 268435456 | bytes 6291456 | tf_op jit(solution)/shard_map/pallas_call | solution.py:332
  25.7 11.9 %shard_map.98 = (bf16[128,256,128]{2,1,0:T(8,128)(2,1)S(1)}, f32[256,128]{1,0:T(8,128)S(1)}, f32[10,128,128]{2,1,0:T(8,128)S(1)}) custom-call(bf16[128,256,128]{2,1,0:T(8,128)(2,1)S(1)} %get-tuple-element.38.partial_v, bf16[128,256,128]{2,1,0:T(8,128)(2,1)S(1)} %bitcast.86, f32[256,128]{1,0:T(8,128)S(1)} %fusion.6.base_ref, ...), custom_call_target="tpu_custom_call" | custom-call | flops 1073741824 | bytes 33554432 | tf_op jit(solution)/shard_map/pallas_call | solution.py:359
  37.8 1.7 %collective-permute-done.5 = f32[768,128]{1,0:T(8,128)S(1)} collective-permute-done((f32[768,128]{1,0:T(8,128)S(1)}, f32[768,128]{1,0:T(8,128)S(1)}, u32[]{:S(2)}, u32[]{:S(2)}) %collective-permute-start.5) | collective-permute-done | bytes 393248 | tf_op jit(solution)/shard_map/ppermute | solution.py:196
  39.6 2.0 %collective-permute-start.6 = (f32[448,128]{1,0:T(8,128)S(1)}, f32[448,128]{1,0:T(8,128)S(1)}, u32[]{:S(2)}, u32[]{:S(2)}) collective-permute-start(f32[448,128]{1,0:T(8,128)S(1)} %pad_maximum_fusion.3), channel_id=1, source_target_pairs={{0,2},{1,3},{2,0},{3,1},{4,6},{5,7},{6,4},{7,5},{8,10},{9,11},{10,... | collective-permute-start | bytes 688136 | tf_op jit(solution)/shard_map/ppermute | solution.py:196
  41.7 5.8 %collective-permute-done.6 = f32[448,128]{1,0:T(8,128)S(1)} collective-permute-done((f32[448,128]{1,0:T(8,128)S(1)}, f32[448,128]{1,0:T(8,128)S(1)}, u32[]{:S(2)}, u32[]{:S(2)}) %collective-permute-start.6) | collective-permute-done | bytes 229408 | tf_op jit(solution)/shard_map/ppermute | solution.py:196
  47.6 1.9 %collective-permute-start.7 = (f32[288,128]{1,0:T(8,128)S(1)}, f32[288,128]{1,0:T(8,128)S(1)}, u32[]{:S(2)}, u32[]{:S(2)}) collective-permute-start(f32[288,128]{1,0:T(8,128)S(1)} %pad_maximum_fusion.5), channel_id=1, source_target_pairs={{0,4},{1,5},{2,6},{3,7},{4,0},{5,1},{6,2},{7,3},{8,12},{9,13},{10,... | collective-permute-start | bytes 442376 | tf_op jit(solution)/shard_map/ppermute | solution.py:196
  49.6 3.3 %collective-permute-done.7 = f32[288,128]{1,0:T(8,128)S(1)} collective-permute-done((f32[288,128]{1,0:T(8,128)S(1)}, f32[288,128]{1,0:T(8,128)S(1)}, u32[]{:S(2)}, u32[]{:S(2)}) %collective-permute-start.7) | collective-permute-done | bytes 147488 | tf_op jit(solution)/shard_map/ppermute | solution.py:196
  53.0 3.1 %collective-permute-start.8 = (f32[208,128]{1,0:T(8,128)S(1)}, f32[208,128]{1,0:T(8,128)S(1)}, u32[]{:S(2)}, u32[]{:S(2)}) collective-permute-start(f32[208,128]{1,0:T(8,128)S(1)} %pad_maximum_fusion.6), channel_id=1, source_target_pairs={{0,8},{1,9},{2,10},{3,11},{4,12},{5,13},{6,14},{7,15},{8,0},{9,1},... | collective-permute-start | bytes 319496 | tf_op jit(solution)/shard_map/ppermute | solution.py:196
  56.3 4.0 %collective-permute-done.8 = f32[208,128]{1,0:T(8,128)S(1)} collective-permute-done((f32[208,128]{1,0:T(8,128)S(1)}, f32[208,128]{1,0:T(8,128)S(1)}, u32[]{:S(2)}, u32[]{:S(2)}) %collective-permute-start.8) | collective-permute-done | bytes 106528 | tf_op jit(solution)/shard_map/ppermute | solution.py:196
  60.6 1.6 %collective-permute-start.10 = (f32[80,128]{1,0:T(8,128)S(1)}, f32[80,128]{1,0:T(8,128)S(1)}, u32[]{:S(2)}, u32[]{:S(2)}) collective-permute-start(f32[80,128]{1,0:T(8,128)S(1)} %slice_add_fusion.8), channel_id=1, source_target_pairs={{0,8},{1,9},{2,10},{3,11},{4,12},{5,13},{6,14},{7,15},{8,0},{9,1},... | collective-permute-start | bytes 122888 | tf_op jit(solution)/shard_map/ppermute | solution.py:196
  62.7 2.9 %collective-permute-done.10 = f32[80,128]{1,0:T(8,128)S(1)} collective-permute-done((f32[80,128]{1,0:T(8,128)S(1)}, f32[80,128]{1,0:T(8,128)S(1)}, u32[]{:S(2)}, u32[]{:S(2)}) %collective-permute-start.10) | collective-permute-done | bytes 40992 | tf_op jit(solution)/shard_map/ppermute | solution.py:196
  65.6 1.3 %collective-permute-start.11 = (f32[160,128]{1,0:T(8,128)S(1)}, f32[160,128]{1,0:T(8,128)S(1)}, u32[]{:S(2)}, u32[]{:S(2)}) collective-permute-start(f32[160,128]{1,0:T(8,128)S(1)} %maximum_select_fusion.7.refs_4_), channel_id=1, source_target_pairs={{0,4},{1,5},{2,6},{3,7},{4,0},{5,1},{6,2},{7,3},{8,12},{9,13},{10,... | collective-permute-start | bytes 245768 | tf_op jit(solution)/shard_map/ppermute | solution.py:196
  66.9 3.0 %shard_map.99 = (bf16[128,256,128]{2,1,0:T(8,128)(2,1)}, f32[1,128]{1,0:T(1,128)S(1)}) custom-call(bf16[128,256,128]{2,1,0:T(8,128)(2,1)S(1)} %get-tuple-element.40.refs_0_.back_v, f32[256,128]{1,0:T(8,128)S(1)} %maximum_select_fusion.6.refs_1_.base_ref, bf16[12,128,128]{2,1,0:T(8,128)(2,1)S(1)} %copy-done.1, bf16[128,128]{1,0:T(8,128)(2,1)S(1)} %copy-done.2, ...), custom_call_target="tpu_custom_call" | custom-call | flops 402653184 | bytes 6291456 | tf_op jit(solution)/shard_map/pallas_call | solution.py:387
  70.1 1.6 %collective-permute-start.12 = (f32[320,128]{1,0:T(8,128)S(1)}, f32[320,128]{1,0:T(8,128)S(1)}, u32[]{:S(2)}, u32[]{:S(2)}) collective-permute-start(f32[320,128]{1,0:T(8,128)S(1)} %maximum_select_fusion.1.token_ref), channel_id=1, source_target_pairs={{0,2},{1,3},{2,0},{3,1},{4,6},{5,7},{6,4},{7,5},{8,10},{9,11},{10,... | collective-permute-start | bytes 491528 | tf_op jit(solution)/shard_map/ppermute | solution.py:196
  71.7 4.4 %shard_map.100 = (bf16[128,256,128]{2,1,0:T(8,128)(2,1)}, f32[1,128]{1,0:T(1,128)S(1)}) custom-call(bf16[128,256,128]{2,1,0:T(8,128)(2,1)S(1)} %get-tuple-element.40.refs_0_.back_v, f32[256,128]{1,0:T(8,128)S(1)} %maximum_select_fusion.6.refs_1_.base_ref, bf16[12,128,128]{2,1,0:T(8,128)(2,1)S(1)} %copy-done.1, ...), custom_call_target="tpu_custom_call", output_to_operand_aliasing={{0}: (5, {})} | custom-call | flops 671088640 | bytes 10485760 | tf_op jit(solution)/shard_map/pallas_call | solution.py:387
  76.2 1.8 %collective-permute-done.13 = f32[904,128]{1,0:T(8,128)S(1)} collective-permute-done((f32[904,128]{1,0:T(8,128)S(1)}, f32[904,128]{1,0:T(8,128)S(1)}, u32[]{:S(2)}, u32[]{:S(2)}) %collective-permute-start.13) | collective-permute-done | bytes 462880 | tf_op jit(solution)/shard_map/ppermute | solution.py:196
  (92 shorter events, 7.9 us)
Async XLA Ops:
  0.6 5.6 %copy-start.3 = (f32[5]{0:T(128)S(1)}, f32[5]{0:T(128)}, u32[]{:S(2)}) copy-start(f32[5]{0:T(128)} %constant.23.clone) | copy-start | bytes 64
  0.7 3.4 %copy-start = (bf16[128,256,128]{2,1,0:T(8,128)(2,1)S(1)}, bf16[128,256,128]{2,1,0:T(8,128)(2,1)}, u32[]{:S(2)}) copy-start(bf16[128,256,128]{2,1,0:T(8,128)(2,1)} %fields_v.7) | copy-start | bytes 25165828
  4.1 2.2 %copy-start.2 = (bf16[128,128]{1,0:T(8,128)(2,1)S(1)}, bf16[128,128]{1,0:T(8,128)(2,1)}, u32[]{:S(2)}) copy-start(bf16[128,128]{1,0:T(8,128)(2,1)} %point_ref.7) | copy-start | bytes 98308
  4.1 2.2 %copy-start.1 = (bf16[12,128,128]{2,1,0:T(8,128)(2,1)S(1)}, bf16[12,128,128]{2,1,0:T(8,128)(2,1)}, u32[]{:S(2)}) copy-start(bf16[12,128,128]{2,1,0:T(8,128)(2,1)} %mix_ref.7) | copy-start | bytes 1179652
  5.7 1.4 %collective-permute-start = (f32[128,128]{1,0:T(8,128)S(1)}, f32[128,128]{1,0:T(8,128)S(1)}, u32[]{:S(2)}, u32[]{:S(2)}) collective-permute-start(f32[128,128]{1,0:T(8,128)S(1)} %slice_select_fusion.6), channel_id=1, source_target_pairs={{0,1},{1,0},{2,3},{3,2},{4,5},{5,4},{6,7},{7,6},{8,9},{9,8},{10,11... | collective-permute-start | bytes 196616 | tf_op jit(solution)/shard_map/ppermute | solution.py:196
  7.2 5.3 %collective-permute-start.1 = (f32[128,128]{1,0:T(8,128)S(1)}, f32[128,128]{1,0:T(8,128)S(1)}, u32[]{:S(2)}, u32[]{:S(2)}) collective-permute-start(f32[128,128]{1,0:T(8,128)S(1)} %get-tuple-element.61.refs_3_), channel_id=1, source_target_pairs={{0,2},{1,3},{2,0},{3,1},{4,6},{5,7},{6,4},{7,5},{8,10},{9,11},{10,... | collective-permute-start | bytes 196616 | tf_op jit(solution)/shard_map/ppermute | solution.py:196
  12.5 4.3 %collective-permute-start.2 = (f32[128,128]{1,0:T(8,128)S(1)}, f32[128,128]{1,0:T(8,128)S(1)}, u32[]{:S(2)}, u32[]{:S(2)}) collective-permute-start(f32[128,128]{1,0:T(8,128)S(1)} %get-tuple-element.74.token_ref), channel_id=1, source_target_pairs={{0,4},{1,5},{2,6},{3,7},{4,0},{5,1},{6,2},{7,3},{8,12},{9,13},{10,... | collective-permute-start | bytes 196616 | tf_op jit(solution)/shard_map/ppermute | solution.py:196
  14.7 8.0 %slice-start = ((s8[8388608]{0:T(1024)(128)(4,1)}), s8[4194304]{0:T(1024)(128)(4,1)S(1)}, s32[]{:S(2)}) async-start(s8[8388608]{0:T(1024)(128)(4,1)} %bitcast.83), calls=%async_computation | async-start | bytes 8388608
  16.9 5.3 %collective-permute-start.3 = (f32[128,128]{1,0:T(8,128)S(1)}, f32[128,128]{1,0:T(8,128)S(1)}, u32[]{:S(2)}, u32[]{:S(2)}) collective-permute-start(f32[128,128]{1,0:T(8,128)S(1)} %get-tuple-element.71.token_ref), channel_id=1, source_target_pairs={{0,8},{1,9},{2,10},{3,11},{4,12},{5,13},{6,14},{7,15},{8,0},{9,1},... | collective-permute-start | bytes 196616 | tf_op jit(solution)/shard_map/ppermute | solution.py:196
  20.0 2.6 %copy-start.4 = (bf16[128]{0:T(256)(128)(2,1)S(1)}, bf16[128]{0:T(256)(128)(2,1)}, u32[]{:S(2)}) copy-start(bf16[128]{0:T(256)(128)(2,1)} %param.10) | copy-start | bytes 772
  20.0 2.6 %slice-start.1 = ((s8[8388608]{0:T(1024)(128)(4,1)}), s8[4194304]{0:T(1024)(128)(4,1)S(1)}, s32[]{:S(2)}) async-start(s8[8388608]{0:T(1024)(128)(4,1)} %bitcast.83), calls=%async_computation.1 | async-start | bytes 8388608
  22.2 2.8 %slice-start.2 = ((s8[8388608]{0:T(1024)(128)(4,1)}), s8[4194304]{0:T(1024)(128)(4,1)S(1)}, s32[]{:S(2)}) async-start(s8[8388608]{0:T(1024)(128)(4,1)} %bitcast.85), calls=%async_computation.2 | async-start | bytes 8388608
  22.5 2.3 %collective-permute-start.4 = (f32[512,128]{1,0:T(8,128)S(1)}, f32[512,128]{1,0:T(8,128)S(1)}, u32[]{:S(2)}, u32[]{:S(2)}) collective-permute-start(f32[512,128]{1,0:T(8,128)S(1)} %pad_maximum_fusion.2.token_ref), channel_id=1, source_target_pairs={{0,1},{1,0},{2,3},{3,2},{4,5},{5,4},{6,7},{7,6},{8,9},{9,8},{10,11... | collective-permute-start | bytes 786440 | tf_op jit(solution)/shard_map/ppermute | solution.py:196
  22.6 3.0 %slice-start.3 = ((s8[8388608]{0:T(1024)(128)(4,1)}), s8[4194304]{0:T(1024)(128)(4,1)S(1)}, s32[]{:S(2)}) async-start(s8[8388608]{0:T(1024)(128)(4,1)} %bitcast.85), calls=%async_computation.3 | async-start | bytes 8388608
  37.7 1.8 %collective-permute-start.5 = (f32[768,128]{1,0:T(8,128)S(1)}, f32[768,128]{1,0:T(8,128)S(1)}, u32[]{:S(2)}, u32[]{:S(2)}) collective-permute-start(f32[768,128]{1,0:T(8,128)S(1)} %pad_maximum_fusion.1), channel_id=1, source_target_pairs={{0,1},{1,0},{2,3},{3,2},{4,5},{5,4},{6,7},{7,6},{8,9},{9,8},{10,11... | collective-permute-start | bytes 1179656 | tf_op jit(solution)/shard_map/ppermute | solution.py:196
  39.6 7.9 %collective-permute-start.6 = (f32[448,128]{1,0:T(8,128)S(1)}, f32[448,128]{1,0:T(8,128)S(1)}, u32[]{:S(2)}, u32[]{:S(2)}) collective-permute-start(f32[448,128]{1,0:T(8,128)S(1)} %pad_maximum_fusion.3), channel_id=1, source_target_pairs={{0,2},{1,3},{2,0},{3,1},{4,6},{5,7},{6,4},{7,5},{8,10},{9,11},{10,... | collective-permute-start | bytes 688136 | tf_op jit(solution)/shard_map/ppermute | solution.py:196
  47.6 5.3 %collective-permute-start.7 = (f32[288,128]{1,0:T(8,128)S(1)}, f32[288,128]{1,0:T(8,128)S(1)}, u32[]{:S(2)}, u32[]{:S(2)}) collective-permute-start(f32[288,128]{1,0:T(8,128)S(1)} %pad_maximum_fusion.5), channel_id=1, source_target_pairs={{0,4},{1,5},{2,6},{3,7},{4,0},{5,1},{6,2},{7,3},{8,12},{9,13},{10,... | collective-permute-start | bytes 442376 | tf_op jit(solution)/shard_map/ppermute | solution.py:196
  53.0 7.2 %collective-permute-start.8 = (f32[208,128]{1,0:T(8,128)S(1)}, f32[208,128]{1,0:T(8,128)S(1)}, u32[]{:S(2)}, u32[]{:S(2)}) collective-permute-start(f32[208,128]{1,0:T(8,128)S(1)} %pad_maximum_fusion.6), channel_id=1, source_target_pairs={{0,8},{1,9},{2,10},{3,11},{4,12},{5,13},{6,14},{7,15},{8,0},{9,1},... | collective-permute-start | bytes 319496 | tf_op jit(solution)/shard_map/ppermute | solution.py:196
  60.6 5.0 %collective-permute-start.10 = (f32[80,128]{1,0:T(8,128)S(1)}, f32[80,128]{1,0:T(8,128)S(1)}, u32[]{:S(2)}, u32[]{:S(2)}) collective-permute-start(f32[80,128]{1,0:T(8,128)S(1)} %slice_add_fusion.8), channel_id=1, source_target_pairs={{0,8},{1,9},{2,10},{3,11},{4,12},{5,13},{6,14},{7,15},{8,0},{9,1},... | collective-permute-start | bytes 122888 | tf_op jit(solution)/shard_map/ppermute | solution.py:196
  62.6 4.2 %collective-permute-start.9 = (f32[128,128]{1,0:T(8,128)S(1)}, f32[128,128]{1,0:T(8,128)S(1)}, u32[]{:S(2)}, u32[]{:S(2)}) collective-permute-start(f32[128,128]{1,0:T(8,128)S(1)} %get-tuple-element.65), channel_id=1, source_target_pairs={{0,1},{1,0},{2,3},{3,2},{4,5},{5,4},{6,7},{7,6},{8,9},{9,8},{10,11... | collective-permute-start | bytes 196616 | tf_op jit(solution)/shard_map/ppermute | solution.py:196
  65.6 4.5 %collective-permute-start.11 = (f32[160,128]{1,0:T(8,128)S(1)}, f32[160,128]{1,0:T(8,128)S(1)}, u32[]{:S(2)}, u32[]{:S(2)}) collective-permute-start(f32[160,128]{1,0:T(8,128)S(1)} %maximum_select_fusion.7.refs_4_), channel_id=1, source_target_pairs={{0,4},{1,5},{2,6},{3,7},{4,0},{5,1},{6,2},{7,3},{8,12},{9,13},{10,... | collective-permute-start | bytes 245768 | tf_op jit(solution)/shard_map/ppermute | solution.py:196
  70.1 6.0 %collective-permute-start.12 = (f32[320,128]{1,0:T(8,128)S(1)}, f32[320,128]{1,0:T(8,128)S(1)}, u32[]{:S(2)}, u32[]{:S(2)}) collective-permute-start(f32[320,128]{1,0:T(8,128)S(1)} %maximum_select_fusion.1.token_ref), channel_id=1, source_target_pairs={{0,2},{1,3},{2,0},{3,1},{4,6},{5,7},{6,4},{7,5},{8,10},{9,11},{10,... | collective-permute-start | bytes 491528 | tf_op jit(solution)/shard_map/ppermute | solution.py:196
  76.2 1.9 %collective-permute-start.13 = (f32[904,128]{1,0:T(8,128)S(1)}, f32[904,128]{1,0:T(8,128)S(1)}, u32[]{:S(2)}, u32[]{:S(2)}) collective-permute-start(f32[904,128]{1,0:T(8,128)S(1)} %pad_maximum_fusion), channel_id=1, source_target_pairs={{0,1},{1,0},{2,3},{3,2},{4,5},{5,4},{6,7},{7,6},{8,9},{9,8},{10,11... | collective-permute-start | bytes 1388552 | tf_op jit(solution)/shard_map/ppermute | solution.py:196

commit v6 on v5

--- a/solution.py
+++ b/solution.py
@@ -307,7 +307,7 @@
     joined_back = (joined_f * UNIT).astype(BF)
 
     coarse, flags = pl.pallas_call(
-        functools.partial(kernel_sum, tile),
+        functools.partial(kernel_sum, min(2 * WIDE, columns)),
         in_specs=[VMEM, VMEM],
         out_specs=[VMEM] * 2,
         out_shape=[

time: 79.2 us -> 78.8 us (level)
  no operation moved by 1% of the time
where the time goes in v6:
time: 78.8 us; the launch traced here: 78.7 us
  Pallas kernels  28.5 us (36%)
  waiting for transfers between devices  22 us (28%)
  starting transfers between devices  20.2 us (26%)
  local copies, waits for them, and re-layouts  4.21 us (5%)
  matrix products  1.79 us (2%)
  between operations  1.1 us (1%)
  other arithmetic  0.93 us (1%)
    ppermute x14, waiting for transfers between devices, swap(): lax.ppermute(block, 'gx', [(low, low ^ stride) for low in range(count)])  22 us
    ppermute x14, starting transfers between devices, swap(): lax.ppermute(block, 'gx', [(low, low ^ stride) for low in range(count)])  20.2 us
    pallas_call x1, Pallas kernels, shards(): pl.pallas_call(functools.partial(kernel_b, depth, wide), in_specs=[VMEM]...  11.9 us
    pallas_call x2, Pallas kernels, beside(): pl.pallas_call(kernel, in_specs=[VMEM, VMEM, VMEM, VMEM, HBM] + [HBM] * l...  7.4 us
    pallas_call x4, Pallas kernels, beside_a(): pl.pallas_call(kernel, in_specs=[VMEM, VMEM, VMEM, HBM] + [VMEM] * len(ol...  7.06 us
    unnamed x18, local copies, waits for them, and re-layouts  4.08 us
  transfers between devices with their start and end apart: 14, of which 11 were waited for; matrix products, arithmetic and copies ran while one was open for 2% of the time, Pallas kernels for 18%

profile of v6, /device:TPU:0, one launch (start us, length us, event | category | flops | bytes accessed | tf_op | source)
XLA Modules:
  0.0 78.7 jit_solution(5534823862140183523)
XLA Ops:
  0.7 3.4 %copy-done = bf16[128,256,128]{2,1,0:T(8,128)(2,1)S(1)} copy-done((bf16[128,256,128]{2,1,0:T(8,128)(2,1)S(1)}, bf16[128,256,128]{2,1,0:T(8,128)(2,1)}, u32[]{:S(2)}) %copy-start) | copy-done | bytes 8388632
  4.1 1.2 %shard_map.93 = (f32[256,128]{1,0:T(8,128)S(1)}, f32[4,128]{1,0:T(4,128)S(1)}) custom-call(bf16[128,256,128]{2,1,0:T(8,128)(2,1)S(1)} %copy-done, f32[4,128]{1,0:T(4,128)S(1)} %broadcast_in_dim.191.flags_ref), custom_call_target="tpu_custom_call" | custom-call | bytes 8388608 | tf_op jit(solution)/shard_map/pallas_call | solution.py:309
  6.8 2.9 %collective-permute-start.1 = (f32[128,128]{1,0:T(8,128)S(1)}, f32[128,128]{1,0:T(8,128)S(1)}, u32[]{:S(2)}, u32[]{:S(2)}) collective-permute-start(f32[128,128]{1,0:T(8,128)S(1)} %get-tuple-element.61.refs_3_), channel_id=1, source_target_pairs={{0,2},{1,3},{2,0},{3,1},{4,6},{5,7},{6,4},{7,5},{8,10},{9,11},{10,... | collective-permute-start | bytes 196616 | tf_op jit(solution)/shard_map/ppermute | solution.py:196
  9.9 1.6 %shard_map.94 = (bf16[128,256,128]{2,1,0:T(8,128)(2,1)S(1)}, bf16[128,256,128]{2,1,0:T(8,128)(2,1)S(1)}, f32[1,128]{1,0:T(1,128)S(1)}) custom-call(bf16[128,256,128]{2,1,0:T(8,128)(2,1)S(1)} %copy-done, bf16[12,128,128]{2,1,0:T(8,128)(2,1)S(1)} %copy-done.1, bf16[128,128]{1,0:T(8,128)(2,1)S(1)} %copy-done.2, f32[128,128]{1,0:T(8,128)S(1)} %get-tuple-element.61.refs_3_), custom_call_target="tpu_custom_call" | custom-call | flops 268435456 | bytes 6291456 | tf_op jit(solution)/shard_map/pallas_call | solution.py:332
  12.2 2.0 %collective-permute-start.2 = (f32[128,128]{1,0:T(8,128)S(1)}, f32[128,128]{1,0:T(8,128)S(1)}, u32[]{:S(2)}, u32[]{:S(2)}) collective-permute-start(f32[128,128]{1,0:T(8,128)S(1)} %get-tuple-element.74.token_ref), channel_id=1, source_target_pairs={{0,4},{1,5},{2,6},{3,7},{4,0},{5,1},{6,2},{7,3},{8,12},{9,13},{10,... | collective-permute-start | bytes 196616 | tf_op jit(solution)/shard_map/ppermute | solution.py:196
  14.3 1.6 %shard_map.95 = (bf16[128,256,128]{2,1,0:T(8,128)(2,1)S(1)}, bf16[128,256,128]{2,1,0:T(8,128)(2,1)S(1)}, f32[1,128]{1,0:T(1,128)S(1)}) custom-call(bf16[128,256,128]{2,1,0:T(8,128)(2,1)S(1)} %copy-done, bf16[12,128,128]{2,1,0:T(8,128)(2,1)S(1)} %copy-done.1, bf16[128,128]{1,0:T(8,128)(2,1)S(1)} %copy-done.2, ...), custom_call_target="tpu_custom_call", output_to_operand_aliasing={{0}: (4, {}), {1}: (5, {})} | custom-call | flops 268435456 | bytes 6291456 | tf_op jit(solution)/shard_map/pallas_call | solution.py:332
  16.5 3.0 %collective-permute-start.3 = (f32[128,128]{1,0:T(8,128)S(1)}, f32[128,128]{1,0:T(8,128)S(1)}, u32[]{:S(2)}, u32[]{:S(2)}) collective-permute-start(f32[128,128]{1,0:T(8,128)S(1)} %get-tuple-element.71.token_ref), channel_id=1, source_target_pairs={{0,8},{1,9},{2,10},{3,11},{4,12},{5,13},{6,14},{7,15},{8,0},{9,1},... | collective-permute-start | bytes 196616 | tf_op jit(solution)/shard_map/ppermute | solution.py:196
  19.7 1.6 %shard_map.96 = (bf16[128,256,128]{2,1,0:T(8,128)(2,1)S(1)}, bf16[128,256,128]{2,1,0:T(8,128)(2,1)S(1)}, f32[1,128]{1,0:T(1,128)S(1)}) custom-call(bf16[128,256,128]{2,1,0:T(8,128)(2,1)S(1)} %copy-done, bf16[12,128,128]{2,1,0:T(8,128)(2,1)S(1)} %copy-done.1, bf16[128,128]{1,0:T(8,128)(2,1)S(1)} %copy-done.2, ...), custom_call_target="tpu_custom_call", output_to_operand_aliasing={{0}: (4, {}), {1}: (5, {})} | custom-call | flops 268435456 | bytes 6291456 | tf_op jit(solution)/shard_map/pallas_call | solution.py:332
  22.3 2.2 %shard_map.97 = (bf16[128,256,128]{2,1,0:T(8,128)(2,1)S(1)}, bf16[128,256,128]{2,1,0:T(8,128)(2,1)S(1)}, f32[1,128]{1,0:T(1,128)}) custom-call(bf16[128,256,128]{2,1,0:T(8,128)(2,1)S(1)} %bitcast.84, bf16[12,128,128]{2,1,0:T(8,128)(2,1)S(1)} %copy-done.1, bf16[128,128]{1,0:T(8,128)(2,1)S(1)} %copy-done.2, ...), custom_call_target="tpu_custom_call", output_to_operand_aliasing={{0}: (4, {}), {1}: (5, {})} | custom-call | flops 268435456 | bytes 6291456 | tf_op jit(solution)/shard_map/pallas_call | solution.py:332
  25.3 11.9 %shard_map.98 = (bf16[128,256,128]{2,1,0:T(8,128)(2,1)S(1)}, f32[256,128]{1,0:T(8,128)S(1)}, f32[10,128,128]{2,1,0:T(8,128)S(1)}) custom-call(bf16[128,256,128]{2,1,0:T(8,128)(2,1)S(1)} %get-tuple-element.38.partial_v, bf16[128,256,128]{2,1,0:T(8,128)(2,1)S(1)} %bitcast.86, f32[256,128]{1,0:T(8,128)S(1)} %fusion.6.base_ref, ...), custom_call_target="tpu_custom_call" | custom-call | flops 1073741824 | bytes 33554432 | tf_op jit(solution)/shard_map/pallas_call | solution.py:359
  37.4 1.7 %collective-permute-done.5 = f32[768,128]{1,0:T(8,128)S(1)} collective-permute-done((f32[768,128]{1,0:T(8,128)S(1)}, f32[768,128]{1,0:T(8,128)S(1)}, u32[]{:S(2)}, u32[]{:S(2)}) %collective-permute-start.5) | collective-permute-done | bytes 393248 | tf_op jit(solution)/shard_map/ppermute | solution.py:196
  39.3 2.0 %collective-permute-start.6 = (f32[448,128]{1,0:T(8,128)S(1)}, f32[448,128]{1,0:T(8,128)S(1)}, u32[]{:S(2)}, u32[]{:S(2)}) collective-permute-start(f32[448,128]{1,0:T(8,128)S(1)} %pad_maximum_fusion.3), channel_id=1, source_target_pairs={{0,2},{1,3},{2,0},{3,1},{4,6},{5,7},{6,4},{7,5},{8,10},{9,11},{10,... | collective-permute-start | bytes 688136 | tf_op jit(solution)/shard_map/ppermute | solution.py:196
  41.4 5.8 %collective-permute-done.6 = f32[448,128]{1,0:T(8,128)S(1)} collective-permute-done((f32[448,128]{1,0:T(8,128)S(1)}, f32[448,128]{1,0:T(8,128)S(1)}, u32[]{:S(2)}, u32[]{:S(2)}) %collective-permute-start.6) | collective-permute-done | bytes 229408 | tf_op jit(solution)/shard_map/ppermute | solution.py:196
  47.2 1.9 %collective-permute-start.7 = (f32[288,128]{1,0:T(8,128)S(1)}, f32[288,128]{1,0:T(8,128)S(1)}, u32[]{:S(2)}, u32[]{:S(2)}) collective-permute-start(f32[288,128]{1,0:T(8,128)S(1)} %pad_maximum_fusion.5), channel_id=1, source_target_pairs={{0,4},{1,5},{2,6},{3,7},{4,0},{5,1},{6,2},{7,3},{8,12},{9,13},{10,... | collective-permute-start | bytes 442376 | tf_op jit(solution)/shard_map/ppermute | solution.py:196
  49.3 3.3 %collective-permute-done.7 = f32[288,128]{1,0:T(8,128)S(1)} collective-permute-done((f32[288,128]{1,0:T(8,128)S(1)}, f32[288,128]{1,0:T(8,128)S(1)}, u32[]{:S(2)}, u32[]{:S(2)}) %collective-permute-start.7) | collective-permute-done | bytes 147488 | tf_op jit(solution)/shard_map/ppermute | solution.py:196
  52.6 3.1 %collective-permute-start.8 = (f32[208,128]{1,0:T(8,128)S(1)}, f32[208,128]{1,0:T(8,128)S(1)}, u32[]{:S(2)}, u32[]{:S(2)}) collective-permute-start(f32[208,128]{1,0:T(8,128)S(1)} %pad_maximum_fusion.6), channel_id=1, source_target_pairs={{0,8},{1,9},{2,10},{3,11},{4,12},{5,13},{6,14},{7,15},{8,0},{9,1},... | collective-permute-start | bytes 319496 | tf_op jit(solution)/shard_map/ppermute | solution.py:196
  55.9 4.0 %collective-permute-done.8 = f32[208,128]{1,0:T(8,128)S(1)} collective-permute-done((f32[208,128]{1,0:T(8,128)S(1)}, f32[208,128]{1,0:T(8,128)S(1)}, u32[]{:S(2)}, u32[]{:S(2)}) %collective-permute-start.8) | collective-permute-done | bytes 106528 | tf_op jit(solution)/shard_map/ppermute | solution.py:196
  60.2 1.6 %collective-permute-start.10 = (f32[80,128]{1,0:T(8,128)S(1)}, f32[80,128]{1,0:T(8,128)S(1)}, u32[]{:S(2)}, u32[]{:S(2)}) collective-permute-start(f32[80,128]{1,0:T(8,128)S(1)} %slice_add_fusion.8), channel_id=1, source_target_pairs={{0,8},{1,9},{2,10},{3,11},{4,12},{5,13},{6,14},{7,15},{8,0},{9,1},... | collective-permute-start | bytes 122888 | tf_op jit(solution)/shard_map/ppermute | solution.py:196
  62.3 2.9 %collective-permute-done.10 = f32[80,128]{1,0:T(8,128)S(1)} collective-permute-done((f32[80,128]{1,0:T(8,128)S(1)}, f32[80,128]{1,0:T(8,128)S(1)}, u32[]{:S(2)}, u32[]{:S(2)}) %collective-permute-start.10) | collective-permute-done | bytes 40992 | tf_op jit(solution)/shard_map/ppermute | solution.py:196
  65.2 1.3 %collective-permute-start.11 = (f32[160,128]{1,0:T(8,128)S(1)}, f32[160,128]{1,0:T(8,128)S(1)}, u32[]{:S(2)}, u32[]{:S(2)}) collective-permute-start(f32[160,128]{1,0:T(8,128)S(1)} %maximum_select_fusion.7.refs_4_), channel_id=1, source_target_pairs={{0,4},{1,5},{2,6},{3,7},{4,0},{5,1},{6,2},{7,3},{8,12},{9,13},{10,... | collective-permute-start | bytes 245768 | tf_op jit(solution)/shard_map/ppermute | solution.py:196
  66.5 3.0 %shard_map.99 = (bf16[128,256,128]{2,1,0:T(8,128)(2,1)}, f32[1,128]{1,0:T(1,128)S(1)}) custom-call(bf16[128,256,128]{2,1,0:T(8,128)(2,1)S(1)} %get-tuple-element.40.refs_0_.back_v, f32[256,128]{1,0:T(8,128)S(1)} %maximum_select_fusion.6.refs_1_.base_ref, bf16[12,128,128]{2,1,0:T(8,128)(2,1)S(1)} %copy-done.1, bf16[128,128]{1,0:T(8,128)(2,1)S(1)} %copy-done.2, ...), custom_call_target="tpu_custom_call" | custom-call | flops 402653184 | bytes 6291456 | tf_op jit(solution)/shard_map/pallas_call | solution.py:387
  69.7 1.6 %collective-permute-start.12 = (f32[320,128]{1,0:T(8,128)S(1)}, f32[320,128]{1,0:T(8,128)S(1)}, u32[]{:S(2)}, u32[]{:S(2)}) collective-permute-start(f32[320,128]{1,0:T(8,128)S(1)} %maximum_select_fusion.1.token_ref), channel_id=1, source_target_pairs={{0,2},{1,3},{2,0},{3,1},{4,6},{5,7},{6,4},{7,5},{8,10},{9,11},{10,... | collective-permute-start | bytes 491528 | tf_op jit(solution)/shard_map/ppermute | solution.py:196
  71.3 4.4 %shard_map.100 = (bf16[128,256,128]{2,1,0:T(8,128)(2,1)}, f32[1,128]{1,0:T(1,128)S(1)}) custom-call(bf16[128,256,128]{2,1,0:T(8,128)(2,1)S(1)} %get-tuple-element.40.refs_0_.back_v, f32[256,128]{1,0:T(8,128)S(1)} %maximum_select_fusion.6.refs_1_.base_ref, bf16[12,128,128]{2,1,0:T(8,128)(2,1)S(1)} %copy-done.1, ...), custom_call_target="tpu_custom_call", output_to_operand_aliasing={{0}: (5, {})} | custom-call | flops 671088640 | bytes 10485760 | tf_op jit(solution)/shard_map/pallas_call | solution.py:387
  75.9 1.8 %collective-permute-done.13 = f32[904,128]{1,0:T(8,128)S(1)} collective-permute-done((f32[904,128]{1,0:T(8,128)S(1)}, f32[904,128]{1,0:T(8,128)S(1)}, u32[]{:S(2)}, u32[]{:S(2)}) %collective-permute-start.13) | collective-permute-done | bytes 462880 | tf_op jit(solution)/shard_map/ppermute | solution.py:196
  (92 shorter events, 7.9 us)
Async XLA Ops:
  0.6 5.3 %copy-start.3 = (f32[5]{0:T(128)S(1)}, f32[5]{0:T(128)}, u32[]{:S(2)}) copy-start(f32[5]{0:T(128)} %constant.23.clone) | copy-start | bytes 64
  0.7 3.4 %copy-start = (bf16[128,256,128]{2,1,0:T(8,128)(2,1)S(1)}, bf16[128,256,128]{2,1,0:T(8,128)(2,1)}, u32[]{:S(2)}) copy-start(bf16[128,256,128]{2,1,0:T(8,128)(2,1)} %fields_v.7) | copy-start | bytes 25165828
  4.1 1.8 %copy-start.2 = (bf16[128,128]{1,0:T(8,128)(2,1)S(1)}, bf16[128,128]{1,0:T(8,128)(2,1)}, u32[]{:S(2)}) copy-start(bf16[128,128]{1,0:T(8,128)(2,1)} %point_ref.7) | copy-start | bytes 98308
  4.1 1.8 %copy-start.1 = (bf16[12,128,128]{2,1,0:T(8,128)(2,1)S(1)}, bf16[12,128,128]{2,1,0:T(8,128)(2,1)}, u32[]{:S(2)}) copy-start(bf16[12,128,128]{2,1,0:T(8,128)(2,1)} %mix_ref.7) | copy-start | bytes 1179652
  5.4 1.4 %collective-permute-start = (f32[128,128]{1,0:T(8,128)S(1)}, f32[128,128]{1,0:T(8,128)S(1)}, u32[]{:S(2)}, u32[]{:S(2)}) collective-permute-start(f32[128,128]{1,0:T(8,128)S(1)} %slice_select_fusion.6), channel_id=1, source_target_pairs={{0,1},{1,0},{2,3},{3,2},{4,5},{5,4},{6,7},{7,6},{8,9},{9,8},{10,11... | collective-permute-start | bytes 196616 | tf_op jit(solution)/shard_map/ppermute | solution.py:196
  6.8 5.3 %collective-permute-start.1 = (f32[128,128]{1,0:T(8,128)S(1)}, f32[128,128]{1,0:T(8,128)S(1)}, u32[]{:S(2)}, u32[]{:S(2)}) collective-permute-start(f32[128,128]{1,0:T(8,128)S(1)} %get-tuple-element.61.refs_3_), channel_id=1, source_target_pairs={{0,2},{1,3},{2,0},{3,1},{4,6},{5,7},{6,4},{7,5},{8,10},{9,11},{10,... | collective-permute-start | bytes 196616 | tf_op jit(solution)/shard_map/ppermute | solution.py:196
  12.2 4.3 %collective-permute-start.2 = (f32[128,128]{1,0:T(8,128)S(1)}, f32[128,128]{1,0:T(8,128)S(1)}, u32[]{:S(2)}, u32[]{:S(2)}) collective-permute-start(f32[128,128]{1,0:T(8,128)S(1)} %get-tuple-element.74.token_ref), channel_id=1, source_target_pairs={{0,4},{1,5},{2,6},{3,7},{4,0},{5,1},{6,2},{7,3},{8,12},{9,13},{10,... | collective-permute-start | bytes 196616 | tf_op jit(solution)/shard_map/ppermute | solution.py:196
  14.3 8.0 %slice-start = ((s8[8388608]{0:T(1024)(128)(4,1)}), s8[4194304]{0:T(1024)(128)(4,1)S(1)}, s32[]{:S(2)}) async-start(s8[8388608]{0:T(1024)(128)(4,1)} %bitcast.83), calls=%async_computation | async-start | bytes 8388608
  16.5 5.3 %collective-permute-start.3 = (f32[128,128]{1,0:T(8,128)S(1)}, f32[128,128]{1,0:T(8,128)S(1)}, u32[]{:S(2)}, u32[]{:S(2)}) collective-permute-start(f32[128,128]{1,0:T(8,128)S(1)} %get-tuple-element.71.token_ref), channel_id=1, source_target_pairs={{0,8},{1,9},{2,10},{3,11},{4,12},{5,13},{6,14},{7,15},{8,0},{9,1},... | collective-permute-start | bytes 196616 | tf_op jit(solution)/shard_map/ppermute | solution.py:196
  19.7 2.6 %copy-start.4 = (bf16[128]{0:T(256)(128)(2,1)S(1)}, bf16[128]{0:T(256)(128)(2,1)}, u32[]{:S(2)}) copy-start(bf16[128]{0:T(256)(128)(2,1)} %param.10) | copy-start | bytes 772
  19.7 2.6 %slice-start.1 = ((s8[8388608]{0:T(1024)(128)(4,1)}), s8[4194304]{0:T(1024)(128)(4,1)S(1)}, s32[]{:S(2)}) async-start(s8[8388608]{0:T(1024)(128)(4,1)} %bitcast.83), calls=%async_computation.1 | async-start | bytes 8388608
  21.8 2.8 %slice-start.2 = ((s8[8388608]{0:T(1024)(128)(4,1)}), s8[4194304]{0:T(1024)(128)(4,1)S(1)}, s32[]{:S(2)}) async-start(s8[8388608]{0:T(1024)(128)(4,1)} %bitcast.85), calls=%async_computation.2 | async-start | bytes 8388608
  22.1 2.3 %collective-permute-start.4 = (f32[512,128]{1,0:T(8,128)S(1)}, f32[512,128]{1,0:T(8,128)S(1)}, u32[]{:S(2)}, u32[]{:S(2)}) collective-permute-start(f32[512,128]{1,0:T(8,128)S(1)} %pad_maximum_fusion.2.token_ref), channel_id=1, source_target_pairs={{0,1},{1,0},{2,3},{3,2},{4,5},{5,4},{6,7},{7,6},{8,9},{9,8},{10,11... | collective-permute-start | bytes 786440 | tf_op jit(solution)/shard_map/ppermute | solution.py:196
  22.3 3.0 %slice-start.3 = ((s8[8388608]{0:T(1024)(128)(4,1)}), s8[4194304]{0:T(1024)(128)(4,1)S(1)}, s32[]{:S(2)}) async-start(s8[8388608]{0:T(1024)(128)(4,1)} %bitcast.85), calls=%async_computation.3 | async-start | bytes 8388608
  37.3 1.8 %collective-permute-start.5 = (f32[768,128]{1,0:T(8,128)S(1)}, f32[768,128]{1,0:T(8,128)S(1)}, u32[]{:S(2)}, u32[]{:S(2)}) collective-permute-start(f32[768,128]{1,0:T(8,128)S(1)} %pad_maximum_fusion.1), channel_id=1, source_target_pairs={{0,1},{1,0},{2,3},{3,2},{4,5},{5,4},{6,7},{7,6},{8,9},{9,8},{10,11... | collective-permute-start | bytes 1179656 | tf_op jit(solution)/shard_map/ppermute | solution.py:196
  39.3 7.9 %collective-permute-start.6 = (f32[448,128]{1,0:T(8,128)S(1)}, f32[448,128]{1,0:T(8,128)S(1)}, u32[]{:S(2)}, u32[]{:S(2)}) collective-permute-start(f32[448,128]{1,0:T(8,128)S(1)} %pad_maximum_fusion.3), channel_id=1, source_target_pairs={{0,2},{1,3},{2,0},{3,1},{4,6},{5,7},{6,4},{7,5},{8,10},{9,11},{10,... | collective-permute-start | bytes 688136 | tf_op jit(solution)/shard_map/ppermute | solution.py:196
  47.2 5.3 %collective-permute-start.7 = (f32[288,128]{1,0:T(8,128)S(1)}, f32[288,128]{1,0:T(8,128)S(1)}, u32[]{:S(2)}, u32[]{:S(2)}) collective-permute-start(f32[288,128]{1,0:T(8,128)S(1)} %pad_maximum_fusion.5), channel_id=1, source_target_pairs={{0,4},{1,5},{2,6},{3,7},{4,0},{5,1},{6,2},{7,3},{8,12},{9,13},{10,... | collective-permute-start | bytes 442376 | tf_op jit(solution)/shard_map/ppermute | solution.py:196
  52.6 7.2 %collective-permute-start.8 = (f32[208,128]{1,0:T(8,128)S(1)}, f32[208,128]{1,0:T(8,128)S(1)}, u32[]{:S(2)}, u32[]{:S(2)}) collective-permute-start(f32[208,128]{1,0:T(8,128)S(1)} %pad_maximum_fusion.6), channel_id=1, source_target_pairs={{0,8},{1,9},{2,10},{3,11},{4,12},{5,13},{6,14},{7,15},{8,0},{9,1},... | collective-permute-start | bytes 319496 | tf_op jit(solution)/shard_map/ppermute | solution.py:196
  60.2 5.0 %collective-permute-start.10 = (f32[80,128]{1,0:T(8,128)S(1)}, f32[80,128]{1,0:T(8,128)S(1)}, u32[]{:S(2)}, u32[]{:S(2)}) collective-permute-start(f32[80,128]{1,0:T(8,128)S(1)} %slice_add_fusion.8), channel_id=1, source_target_pairs={{0,8},{1,9},{2,10},{3,11},{4,12},{5,13},{6,14},{7,15},{8,0},{9,1},... | collective-permute-start | bytes 122888 | tf_op jit(solution)/shard_map/ppermute | solution.py:196
  62.3 4.2 %collective-permute-start.9 = (f32[128,128]{1,0:T(8,128)S(1)}, f32[128,128]{1,0:T(8,128)S(1)}, u32[]{:S(2)}, u32[]{:S(2)}) collective-permute-start(f32[128,128]{1,0:T(8,128)S(1)} %get-tuple-element.65), channel_id=1, source_target_pairs={{0,1},{1,0},{2,3},{3,2},{4,5},{5,4},{6,7},{7,6},{8,9},{9,8},{10,11... | collective-permute-start | bytes 196616 | tf_op jit(solution)/shard_map/ppermute | solution.py:196
  65.2 4.5 %collective-permute-start.11 = (f32[160,128]{1,0:T(8,128)S(1)}, f32[160,128]{1,0:T(8,128)S(1)}, u32[]{:S(2)}, u32[]{:S(2)}) collective-permute-start(f32[160,128]{1,0:T(8,128)S(1)} %maximum_select_fusion.7.refs_4_), channel_id=1, source_target_pairs={{0,4},{1,5},{2,6},{3,7},{4,0},{5,1},{6,2},{7,3},{8,12},{9,13},{10,... | collective-permute-start | bytes 245768 | tf_op jit(solution)/shard_map/ppermute | solution.py:196
  69.7 6.0 %collective-permute-start.12 = (f32[320,128]{1,0:T(8,128)S(1)}, f32[320,128]{1,0:T(8,128)S(1)}, u32[]{:S(2)}, u32[]{:S(2)}) collective-permute-start(f32[320,128]{1,0:T(8,128)S(1)} %maximum_select_fusion.1.token_ref), channel_id=1, source_target_pairs={{0,2},{1,3},{2,0},{3,1},{4,6},{5,7},{6,4},{7,5},{8,10},{9,11},{10,... | collective-permute-start | bytes 491528 | tf_op jit(solution)/shard_map/ppermute | solution.py:196
  75.8 1.9 %collective-permute-start.13 = (f32[904,128]{1,0:T(8,128)S(1)}, f32[904,128]{1,0:T(8,128)S(1)}, u32[]{:S(2)}, u32[]{:S(2)}) collective-permute-start(f32[904,128]{1,0:T(8,128)S(1)} %pad_maximum_fusion), channel_id=1, source_target_pairs={{0,1},{1,0},{2,3},{3,2},{4,5},{5,4},{6,7},{7,6},{8,9},{9,8},{10,11... | collective-permute-start | bytes 1388552 | tf_op jit(solution)/shard_map/ppermute | solution.py:196
